TPU v7x, 32 devices: a whole 2x2x4 slice. The times are simulated.
32 devices in a mesh: stream: 2 (over x), dp: 16 (over z, y, core).
Axes of the slice: x: 2, y: 2, z: 4, core: 2. Of those that a mesh axis runs over, the one named last changes fastest.
Arguments:
- text_states: bfloat16 [8192, 768], P(('stream', 'dp')), may hold values from -6 to 6
- image_states: bfloat16 [2304, 1024], P(('stream', 'dp')), may hold values from -6 to 6
- caption_lengths: int32 [64], P(('stream', 'dp')), may hold values from 8 to 128, as said below
- text_query: bfloat16 [768, 1024], replicated, may hold values from -0.21875 to 0.21875
- text_keyval: bfloat16 [768, 2048], replicated, may hold values from -0.21875 to 0.21875
- text_attend: bfloat16 [1024, 768], replicated, may hold values from -0.75 to 0.75
- text_up: bfloat16 [768, 3072], replicated, may hold values from -0.21875 to 0.21875
- text_down: bfloat16 [3072, 768], replicated, may hold values from -0.109375 to 0.109375
- text_qkv: bfloat16 [768, 2304], replicated, may hold values from -0.21875 to 0.21875
- text_output: bfloat16 [768, 768], replicated, may hold values from -0.875 to 0.875
- text_gains: float32 [3, 768], replicated, may hold values from 0.5 to 1.5
- image_query: bfloat16 [1024, 1024], replicated, may hold values from -0.1875 to 0.1875
- image_keyval: bfloat16 [1024, 2048], replicated, may hold values from -0.1875 to 0.1875
- image_attend: bfloat16 [1024, 1024], replicated, may hold values from -0.75 to 0.75
- image_up: bfloat16 [1024, 1024], replicated, may hold values from -0.1875 to 0.1875
- image_down: bfloat16 [1024, 1024], replicated, may hold values from -0.1875 to 0.1875
- image_qkv: bfloat16 [1024, 3072], replicated, may hold values from -0.1875 to 0.1875
- image_output: bfloat16 [1024, 1024], replicated, may hold values from -0.75 to 0.75
- image_gains: float32 [3, 1024], replicated, may hold values from 0.5 to 1.5
- text_cotangent: bfloat16 [8192, 768], P(('stream', 'dp')), may hold values from -6 to 6
- image_cotangent: bfloat16 [2304, 1024], P(('stream', 'dp')), may hold values from -6 to 6
Outputs:
- text_result: bfloat16 [8192, 768], P(('stream', 'dp'))
- image_result: bfloat16 [2304, 1024], P(('stream', 'dp'))
- text_grad: bfloat16 [8192, 768], P(('stream', 'dp'))
- image_grad: bfloat16 [2304, 1024], P(('stream', 'dp'))
- text_weight_grads: float32 [10223616], P(('stream', 'dp'))
- image_weight_grads: float32 [10485760], P(('stream', 'dp'))
- text_gain_grads: float32 [3, 768], replicated
- image_gain_grads: float32 [3, 1024], replicated
Inputs may be any that keep to these rules, and one draw needn't show every extreme that they name: `caption_lengths`: on every device the first of its pairs has a caption of 128 tokens.
All inputs are finite; a program needn't handle non-finite values.
Results may differ from a plain program's by a relative error of at most 0.02.
Values may be sent and summed in bfloat16 or wider, within the bound.
No kernel may reach another device: no remote copies, remote signals or barrier semaphores. Data moves between devices by JAX's collectives and lax.ppermute only.
A program may use at most 448 MiB of HBM per device.

v0:
```python
import functools

import jax
import jax.numpy as jnp
from jax import lax
from jax.experimental import pallas as pl
from jax.experimental.pallas import tpu as pltpu
from jax.sharding import PartitionSpec as P

H_T = 12
H_I = 8
H_C = 8
D_C = 1024
LANES = 128
UNIT = 256
masked_score = -1e30
F32 = jnp.float32
BF16 = jnp.bfloat16


def mm(a, b):
    return jnp.dot(a, b, preferred_element_type=F32)


def mm_nt(a, b):
    return lax.dot_general(a, b, (((1,), (1,)), ((), ())), preferred_element_type=F32)


def mm_tn(a, b):
    return lax.dot_general(a, b, (((0,), (0,)), ((), ())), preferred_element_type=F32)


def cost(us):
    return pl.CostEstimate(flops=int(us * 1e9), bytes_accessed=1000, transcendentals=0)


def lane_block(ref, rows, block):
    return ref[rows, pl.ds(pl.multiple_of(block * LANES, LANES), LANES)]


def put_block(ref, rows, block, value):
    ref[rows, pl.ds(pl.multiple_of(block * LANES, LANES), LANES)] = value


def split_heads(block, heads_in):
    if heads_in == 1:
        return block
    lanes = lax.broadcasted_iota(jnp.int32, block.shape, 1)
    zero = jnp.zeros_like(block)
    low = lanes < LANES // 2
    return jnp.concatenate([jnp.where(low, block, zero), jnp.where(low, zero, block)], axis=0)


def side_by_side(block, heads_in):
    if heads_in == 1:
        return block
    rows = block.shape[0] // 2
    return jnp.concatenate([block[:rows], block[rows:]], axis=1)


def attend_kernel(
    lens_ref, q_ref, k_ref, v_ref, o_ref, *, pairs, blocks, cols, heads_in, fixed, scaling
):
    ql = q_ref.shape[0] // pairs
    kl = k_ref.shape[0] // pairs
    chain = heads_in * ql
    keys = lax.broadcasted_iota(jnp.int32, (chain, kl), 1)
    if fixed is None:
        masks = [keys < lens_ref[p] for p in range(pairs)]
    else:
        masks = [keys < fixed] * pairs

    @pl.loop(0, blocks)
    def _(j):
        scores = []
        for p in range(pairs):
            q = split_heads(lane_block(q_ref, slice(p * ql, (p + 1) * ql), cols[0] + j), heads_in)
            k = lane_block(k_ref, slice(p * kl, (p + 1) * kl), cols[1] + j)
            scores.append(jnp.where(masks[p], mm_nt(q, k) * scaling, masked_score))
        s = jnp.concatenate(scores, axis=0)
        raised = jnp.exp(s - jnp.max(s, axis=-1, keepdims=True))
        w = (raised * (1.0 / jnp.sum(raised, axis=-1, keepdims=True))).astype(BF16)
        for p in range(pairs):
            v = split_heads(lane_block(v_ref, slice(p * kl, (p + 1) * kl), cols[2] + j), heads_in)
            o = mm(side_by_side(w[p * chain : (p + 1) * chain], heads_in), v)
            put_block(o_ref, slice(p * ql, (p + 1) * ql), j, o.astype(BF16))


def attend(lens, q, k, v, cols, pairs, blocks, heads_in, fixed, scaling):
    rows = q.shape[0]
    krows = k.shape[0]
    same = k is v
    vmem = pl.BlockSpec(memory_space=pltpu.VMEM)
    operands = [lens, q, k] if same else [lens, q, k, v]
    if q is k:
        operands = [lens, q]

    def body(lens_ref, *refs, **kw):
        refs = list(refs)
        o_ref = refs.pop()
        while len(refs) < 3:
            refs.append(refs[-1])
        attend_kernel(lens_ref, *refs, o_ref, **kw)

    return pl.pallas_call(
        functools.partial(
            body,
            pairs=pairs,
            blocks=blocks,
            cols=cols,
            heads_in=heads_in,
            fixed=fixed,
            scaling=scaling,
        ),
        in_specs=[pl.BlockSpec(memory_space=pltpu.SMEM)] + [vmem] * (len(operands) - 1),
        out_specs=vmem,
        out_shape=jax.ShapeDtypeStruct((rows, blocks * LANES), BF16),
        compiler_params=pltpu.CompilerParams(vmem_limit_bytes=24 * 1024 * 1024),
        cost_estimate=cost(5),
        name="attend",
    )(*operands)


def attend_back_kernel(
    lens_ref,
    q_ref,
    k_ref,
    v_ref,
    g_ref,
    dq_ref,
    dk_ref,
    dv_ref,
    *,
    pairs,
    blocks,
    cols,
    out_cols,
    heads_in,
    fixed,
    scaling,
):
    ql = q_ref.shape[0] // pairs
    kl = k_ref.shape[0] // pairs
    keys = lax.broadcasted_iota(jnp.int32, (heads_in * kl, ql), 0)
    if heads_in == 2:
        keys = jnp.where(keys >= kl, keys - kl, keys)
    if fixed is None:
        masks = [keys < lens_ref[p] for p in range(pairs)]
    else:
        masks = [keys < fixed] * pairs

    @pl.loop(0, blocks)
    def _(j):
        scores, slopes = [], []
        for p in range(pairs):
            qs, ks = slice(p * ql, (p + 1) * ql), slice(p * kl, (p + 1) * kl)
            q, g = lane_block(q_ref, qs, cols[0] + j), lane_block(g_ref, qs, j)
            k = split_heads(lane_block(k_ref, ks, cols[1] + j), heads_in)
            v = split_heads(lane_block(v_ref, ks, cols[2] + j), heads_in)
            scores.append(jnp.where(masks[p], mm_nt(k, q) * scaling, masked_score))
            slopes.append(mm_nt(v, g))
        stacked = (pairs * heads_in, kl, ql)
        s = jnp.concatenate(scores, axis=0).reshape(stacked)
        dp = jnp.concatenate(slopes, axis=0).reshape(stacked)
        raised = jnp.exp(s - jnp.max(s, axis=1, keepdims=True))
        w = raised * (1.0 / jnp.sum(raised, axis=1, keepdims=True))
        inner = jnp.sum(w * dp, axis=1, keepdims=True)
        ds = (w * (dp - inner)).astype(BF16).reshape(-1, ql)
        w = w.astype(BF16).reshape(-1, ql)
        chain = heads_in * kl
        for p in range(pairs):
            qs, ks = slice(p * ql, (p + 1) * ql), slice(p * kl, (p + 1) * kl)
            own = slice(p * chain, (p + 1) * chain)
            q = split_heads(lane_block(q_ref, qs, cols[0] + j), heads_in)
            g = split_heads(lane_block(g_ref, qs, j), heads_in)
            k = split_heads(lane_block(k_ref, ks, cols[1] + j), heads_in)
            dq = mm_tn(ds[own], k) * scaling
            dk = mm(side_by_side(ds[own], heads_in), q) * scaling
            dv = mm(side_by_side(w[own], heads_in), g)
            put_block(dq_ref, qs, out_cols[0] + j, dq.astype(BF16))
            put_block(dk_ref, ks, out_cols[1] + j, dk.astype(BF16))
            put_block(dv_ref, ks, out_cols[2] + j, dv.astype(BF16))


def attend_back(lens, q, k, v, g, cols, pairs, blocks, heads_in, fixed, scaling, packed):
    rows = q.shape[0]
    krows = k.shape[0]
    vmem = pl.BlockSpec(memory_space=pltpu.VMEM)
    width = blocks * LANES
    if packed:
        operands = [lens, q, g]
        out_cols = (0, blocks, 2 * blocks)
        out_shape = jax.ShapeDtypeStruct((rows, 3 * width), BF16)
        out_specs = vmem
    else:
        operands = [lens, q, k, g]
        out_cols = (0, 0, blocks)
        out_shape = [
            jax.ShapeDtypeStruct((rows, width), BF16),
            jax.ShapeDtypeStruct((krows, 2 * width), BF16),
        ]
        out_specs = [vmem, vmem]

    def body(lens_ref, *refs, **kw):
        if packed:
            q_ref, g_ref, out_ref = refs
            ins, outs = (q_ref, q_ref, q_ref, g_ref), (out_ref,) * 3
        else:
            q_ref, k_ref, g_ref, dq_ref, dkv_ref = refs
            ins, outs = (q_ref, k_ref, k_ref, g_ref), (dq_ref, dkv_ref, dkv_ref)
        attend_back_kernel(lens_ref, *ins, *outs, **kw)

    return pl.pallas_call(
        functools.partial(
            body,
            pairs=pairs,
            blocks=blocks,
            cols=cols,
            out_cols=out_cols,
            heads_in=heads_in,
            fixed=fixed,
            scaling=scaling,
        ),
        in_specs=[pl.BlockSpec(memory_space=pltpu.SMEM)] + [vmem] * (len(operands) - 1),
        out_specs=out_specs,
        out_shape=out_shape,
        compiler_params=pltpu.CompilerParams(vmem_limit_bytes=24 * 1024 * 1024),
        cost_estimate=cost(6),
        name="attend_back",
    )(*operands)


class Job:
    def __init__(self, a, b, low, high, place):
        self.a, self.b = a, b
        self.low, self.count = low, high - low
        self.columns = b[3]
        self.place = place


def flat_kernel(side_ref, *refs, plans, found, quarter, resident):
    out_ref, chosen_ref, stage_ref = refs[len(found) : len(found) + 3]
    core = side_ref[0]
    depth = chosen_ref.shape[0] // 2
    if not resident:
        a_buf, b_buf, in_sem = refs[-3:]

    def loads(jobs, k):
        job, slot = jobs[k], k % 2
        copies = []
        for side, buf, start, width in (
            (job.a, a_buf, job.a[2] + job.low, job.count),
            (job.b, b_buf, job.b[2], job.columns),
        ):
            for half in range(2):
                copies.append(
                    pltpu.make_async_copy(
                        refs[found[id(side[half])]].at[:, start : start + width],
                        buf.at[slot, half * depth : (half + 1) * depth, 0:width],
                        in_sem.at[slot, len(copies)],
                    )
                )
        return copies

    def run(jobs):
        if not resident:
            for copy in loads(jobs, 0):
                copy.start()
        for k, job in enumerate(jobs):
            if resident:
                a_refs = [refs[found[id(job.a[half])]] for half in range(2)]
                b_refs = [refs[found[id(job.b[half])]] for half in range(2)]
                a_first, b_first = job.a[2] + job.low, job.b[2]
            else:
                if k + 1 < len(jobs):
                    for copy in loads(jobs, k + 1):
                        copy.start()
                for copy in loads(jobs, k):
                    copy.wait()
                halves = [slice(0, depth), slice(depth, 2 * depth)]
                a_refs = [a_buf.at[k % 2, half] for half in halves]
                b_refs = [b_buf.at[k % 2, half] for half in halves]
                a_first = b_first = 0
            units = job.columns // (2 * UNIT if quarter else UNIT)
            for u in range(units):
                at = 4 * u + 2 * side_ref[1] + core if quarter else 2 * u + core
                block = pl.ds(pl.multiple_of(at * LANES + b_first, LANES), LANES)
                for half in range(2):
                    chosen_ref[half * depth : (half + 1) * depth, u * LANES : (u + 1) * LANES] = (
                        b_refs[half][:, block]
                    )
            bm = best_rows(job.count, units)
            rows = bm * units

            @pl.loop(0, job.count // bm)
            def _(i, job=job, units=units, bm=bm, rows=rows, a_refs=a_refs, a_first=a_first):
                columns = pl.ds(pl.multiple_of(a_first + i * bm, LANES), bm)
                a = jnp.concatenate([a_ref[:, columns] for a_ref in a_refs], axis=0).T
                for u0 in range(0, units, 4):
                    u1 = min(u0 + 4, units)
                    total = mm(a, chosen_ref[:, u0 * LANES : u1 * LANES])
                    for u in range(u0, u1):
                        stage_ref[pl.ds(u, bm, stride=units), :] = total[
                            :, (u - u0) * LANES : (u - u0 + 1) * LANES
                        ]
                first = pl.multiple_of(job.place + i * rows, LANES)
                out_ref[pl.ds(first, rows), :] = stage_ref[:rows].astype(BF16)

    if len(plans) == 1:
        run(plans[0])
    else:
        for side, jobs in enumerate(plans):

            @pl.when(side_ref[1] == side)
            def _(jobs=jobs):
                run(jobs)


def best_rows(count, units):
    most = 512 if units <= 8 else 384
    return max(size for size in range(LANES, most + 1, LANES) if count % size == 0)


def flat_grads(side, total_rows, plans, us, quarter=False, resident=True):
    arrays, found = [], {}
    jobs = [job for plan in plans for job in plan]
    for job in jobs:
        for array in (*job.a[:2], *job.b[:2]):
            if id(array) not in found:
                found[id(array)] = len(arrays)
                arrays.append(array)
    depth = 2 * arrays[0].shape[0]
    widest = max(job.columns for job in jobs)
    tallest = max(job.count for job in jobs)
    factor = 2 * UNIT if quarter else UNIT
    rows = max(best_rows(job.count, job.columns // factor) * job.columns // factor for job in jobs)
    held = 2 * depth * widest * LANES // factor + 4 * rows * LANES
    scratch = [
        pltpu.VMEM((depth, widest * LANES // factor), BF16),
        pltpu.VMEM((rows, LANES), F32),
    ]
    if not resident:
        held += 4 * depth * (tallest + widest)
        scratch += [
            pltpu.VMEM((2, depth, tallest), BF16),
            pltpu.VMEM((2, depth, widest), BF16),
            pltpu.SemaphoreType.DMA((2, 4)),
        ]
    place = pltpu.VMEM if resident else pltpu.HBM
    return pl.pallas_call(
        functools.partial(
            flat_kernel, plans=plans, found=found, quarter=quarter, resident=resident
        ),
        in_specs=[pl.BlockSpec(memory_space=pltpu.SMEM)]
        + [pl.BlockSpec(memory_space=place)] * len(arrays),
        out_specs=pl.BlockSpec(memory_space=pltpu.VMEM),
        out_shape=jax.ShapeDtypeStruct((total_rows, LANES), BF16),
        scratch_shapes=scratch,
        compiler_params=pltpu.CompilerParams(vmem_limit_bytes=held + 6 * 1024 * 1024),
        cost_estimate=cost(us),
        name="flat_grads",
    )(side, *arrays)


def dp_swap(block, bit):
    count = lax.axis_size("dp")
    return lax.ppermute(block, "dp", [(i, i ^ bit) for i in range(count)])


def stream_swap(block):
    return lax.ppermute(block, "stream", [(0, 1), (1, 0)])


def pick(block, index, axis=0):
    return lax.dynamic_index_in_dim(block, index, axis, keepdims=False)


def plus(a, b):
    return (a.astype(F32) + b.astype(F32)).astype(BF16)


def tied(*values):
    return lax.optimization_barrier(values)


def scatter_parts(flat, cuts):
    count = lax.axis_size("dp")
    top = count.bit_length() - 2
    bits = tuple(range(top, 0, -1))
    rows = flat.shape[0] // (count // 2)
    blocks = flat.reshape((2,) * len(bits) + (rows, LANES))
    natural = tuple(range(1, top + 1))
    turned = natural[1:2] + natural[:1] + natural[2:]
    parts, start = [], 0
    for share, turn in cuts:
        part = lax.slice_in_dim(blocks, start, start + rows * share // 8, axis=len(bits))
        start += rows * share // 8
        parts.append((part, bits, turned if turn else natural))
    return parts


def scatter_step(parts):
    me = lax.axis_index("dp")
    done = []
    for block, left, order in parts:
        bit = order[0]
        axis = left.index(bit)
        mine = (me >> bit) & 1
        keep = pick(block, mine, axis)
        far = dp_swap(pick(block, 1 - mine, axis), 1 << bit)
        block = plus(keep, far) if len(order) > 1 else keep.astype(F32) + far.astype(F32)
        done.append((block, left[:axis] + left[axis + 1 :], order[1:]))
    return done


def scatter_end(parts):
    while parts[0][2]:
        parts = scatter_step(parts)
    blocks = [block for block, _, _ in parts]
    return jnp.concatenate(blocks) if len(blocks) > 1 else blocks[0]


def reduce_scatter(flat, cuts):
    return scatter_end(scatter_parts(flat, cuts))


def share_of(result):
    core = lax.axis_index("dp") & 1
    halves = result.reshape(2, result.shape[0] // 2, LANES)
    mine = pick(halves, core)
    far = dp_swap(pick(halves, 1 - core), 1)
    first = jnp.where(core == 0, mine, far)
    second = jnp.where(core == 0, far, mine)
    return jnp.stack([first, second], axis=1).reshape(-1)


def choices(stream):
    me = lax.axis_index("dp")
    y, odd = (me >> 1) & 1, (me >> 2) & 1
    own = jnp.where(y == 1, odd, 1 - odd)
    values = [me & 1, y, odd, (me >> 3) & 1, 1 - y, own, stream, me >> 1]
    return jnp.stack(values).astype(jnp.int32)


LATE_Y, LATE_OWN, STREAM, CHIP = 4, 5, 6, 7
TEXT_SHARES = (48, 46, 38, 24)


def split_kernel(choice_ref, flat_ref, *refs, chunk, cuts):
    for k, (start, rows, bases, weight, which) in enumerate(cuts):
        mine = choice_ref[which]
        for i, base in enumerate(bases):
            for out_ref, index in ((refs[2 * k], mine), (refs[2 * k + 1], 1 - mine)):
                first = (base + index * weight) * chunk + start
                out_ref[i] = flat_ref[pl.ds(pl.multiple_of(first, 16), rows), :]


def split(choice, flat, chunk, cuts):
    shapes = [
        jax.ShapeDtypeStruct((len(bases), rows, LANES), BF16)
        for _, rows, bases, _, _ in cuts
        for _ in range(2)
    ]
    return pl.pallas_call(
        functools.partial(split_kernel, chunk=chunk, cuts=cuts),
        in_specs=[
            pl.BlockSpec(memory_space=pltpu.SMEM),
            pl.BlockSpec(memory_space=pltpu.VMEM),
        ],
        out_specs=[pl.BlockSpec(memory_space=pltpu.VMEM)] * len(shapes),
        out_shape=shapes,
        compiler_params=pltpu.CompilerParams(vmem_limit_bytes=4 * 1024 * 1024),
        cost_estimate=cost(3),
        name="split",
    )(choice, flat)


def piece_set(choice, flat, firsts, shares):
    chunk = flat.shape[0] // 8
    unit = chunk // sum(shares)
    cuts, start = [], 0
    for first, share in zip(firsts, shares):
        bits = [bit for bit in (3, 2, 1) if bit != first]
        bases = tuple(
            sum(((n >> (1 - at)) & 1) << (b - 1) for at, b in enumerate(bits)) for n in range(4)
        )
        cuts.append((start, unit * share, bases, 1 << (first - 1), first))
        start += unit * share
    arrays = split(choice, flat, chunk, tuple(cuts))
    return [
        Piece(keep, out, first) for keep, out, first in zip(arrays[::2], arrays[1::2], firsts)
    ]


class Piece:
    def __init__(self, keep, out, bit):
        self.keep, self.out, self.bit = keep, out, bit

    def send(self):
        self.far = dp_swap(self.out, 1 << self.bit)


def after(value, pieces, name="far"):
    value, *got = tied(value, *(getattr(piece, name) for piece in pieces))
    for piece, array in zip(pieces, got):
        setattr(piece, name, array)
    return value


def paced(came, leaving, values=()):
    got = tied(*(item.far for item in came), *(item.out for item in leaving), *values)
    for item, array in zip(came, got):
        item.far = array
    for item, array in zip(leaving, got[len(came) :]):
        item.out = array
    return got[len(came) + len(leaving) :]


def added(a_ref, b_ref, index):
    return a_ref[index].astype(F32) + b_ref[index].astype(F32)


def add_split_kernel(choice_ref, *refs, plan, inputs):
    outs = refs[2 * inputs :]
    for k, base, stride, which, out, at in plan:
        keep_ref, far_ref = refs[2 * k : 2 * k + 2]
        mine = choice_ref[which]
        for ref, index in ((outs[2 * out], mine), (outs[2 * out + 1], 1 - mine)):
            ref[at] = added(keep_ref, far_ref, base + index * stride).astype(BF16)


def add_split(choice, groups, which=None):
    operands, plan, shapes = [], [], []
    for out, (bit, pieces) in enumerate(groups):
        at = 0
        for piece in pieces:
            for base in range(0, piece.keep.shape[0], 2):
                plan.append((len(operands) // 2, base, 1, which or bit, out, at))
                at += 1
            operands += [piece.keep, piece.far]
        shape = jax.ShapeDtypeStruct((at,) + pieces[0].keep.shape[1:], BF16)
        shapes += [shape, shape]
    vmem = pl.BlockSpec(memory_space=pltpu.VMEM)
    arrays = pl.pallas_call(
        functools.partial(add_split_kernel, plan=tuple(plan), inputs=len(operands) // 2),
        in_specs=[pl.BlockSpec(memory_space=pltpu.SMEM)] + [vmem] * len(operands),
        out_specs=[vmem] * len(shapes),
        out_shape=shapes,
        compiler_params=pltpu.CompilerParams(vmem_limit_bytes=4 * 1024 * 1024),
        cost_estimate=cost(1),
        name="add_split",
    )(choice, *operands)
    return [
        Piece(arrays[2 * out], arrays[2 * out + 1], bit) for out, (bit, _) in enumerate(groups)
    ]


def finish_kernel(choice_ref, *refs, rows):
    refs = list(refs)
    pairs = [[(refs.pop(0), refs.pop(0)) for _ in group] for group in rows]
    near_ref, far_ref = refs.pop(0), refs.pop(0)
    out_ref, send_ref, *totals, joined_ref = refs
    for total_ref, group, starts in zip(totals, pairs, rows):
        for (keep_ref, came_ref), firsts in zip(group, starts):
            count = keep_ref.shape[1]
            for at, first in enumerate(firsts):
                total_ref[first : first + count] = added(keep_ref, came_ref, at)
    half = near_ref.shape[0]
    joined_ref[pl.ds(0, half, stride=2), :] = near_ref[...].astype(F32)
    joined_ref[pl.ds(1, half, stride=2), :] = far_ref[...].astype(F32)
    image_ref = totals[0]
    total_rows = image_ref.shape[0]
    chip = choice_ref[CHIP]
    first = jnp.where(chip == 1, 1536, 0)
    last = jnp.where(chip == 4, 2048, total_rows)
    here = (chip >= 1) & (chip <= 4) & (choice_ref[STREAM] == 0)
    last = jnp.where(here, last, 0)
    at = lax.broadcasted_iota(jnp.int32, (total_rows, 1), 0)
    image_ref[...] = jnp.where((at >= first) & (at < last), joined_ref[...], image_ref[...])
    core = choice_ref[0]
    row = 0
    for total_ref in totals:
        half = total_ref.shape[0] // 2
        for ref, index in ((out_ref, core), (send_ref, 1 - core)):
            ref[row : row + half, :] = total_ref[pl.ds(pl.multiple_of(index * half, 8), half), :]
        row += half


def join_kernel(choice_ref, near_ref, far_ref, *outs):
    core = choice_ref[0]
    row = 0
    for out_ref in outs:
        half = out_ref.shape[0] // 2
        out_ref[pl.ds(core, half, stride=2), :] = near_ref[row : row + half, :]
        out_ref[pl.ds(1 - core, half, stride=2), :] = far_ref[row : row + half, :]
        row += half


def finished(choice, groups, rows, late):
    sizes = [
        sum(piece.keep.shape[0] * piece.keep.shape[1] for piece in group) for group in groups
    ]
    vmem = pl.BlockSpec(memory_space=pltpu.VMEM)
    smem = pl.BlockSpec(memory_space=pltpu.SMEM)
    operands = [ref for group in groups for piece in group for ref in (piece.keep, piece.far)]
    operands += list(late)
    half = jax.ShapeDtypeStruct((sum(sizes) // 2, LANES), F32)
    near, send = pl.pallas_call(
        functools.partial(finish_kernel, rows=rows),
        in_specs=[smem] + [vmem] * len(operands),
        out_specs=[vmem] * 2,
        out_shape=[half] * 2,
        scratch_shapes=[pltpu.VMEM((rows, LANES), F32) for rows in (*sizes, sizes[0])],
        compiler_params=pltpu.CompilerParams(vmem_limit_bytes=16 * 1024 * 1024),
        cost_estimate=cost(3),
        name="finish",
    )(choice, *operands)
    joined = pl.pallas_call(
        join_kernel,
        in_specs=[smem, vmem, vmem],
        out_specs=[vmem] * 2,
        out_shape=[jax.ShapeDtypeStruct((rows, LANES), F32) for rows in sizes],
        compiler_params=pltpu.CompilerParams(vmem_limit_bytes=8 * 1024 * 1024),
        cost_estimate=cost(2),
        name="join",
    )(choice, near, dp_swap(send, 1))
    return [block.reshape(-1) for block in joined]


CHUNK = 64
ROWS = 128
WIDEST = 1024
WIDEST_GELU = 1024


def tiles(columns, body, widest=None):
    size = max(c for c in range(LANES, (widest or WIDEST) + 1, LANES) if columns % c == 0)
    if size == columns:
        return body(slice(0, columns))

    @pl.loop(0, columns // size)
    def _(j):
        body(pl.ds(pl.multiple_of(j * size, size), size))


def views(pack_ref, *widths):
    found, start = [], 0
    for width in widths:
        found.append(pack_ref.at[:, start : start + width])
        start += width
    return found


def row_chunks(rows, body):
    size = ROWS if rows % ROWS == 0 else CHUNK

    @pl.loop(0, rows // size)
    def _(i):
        body(i * size, pl.ds(pl.multiple_of(i * size, size), size), size)


def normed_chunk(a):
    centred = a - jnp.mean(a, axis=-1, keepdims=True)
    inverse = lax.rsqrt(jnp.mean(centred * centred, axis=-1, keepdims=True) + 1e-05)
    return centred * inverse, inverse


def normed_back_chunk(grad, n, inverse, gain_row):
    scaled = grad * gain_row
    low = jnp.mean(scaled, axis=-1, keepdims=True)
    tilt = jnp.mean(scaled * n, axis=-1, keepdims=True)
    return (scaled - low - n * tilt) * inverse, jnp.sum(grad * n, axis=0, keepdims=True)


def co_kernel(
    lens_ref, x_ref, o_ref, g_ref, wq_ref, wkv_ref, wat_ref,
    q_ref, kv_ref, pack_ref, n_ref, inv_ref, a_ref, *, pairs, fixed, scaling,
):
    rows, width = x_ref.shape
    c_ref, h_ref = views(pack_ref, D_C, width)

    def kv_tile(cols):
        kv_ref[:, cols] = mm(o_ref[...], wkv_ref[:, cols]).astype(BF16)

    def q_tile(cols):
        q_ref[:, cols] = mm(x_ref[...], wq_ref[:, cols]).astype(BF16)

    def a_tile(cols):
        a_ref[:, cols] = x_ref[:, cols].astype(F32) + mm(c_ref[...], wat_ref[:, cols])

    def norm(i, at, size):
        n, inverse = normed_chunk(a_ref[at, :])
        n_ref[at, :] = n
        inv_ref[at, :] = jnp.broadcast_to(inverse, (size, LANES))
        h_ref[at, :] = (n * g_ref[0:1, :]).astype(BF16)

    tiles(kv_ref.shape[1], kv_tile)
    tiles(q_ref.shape[1], q_tile)
    blocks = q_ref.shape[1] // LANES
    attend_kernel(
        lens_ref, q_ref, kv_ref, kv_ref, c_ref, pairs=pairs, blocks=blocks,
        cols=(0, 0, blocks), heads_in=1, fixed=fixed, scaling=scaling,
    )
    tiles(width, a_tile)
    row_chunks(rows, norm)


def mlp_kernel(
    pack1_ref, n1_ref, g_ref, wup_ref, wdown_ref, wqkv_ref,
    pack_ref, slope_ref, n_ref, inv_ref, r_ref, a_ref,
):
    rows, width = n1_ref.shape
    _, h1_ref = views(pack1_ref, D_C, width)
    hid_ref, h_ref = views(pack_ref, wup_ref.shape[1], width)

    def up_tile(cols):
        u_all = mm(h1_ref[...], wup_ref[:, cols])
        for at in range(0, rows, CHUNK):
            u = u_all[at : at + CHUNK]
            share = 0.5 + 0.5 * lax.erf(u * 0.7071067811865476)
            hid_ref[at : at + CHUNK, cols] = (u * share).astype(BF16)
            slope = share + u * (0.3989422804014327 * jnp.exp(-0.5 * u * u))
            slope_ref[at : at + CHUNK, cols] = slope.astype(BF16)

    def down_tile(cols):
        a_ref[:, cols] = n1_ref[:, cols] * g_ref[0:1, cols] + mm(hid_ref[...], wdown_ref[:, cols])

    def norm(i, at, size):
        n, inverse = normed_chunk(a_ref[at, :])
        n_ref[at, :] = n
        inv_ref[at, :] = jnp.broadcast_to(inverse, (size, LANES))
        h_ref[at, :] = (n * g_ref[1:2, :]).astype(BF16)

    def qkv_tile(cols):
        r_ref[:, cols] = mm(h_ref[...], wqkv_ref[:, cols]).astype(BF16)

    tiles(wup_ref.shape[1], up_tile, WIDEST_GELU)
    tiles(width, down_tile)
    row_chunks(rows, norm)
    tiles(r_ref.shape[1], qkv_tile)


def self_kernel(
    lens_ref, r_ref, n2_ref, g_ref, wout_ref, cot_ref,
    pack_ref, y_ref, de_ref, dg_ref, a_ref, dz_ref,
    *, pairs, heads_in, fixed, scaling,
):
    rows, width = n2_ref.shape
    z_ref, de_low_ref, dr_ref = views(pack_ref, width, width, 3 * width)
    blocks = width // LANES
    cols = (0, blocks, 2 * blocks)
    shared = dict(
        pairs=pairs, blocks=blocks, cols=cols, heads_in=heads_in, fixed=fixed, scaling=scaling
    )

    def out_tile(at):
        a_ref[:, at] = n2_ref[:, at] * g_ref[1:2, at] + mm(z_ref[...], wout_ref[:, at])

    def last(start, at, size):
        n, inverse = normed_chunk(a_ref[at, :])
        y = n * g_ref[2:3, :]
        grad = cot_ref[at, :].astype(F32)
        if fixed is None:
            slots = rows // pairs
            place = lax.broadcasted_iota(jnp.int32, (size, 1), 0) + lax.rem(start, slots)
            valid = (place < lens_ref[lax.div(start, slots)]).astype(F32)
            y, grad = y * valid, grad * valid
        y_ref[at, :] = y.astype(BF16)
        de, dg = normed_back_chunk(grad, n, inverse, g_ref[2:3, :])
        de_ref[at, :] = de
        de_low_ref[at, :] = de.astype(BF16)
        dg_ref[...] += dg

    def dz_tile(at):
        dz_ref[:, at] = mm_nt(de_low_ref[...], wout_ref[at, :]).astype(BF16)

    attend_kernel(lens_ref, r_ref, r_ref, r_ref, z_ref, **shared)
    tiles(width, out_tile)
    dg_ref[...] = jnp.zeros_like(dg_ref)
    row_chunks(rows, last)
    tiles(width, dz_tile)
    attend_back_kernel(
        lens_ref, r_ref, r_ref, r_ref, dz_ref, dr_ref, dr_ref, dr_ref, out_cols=cols, **shared
    )


def mlp_back_kernel(
    pack3_ref, de_ref, n2_ref, inv2_ref, g_ref, slope_ref, wqkv_ref, wdown_ref,
    pack_ref, db_ref, dg_ref, a_ref,
):
    rows, width = n2_ref.shape
    _, _, dr_ref = views(pack3_ref, width, width, 3 * width)
    db_low_ref, du_ref = views(pack_ref, width, slope_ref.shape[1])
    dg_ref[...] = jnp.zeros_like(dg_ref)

    def second_tile(at):
        a_ref[:, at] = de_ref[:, at] + mm_nt(dr_ref[...], wqkv_ref[at, :])

    def second_norm(i, at, size):
        db, dg = normed_back_chunk(a_ref[at, :], n2_ref[at, :], inv2_ref[at, 0:1], g_ref[1:2, :])
        db_ref[at, :] = db
        db_low_ref[at, :] = db.astype(BF16)
        dg_ref[...] += dg

    def du_tile(at):
        grad = mm_nt(db_low_ref[...], wdown_ref[at, :])
        du_ref[:, at] = (grad * slope_ref[:, at].astype(F32)).astype(BF16)

    tiles(width, second_tile)
    row_chunks(rows, second_norm)
    tiles(du_ref.shape[1], du_tile)


def context_back_kernel(
    pack4_ref, db_ref, n1_ref, inv1_ref, g_ref, wup_ref, wat_ref,
    da_low_ref, da_ref, dc_ref, dg_ref, a_ref,
):
    rows, width = n1_ref.shape
    _, du_ref = views(pack4_ref, width, wup_ref.shape[1])
    dg_ref[...] = jnp.zeros_like(dg_ref)

    def first_tile(at):
        a_ref[:, at] = db_ref[:, at] + mm_nt(du_ref[...], wup_ref[at, :])

    def first_norm(i, at, size):
        da, dg = normed_back_chunk(a_ref[at, :], n1_ref[at, :], inv1_ref[at, 0:1], g_ref[0:1, :])
        da_ref[at, :] = da
        da_low_ref[at, :] = da.astype(BF16)
        dg_ref[...] += dg

    def dc_tile(at):
        dc_ref[:, at] = mm_nt(da_low_ref[...], wat_ref[at, :]).astype(BF16)

    tiles(width, first_tile)
    row_chunks(rows, first_norm)
    tiles(dc_ref.shape[1], dc_tile)


def fused(kernel, operands, outs, scratch, name, us, smem_first=False, limit=14):
    vmem = pl.BlockSpec(memory_space=pltpu.VMEM)
    in_specs = [vmem] * len(operands)
    if smem_first:
        in_specs[0] = pl.BlockSpec(memory_space=pltpu.SMEM)
    return pl.pallas_call(
        kernel,
        in_specs=in_specs,
        out_specs=[vmem] * len(outs),
        out_shape=[jax.ShapeDtypeStruct(shape, kind) for shape, kind in outs],
        scratch_shapes=[pltpu.VMEM(shape, kind) for shape, kind in scratch],
        compiler_params=pltpu.CompilerParams(vmem_limit_bytes=limit * 1024 * 1024),
        cost_estimate=cost(us),
        name=name,
    )(*operands)


def co_forward(lens, states, other, gains, query_w, keyval_w, attend_w, pairs, fixed):
    rows, width = states.shape
    orows = other.shape[0]
    return fused(
        functools.partial(co_kernel, pairs=pairs, fixed=fixed, scaling=(D_C // H_C) ** (-0.5)),
        (lens, states, other, gains, query_w, keyval_w, attend_w),
        [
            ((rows, D_C), BF16),
            ((orows, 2 * D_C), BF16),
            ((rows, D_C + width), BF16),
            ((rows, width), F32),
            ((rows, LANES), F32),
        ],
        [((rows, width), F32)],
        "co_forward",
        9,
        True,
    )


def mlp_forward(pack1, n1, gains, up_w, down_w, qkv_w):
    rows, width = n1.shape
    hidden = up_w.shape[1]
    return fused(
        mlp_kernel,
        (pack1, n1, gains, up_w, down_w, qkv_w),
        [
            ((rows, hidden + width), BF16),
            ((rows, hidden), BF16),
            ((rows, width), F32),
            ((rows, LANES), F32),
            ((rows, 3 * width), BF16),
        ],
        [((rows, width), F32)],
        "mlp_forward",
        rows / 40,
    )


def self_turn(lens, r, n2, gains, output_w, cot, pairs, heads, fixed):
    rows, width = n2.shape
    size = width // heads
    return fused(
        functools.partial(
            self_kernel, pairs=pairs, heads_in=LANES // size, fixed=fixed, scaling=size ** (-0.5)
        ),
        (lens, r, n2, gains, output_w, cot),
        [
            ((rows, 5 * width), BF16),
            ((rows, width), BF16),
            ((rows, width), F32),
            ((1, width), F32),
        ],
        [((rows, width), F32), ((rows, width), BF16)],
        "self_turn",
        rows / 128 + 9,
        True,
    )


def input_kernel(da_ref, dq_ref, dkv_ref, y_ref, trim_ref, wq_ref, wkv_ref, *outs, first):
    grad_ref, result_ref = outs
    rows = pl.ds(first, da_ref.shape[0] // 2)
    grad = da_ref[rows, :] + mm_nt(dq_ref[rows, :], wq_ref[...])
    grad = (grad + mm_nt(dkv_ref[rows, :], wkv_ref[...])).astype(BF16)
    y = y_ref[rows, :]
    if trim_ref.shape[0] < 8:
        grad_ref[...], result_ref[...] = grad, y
    else:
        grad_ref[...] = mm(trim_ref[...], grad).astype(BF16)
        result_ref[...] = mm(trim_ref[...], y).astype(BF16)


def input_grads(da, dq, dkv, y, trim, query_w, keyval_w, first, own):
    vmem = pl.BlockSpec(memory_space=pltpu.VMEM)
    return pl.pallas_call(
        functools.partial(input_kernel, first=first),
        in_specs=[vmem] * 7,
        out_specs=[vmem] * 2,
        out_shape=[jax.ShapeDtypeStruct((own, da.shape[1]), BF16)] * 2,
        compiler_params=pltpu.CompilerParams(vmem_limit_bytes=10 * 1024 * 1024),
        cost_estimate=cost(0.2),
        name="input_grads",
    )(da, dq, dkv, y, trim, query_w, keyval_w)


def mlp_back(pack3, de, n2, inv2, gains, slope, qkv_w, down_w):
    rows, width = n2.shape
    return fused(
        mlp_back_kernel,
        (pack3, de, n2, inv2, gains, slope, qkv_w, down_w),
        [
            ((rows, width + slope.shape[1]), BF16),
            ((rows, width), F32),
            ((1, width), F32),
        ],
        [((rows, width), F32)],
        "mlp_back",
        rows / 70,
    )


def context_back(pack4, db, n1, inv1, gains, up_w, attend_w):
    rows, width = n1.shape
    return fused(
        context_back_kernel,
        (pack4, db, n1, inv1, gains, up_w, attend_w),
        [
            ((rows, width), BF16),
            ((rows, width), F32),
            ((rows, D_C), BF16),
            ((1, width), F32),
        ],
        [((rows, width), F32)],
        "context_back",
        rows / 80,
    )


class Exchange:
    def __init__(self):
        self.far = {}
        self.pending = []
        self.parts = None

    def send(self, **arrays):
        for name, array in arrays.items():
            self.far[name] = dp_swap(array, 1)
            self.pending.append(name)

    def settle(self, value):
        names, self.pending = self.pending, []
        if names:
            value, *got = tied(value, *(self.far[name] for name in names))
            self.far.update(zip(names, got))
        return value

    def pair(self, name, array, start=0, width=None):
        return array, self.far[name], start, width or array.shape[1]


def stream_forward(
    lens, states, other, cot, weights, gains, heads, fixed, other_fixed, pairs, moves, hook
):
    query_w, other_keyval_w, attend_w, up_w, down_w, qkv_w, output_w = weights
    q, kv, pack1, n1, inv1 = co_forward(
        lens, states, other, gains, query_w, other_keyval_w, attend_w, pairs, other_fixed
    )
    pack1 = moves.settle(hook("co", pack1))
    moves.send(pack1=pack1)
    pack2, slope, n2, inv2, r = mlp_forward(pack1, n1, gains, up_w, down_w, qkv_w)
    r, pack2 = tied(moves.settle(hook("mlp", r)), pack2)
    moves.send(pack2=pack2)
    pack3, result, de, dg2 = self_turn(lens, r, n2, gains, output_w, cot, pairs, heads, fixed)
    pack3 = moves.settle(hook("self", pack3))
    moves.send(pack3=pack3)
    pack4, db, dg1 = mlp_back(pack3, de, n2, inv2, gains, slope, qkv_w, down_w)
    pack4 = moves.settle(hook("mid", pack4))
    moves.send(pack4=pack4)
    da_low, da, dc, dg0 = context_back(pack4, db, n1, inv1, gains, up_w, attend_w)
    dc, da_low = tied(moves.settle(hook("back", dc)), da_low)
    moves.send(da=da_low)
    width, hidden = up_w.shape

    def sides(dq):
        def side(number, start, count):
            pack = (pack1, pack2, pack3, pack4)[number - 1]
            return moves.pair("pack%d" % number, pack, start, count)

        return {
            "query": (moves.pair("states", states), moves.pair("dq", dq)),
            "attend": (side(1, 0, D_C), moves.pair("da", da_low)),
            "up": (side(1, D_C, width), side(4, width, hidden)),
            "down": (side(2, 0, hidden), side(4, 0, width)),
            "qkv": (side(2, hidden, width), side(3, 2 * width, 3 * width)),
            "output": (side(3, 0, width), side(3, width, width)),
        }

    return result, da, dc, q, kv, sides, jnp.concatenate([dg0, dg1, dg2])


NAMES = ("query", "keyval", "attend", "up", "down", "qkv", "output")


def half_jobs(both, sizes, total):
    plans, filled = ([], []), 0
    for name in NAMES:
        m, n = sizes[name]
        room = min(max((total // 2 - filled) // n, 0), m)
        for plan, low, high in ((plans[0], 0, room), (plans[1], room, m)):
            if low < high and name in both:
                start = filled + low * n - (0 if plan is plans[0] else total // 2)
                step = 1536 if (high - low) > 1536 else high - low
                for at in range(low, high, step):
                    place = (start + (at - low) * n) // UNIT
                    plan.append(Job(*both[name], at, at + step, place))
        filled += m * n
    return plans


def spread(count, regions, padded, offset, rows):
    target = lax.broadcasted_iota(jnp.int32, (rows, count * regions), 0) - offset
    source = lax.broadcasted_iota(jnp.int32, (rows, count * regions), 1)
    return (target == source // regions * padded + source % regions).astype(BF16)


def local(
    text_states,
    image_states,
    caption_lengths,
    text_query,
    text_keyval,
    text_attend,
    text_up,
    text_down,
    text_qkv,
    text_output,
    text_gains,
    image_query,
    image_keyval,
    image_attend,
    image_up,
    image_down,
    image_qkv,
    image_output,
    image_gains,
    text_cotangent,
    image_cotangent,
):
    own_pairs = caption_lengths.shape[0]
    own_text = text_states.shape[0]
    text_len = own_text // own_pairs
    regions = image_states.shape[0] // own_pairs
    padded = -(-regions // 16) * 16
    own_image = own_pairs * padded
    pairs = 2 * own_pairs
    d_t, d_i = text_states.shape[1], image_states.shape[1]
    stream = lax.axis_index("stream")
    core = lax.axis_index("dp") & 1
    side = jnp.stack([core, stream]).astype(jnp.int32)

    far_put = spread(own_pairs, regions, padded, 0, 2 * own_image)
    near_put = spread(own_pairs, regions, padded, own_image, 2 * own_image)
    trim = near_put[own_image:].T

    def both_images(near):
        return (mm(far_put, stream_swap(near)) + mm(near_put, near)).astype(BF16)

    choice = choices(stream)
    image_all = both_images(image_states)
    far_text = stream_swap(text_states)
    text_all = jnp.concatenate([text_states, far_text])
    lens = jnp.concatenate([caption_lengths, stream_swap(caption_lengths)])
    image_cotangent, text_cotangent, text_all = tied(image_cotangent, text_cotangent, text_all)
    image_cot = both_images(image_cotangent)
    far_text_cot = stream_swap(text_cotangent)

    co_blocks = D_C // LANES
    co_cols = (0, 0, co_blocks)
    co_scale = (D_C // H_C) ** (-0.5)

    image_moves, text_moves = Exchange(), Exchange()
    image_moves.send(states=image_all)
    cots = [far_text_cot]

    def image_hook(name, value):
        if name == "self":
            value, cots[0] = tied(value, cots[0])
        return value

    image_out, image_da, image_dc, image_q, text_kv, image_sides, image_dg = stream_forward(
        lens,
        image_all,
        text_all,
        image_cot,
        (image_query, text_keyval, image_attend, image_up, image_down, image_qkv, image_output),
        image_gains,
        H_I,
        regions,
        None,
        pairs,
        image_moves,
        image_hook,
    )
    image_dq, text_dkv = attend_back(
        lens, image_q, text_kv, text_kv, image_dc, co_cols, pairs, co_blocks, 1, None, co_scale, False
    )
    image_moves.send(dq=image_dq)
    image_sides = image_sides(image_dq)
    text_moves.send(states=text_all, dkv=text_dkv)

    def sizes_of(*weights):
        return {name: weight.shape for name, weight in zip(NAMES, weights)}

    def gather_half(both, sizes):
        total = sum(m * n for m, n in sizes.values())
        total_rows = total // (2 * UNIT)
        plans = half_jobs(both, sizes, total)
        image = both["query"][0][0] is image_all
        return flat_grads(side, total_rows, plans, 6 if image else 14, resident=image)

    image_sizes = sizes_of(
        image_query, image_keyval, image_attend, image_up, image_down, image_qkv, image_output
    )
    text_sizes = sizes_of(
        text_query, text_keyval, text_attend, text_up, text_down, text_qkv, text_output
    )
    early = lax.axis_size("dp") == 16
    if early:
        image_flat = gather_half(image_sides, image_sizes)

    pieces = []

    def hook(name, value):
        if not early:
            return value
        if name == "co":
            value, flat = tied(value, image_flat)
            pieces.extend(piece_set(choice, flat, (1, 2, 1, 2), (1, 1, 1, 1)))
            value = after(value, pieces, "out")
            for piece in pieces[:2]:
                piece.send()
        if name == "mlp":
            (value,) = paced(pieces[:2], pieces[2:], (value,))
            for piece in pieces[2:]:
                piece.send()
        if name == "self":
            (value,) = paced(pieces[2:], (), (value,))
            pieces[:] = add_split(choice, ((2, pieces[0::2]), (1, pieces[1::2])))
            for piece in pieces:
                piece.send()
        if name == "back":
            (value,) = paced(pieces, (), (value,))
            pieces[:] = add_split(choice, ((3, pieces),))
            pieces[0].send()
        return value

    text_out, text_da, text_dc, text_q, image_kv, text_sides, text_dg = stream_forward(
        lens,
        text_all,
        image_all,
        jnp.concatenate([text_cotangent, cots[0]]),
        (text_query, image_keyval, text_attend, text_up, text_down, text_qkv, text_output),
        text_gains,
        H_T,
        None,
        regions,
        pairs,
        text_moves,
        hook,
    )
    gains = pack_gains(text_dg, image_dg)
    bits = [1 << b for b in range(lax.axis_size("dp").bit_length() - 1)]
    text_dq, image_dkv = attend_back(
        lens, text_q, image_kv, image_kv, text_dc, co_cols, pairs, co_blocks, 1, regions, co_scale, False
    )

    image_moves.send(dkv=image_dkv)
    text_moves.send(dq=text_dq)
    text_sides = text_sides(text_dq)
    text_sides["keyval"] = (text_moves.pair("states", text_all), text_moves.pair("dkv", text_dkv))

    def all_input_grads(text_dq, image_dq):
        text = input_grads(
            text_da, text_dq, text_dkv, text_out, trim[:1], text_query, text_keyval, 0, own_text
        )
        image = input_grads(
            image_da,
            image_dq,
            image_dkv,
            image_out,
            trim,
            image_query,
            image_keyval,
            own_image,
            own_pairs * regions,
        )
        return (*text, *image)

    if early:
        late = Late(
            choice,
            side,
            image_moves.pair("states", image_all),
            image_moves.pair("dkv", image_dkv),
        )
        near_dq, *rest = text_sides["query"][1]
        near_dq, late.out = tied(near_dq, late.out)
        text_sides["query"] = (text_sides["query"][0], (near_dq, *rest))
        late.send()
        text_flat = gather_half(text_sides, text_sizes)
        text_flat = after(text_flat, pieces + [late])
        text_pieces = piece_set(choice, text_flat, (1, 1, 1, 1), TEXT_SHARES)
        one, two, three, four = text_pieces
        late.turn()
        one.out, late.out, text_dq, image_dq, gains = tied(
            one.out, late.out, text_dq, image_dq, gains
        )
        one.send()
        late.send()
        gains = gain_step(gains, bits.pop())
        grads = all_input_grads(text_dq, image_dq)
        *grads, gains = paced((one, late), (two,), (*grads, gains))
        (one,) = add_split(choice, ((2, (one,)),))
        late.add(gather=True)
        two.send()
        one.send()
        gains = gain_step(gains, bits.pop())
        (gains,) = paced((one, two, late), (three,), (gains,))
        (one,) = add_split(choice, ((3, (one,)),))
        (two,) = add_split(choice, ((2, (two,)),))
        late.add()
        three.send()
        two.send()
        one.send()
        gains = gain_step(gains, bits.pop())
        (gains,) = paced((one, two, three, late), (four,), (gains,))
        (two,) = add_split(choice, ((3, (two,)),))
        (three,) = add_split(choice, ((2, (three,)),))
        four.send()
        three.send()
        two.send()
        gains = gain_step(gains, bits.pop())
        (gains,) = paced((two, three, four), (), (gains,))
        (three,) = add_split(choice, ((3, (three,)),))
        (four,) = add_split(choice, ((2, (four,)),))
        three.send()
        four.send()
        paced((three, four), ())
        (four,) = add_split(choice, ((3, (four,)),))
        four.send()
        unit = image_flat.shape[0] // 8 // 4
        starts, row = [], 0
        for piece in (one, two, three, four):
            starts.append((row,))
            row += piece.keep.shape[1]
        image_share, text_share = finished(
            choice,
            (pieces, (one, two, three, four)),
            (((0, 2 * unit, unit, 3 * unit),), tuple(starts)),
            (late.keep[0], late.far[0]),
        )
    else:
        image_sides["keyval"] = (
            image_moves.pair("states", image_all),
            image_moves.pair("dkv", image_dkv),
        )
        image_share = share_of(
            reduce_scatter(gather_half(image_sides, image_sizes), ((8, False),))
        )
        text_share = share_of(reduce_scatter(gather_half(text_sides, text_sizes), ((8, False),)))
        grads = all_input_grads(text_dq, image_dq)
        while bits:
            gains = gain_step(gains, bits.pop())
    text_grad, text_result, image_grad, image_result = grads
    text_gain_sum, image_gain_sum = unpack_gains(gains, text_dg.shape[1])
    return (
        text_result,
        image_result,
        text_grad,
        image_grad,
        text_share,
        image_share,
        text_gain_sum,
        image_gain_sum,
    )


def pack_gains(text_dg, image_dg):
    return jnp.concatenate([text_dg, image_dg], axis=1)


def gain_step(gains, bit):
    return gains + dp_swap(gains, bit)


def unpack_gains(gains, width):
    return gains[:, :width], gains[:, width:]


class Late:
    rows = 1280

    def __init__(self, choice, side, states, grads):
        self.choice = choice
        job = Job(states, grads, 0, states[0].shape[1], 768)
        flat = flat_grads(side, 4 * self.rows, [[job]], 2, True)
        self.keep, self.out = split(choice, flat, self.rows, ((0, self.rows, (0, 2), 1, LATE_Y),))
        self.bit = 2

    def send(self):
        self.far = dp_swap(self.out, self.bit)

    def turn(self):
        (piece,) = add_split(self.choice, ((LATE_OWN, (self,)),))
        self.keep, self.out, self.bit = piece.keep, piece.out, 4

    def add(self, gather=False):
        self.keep = plus(self.keep, self.far)
        if gather:
            route = []
            for i in range(16):
                z, y = i >> 2, (i >> 1) & 1
                goal = 1 if z & 1 else (0 if y else 2)
                if z != goal:
                    route.append((i, goal * 4 + (i & 3)))
            self.far = lax.ppermute(self.keep, "dp", route)
        else:
            self.far = lax.ppermute(self.keep, "stream", [(1, 0)])


def solution(mesh):
    split = P(("stream", "dp"), None)
    flat = P(("stream", "dp"))
    whole = P()
    return jax.shard_map(
        local,
        mesh=mesh,
        in_specs=(split, split, flat) + (whole,) * 16 + (split, split),
        out_specs=(split, split, split, split, flat, flat, whole, whole),
        check_vma=False,
    )
```

profile of v0, /device:TPU:3, one launch (start us, length us, event | category | flops | bytes accessed | tf_op | source)
XLA Modules:
  0.0 306.0 jit_solution(14714305602738658747)
XLA Ops:
  0.7 1.5 collective-permute-start
  3.7 10.4 %collective-permute-done.1 = s32[2]{0:T(128)S(1)} collective-permute-done((s32[2]{0:T(128)}, s32[2]{0:T(128)S(1)}, u32[]{:S(2)}, u32[]{:S(2)}) %collective-permute-start.1) | collective-permute-done | bytes 40 | tf_op jit(solution)/shard_map/ppermute | solution.py:371
  15.2 1.7 collective-permute-start.3
  18.2 2.1 copy-done.3
  21.0 1.6 copy-done.30
  22.6 8.2 %co_forward.3 = (bf16[192,1024]{1,0:T(8,128)(2,1)S(1)}, bf16[512,2048]{1,0:T(8,128)(2,1)S(1)}, bf16[192,2048]{1,0:T(8,128)(2,1)S(1)}, f32[192,1024]{1,0:T(8,128)S(1)}, f32[192,128]{1,0:T(8,128)S(1)}) custom-call(s32[4]{0:T(128)S(1)} %pad_add_fusion.1.lens_ref, bf16[192,1024]{1,0:T(8,128)(2,1)S(1)} %fusion.o_ref.x_ref.refs_0_, ...), custom_call_target="tpu_custom_call" | custom-call | flops 8999999488 | bytes 1000 | tf_op jit(solution)/shard_map/co_forward/pallas_call | solution.py:844
  33.3 3.7 %mlp_forward.2 = (bf16[192,2048]{1,0:T(8,128)(2,1)S(1)}, bf16[192,1024]{1,0:T(8,128)(2,1)S(1)}, f32[192,1024]{1,0:T(8,128)S(1)}, f32[192,128]{1,0:T(8,128)S(1)}, bf16[192,3072]{1,0:T(8,128)(2,1)S(1)}) custom-call(bf16[192,2048]{1,0:T(8,128)(2,1)S(1)} %get-tuple-element.197.pack1_ref.refs_4_, f32[192,1024]{1,0:T(8,128)S(1)} %get-tuple-element.198.n1_ref, ...), custom_call_target="tpu_custom_call" | custom-call | flops 4800000000 | bytes 1000 | tf_op jit(solution)/shard_map/mlp_forward/pallas_call | solution.py:844
  37.6 10.5 %self_turn.2 = (bf16[192,5120]{1,0:T(8,128)(2,1)S(1)}, bf16[192,1024]{1,0:T(8,128)(2,1)S(1)}, f32[192,1024]{1,0:T(8,128)S(1)}, f32[1,1024]{1,0:T(1,128)S(1)}) custom-call(s32[4]{0:T(128)S(1)} %pad_add_fusion.1.lens_ref, bf16[192,3072]{1,0:T(8,128)(2,1)S(1)} %get-tuple-element.202.r_ref, f32[192,1024]{1,0:T(8,128)S(1)} %get-tuple-element.203.n2_ref, ...), custom_call_target="tpu_custom_call" | custom-call | flops 10499999744 | bytes 1000 | tf_op jit(solution)/shard_map/self_turn/pallas_call | solution.py:844
  49.2 3.6 %mlp_back.2 = (bf16[192,2048]{1,0:T(8,128)(2,1)S(1)}, f32[192,1024]{1,0:T(8,128)S(1)}, f32[1,1024]{1,0:T(1,128)S(1)}) custom-call(bf16[192,5120]{1,0:T(8,128)(2,1)S(1)} %get-tuple-element.209.pack3_ref.refs_12_, f32[192,1024]{1,0:T(8,128)S(1)} %get-tuple-element.210.de_ref, f32[192,1024]{1,0:T(8,128)S(1)} %get-tuple-element.203.n2_ref, ...), custom_call_target="tpu_custom_call" | custom-call | flops 2742857216 | bytes 1000 | tf_op jit(solution)/shard_map/mlp_back/pallas_call | solution.py:844
  53.4 2.2 context_back.2
  58.2 6.6 %attend_back.2 = (bf16[192,1024]{1,0:T(8,128)(2,1)S(1)}, bf16[512,2048]{1,0:T(8,128)(2,1)}) custom-call(s32[4]{0:T(128)S(1)} %pad_add_fusion.1.lens_ref, bf16[192,1024]{1,0:T(8,128)(2,1)S(1)} %get-tuple-element.195.refs_0_, bf16[512,2048]{1,0:T(8,128)(2,1)S(1)} %get-tuple-element.196.refs_1_, bf16[192,1024]{1,0:T(8,128)(2,1)S(1)} %get-tuple-element.220.refs_2_), custom_call_target="tpu_custom_call" | custom-call | flops 6000000000 | bytes 1000 | tf_op jit(solution)/shard_map/attend_back/pallas_call | solution.py:213
  66.7 2.2 copy-done
  68.9 1.4 copy-done.8
  72.4 1.4 copy-done.39
  75.3 20.1 %co_forward.2 = (bf16[512,1024]{1,0:T(8,128)(2,1)S(1)}, bf16[192,2048]{1,0:T(8,128)(2,1)S(1)}, bf16[512,1792]{1,0:T(8,128)(2,1)S(1)}, f32[512,768]{1,0:T(8,128)S(1)}, f32[512,128]{1,0:T(8,128)S(1)}) custom-call(s32[4]{0:T(128)S(1)} %copy-done.64, bf16[512,768]{1,0:T(8,128)(2,1)S(1)} %copy-done.13, bf16[192,1024]{1,0:T(8,128)(2,1)S(1)} %copy-done.18, ...), custom_call_target="tpu_custom_call" | custom-call | flops 8999999488 | bytes 1000 | tf_op jit(solution)/shard_map/co_forward/pallas_call | solution.py:844
  95.6 5.9 %flat_grads.3.flat_ref = bf16[20480,128]{1,0:T(8,128)(2,1)S(1)} custom-call(s32[2]{0:T(128)S(1)} %pad_add_fusion.side_ref, bf16[192,1024]{1,0:T(8,128)(2,1)S(1)} %copy-done.18, bf16[192,1024]{1,0:T(8,128)(2,1)S(1)} %copy-done.57, bf16[192,1024]{1,0:T(8,128)(2,1)S(1)} %copy-done.16, bf16[192,1024]{1,0:T(8,128)(2,1)S(1)} %collective-permute-done.10.refs_3_, ...), custom_call_target="tpu_custom_call" | custom-call | flops 6000000000 | bytes 1000 | tf_op jit(solution)/shard_map/flat_grads/pallas_call | solution.py:350
  101.5 1.7 split.3
  106.2 10.7 %mlp_forward.3 = (bf16[512,3840]{1,0:T(8,128)(2,1)S(1)}, bf16[512,3072]{1,0:T(8,128)(2,1)S(1)}, f32[512,768]{1,0:T(8,128)S(1)}, f32[512,128]{1,0:T(8,128)S(1)}, bf16[512,2304]{1,0:T(8,128)(2,1)S(1)}) custom-call(bf16[512,1792]{1,0:T(8,128)(2,1)S(1)} %get-tuple-element.243.pack1_ref.refs_6_, f32[512,768]{1,0:T(8,128)S(1)} %get-tuple-element.244.n1_ref, ...), custom_call_target="tpu_custom_call" | custom-call | flops 12800000000 | bytes 1000 | tf_op jit(solution)/shard_map/mlp_forward/pallas_call | solution.py:844
  116.9 1.5 copy-done.67
  120.6 1.4 collective-permute-start.21
  123.6 1.7 copy-done.68
  125.3 12.5 %self_turn.3 = (bf16[512,3840]{1,0:T(8,128)(2,1)S(1)}, bf16[512,768]{1,0:T(8,128)(2,1)S(1)}, f32[512,768]{1,0:T(8,128)S(1)}, f32[1,768]{1,0:T(1,128)S(1)}) custom-call(s32[4]{0:T(128)S(1)} %copy-done.65, bf16[512,2304]{1,0:T(8,128)(2,1)S(1)} %copy-done.68, f32[512,768]{1,0:T(8,128)S(1)} %get-tuple-element.254.n2_ref, f32[3,768]{1,0:T(4,128)S(1)} %copy-done.62, ...), custom_call_target="tpu_custom_call" | custom-call | flops 12999999488 | bytes 1000 | tf_op jit(solution)/shard_map/self_turn/pallas_call | solution.py:844
  139.5 6.0 %mlp_back.3 = (bf16[512,3840]{1,0:T(8,128)(2,1)S(1)}, f32[512,768]{1,0:T(8,128)S(1)}, f32[1,768]{1,0:T(1,128)S(1)}) custom-call(bf16[512,3840]{1,0:T(8,128)(2,1)S(1)} %get-tuple-element.266.pack3_ref.refs_14_, f32[512,768]{1,0:T(8,128)S(1)} %get-tuple-element.267.de_ref, f32[512,768]{1,0:T(8,128)S(1)} %get-tuple-element.254.n2_ref, ...), custom_call_target="tpu_custom_call" | custom-call | flops 7314285568 | bytes 1000 | tf_op jit(solution)/shard_map/mlp_back/pallas_call | solution.py:844
  145.9 2.1 copy-done.90
  152.3 6.5 %context_back.3 = (bf16[512,768]{1,0:T(8,128)(2,1)S(1)}, f32[512,768]{1,0:T(8,128)S(1)}, bf16[512,1024]{1,0:T(8,128)(2,1)S(1)}, f32[1,768]{1,0:T(1,128)S(1)}) custom-call(bf16[512,3840]{1,0:T(8,128)(2,1)S(1)} %get-tuple-element.271.pack4_ref.refs_10_, f32[512,768]{1,0:T(8,128)S(1)} %get-tuple-element.272.db_ref, f32[512,768]{1,0:T(8,128)S(1)} %get-tuple-element.244.n1_ref, ...), custom_call_target="tpu_custom_call" | custom-call | flops 6400000000 | bytes 1000 | tf_op jit(solution)/shard_map/context_back/pallas_call | solution.py:844
  158.8 7.3 %collective-permute-done.19.refs_1_ = bf16[4,640,128]{2,1,0:T(8,128)(2,1)S(1)} collective-permute-done((bf16[4,640,128]{2,1,0:T(8,128)(2,1)S(1)}, bf16[4,640,128]{2,1,0:T(8,128)(2,1)S(1)}, u32[]{:S(2)}, u32[]{:S(2)}) %collective-permute-start.19) | collective-permute-done | bytes 655392 | tf_op jit(solution)/shard_map/ppermute | solution.py:367
  167.1 5.1 %attend_back.3 = (bf16[512,1024]{1,0:T(8,128)(2,1)S(1)}, bf16[192,2048]{1,0:T(8,128)(2,1)S(1)}) custom-call(s32[4]{0:T(128)S(1)} %copy-done.65, bf16[512,1024]{1,0:T(8,128)(2,1)S(1)} %get-tuple-element.236.refs_0_, bf16[192,2048]{1,0:T(8,128)(2,1)S(1)} %copy-done.70, bf16[512,1024]{1,0:T(8,128)(2,1)S(1)} %get-tuple-element.278.refs_2_), custom_call_target="tpu_custom_call" | custom-call | flops 6000000000 | bytes 1000 | tf_op jit(solution)/shard_map/attend_back/pallas_call | solution.py:213
  174.7 2.4 collective-permute-start.27
  177.2 1.7 flat_grads.4.flat_ref
  182.9 16.3 %flat_grads.5.flat_ref = bf16[19968,128]{1,0:T(8,128)(2,1)} custom-call(s32[2]{0:T(128)S(1)} %pad_add_fusion.side_ref, bf16[512,768]{1,0:T(8,128)(2,1)S(1)} %copy-done.14, bf16[512,768]{1,0:T(8,128)(2,1)S(1)} %copy-done.43, bf16[512,1024]{1,0:T(8,128)(2,1)S(1)} %get-tuple-element.310.refs_2_.dq_ref, bf16[512,1024]{1,0:T(8,128)(2,1)S(1)} %collective-permute-done.25.refs_3_, ...), custom_call_target="tpu_custom_call" | custom-call | flops 14000000000 | bytes 1000 | tf_op jit(solution)/shard_map/flat_grads/pallas_call | solution.py:350
  199.2 7.1 %collective-permute-done.27.refs_1_ = bf16[4,640,128]{2,1,0:T(8,128)(2,1)S(1)} collective-permute-done((bf16[4,640,128]{2,1,0:T(8,128)(2,1)S(1)}, bf16[4,640,128]{2,1,0:T(8,128)(2,1)S(1)}, u32[]{:S(2)}, u32[]{:S(2)}) %collective-permute-start.27) | collective-permute-done | bytes 655392 | tf_op jit(solution)/shard_map/ppermute | solution.py:367
  206.3 2.4 copy-done.66
  212.0 2.2 collective-permute-start.31
  214.3 2.9 input_grads.3
  217.2 3.9 %input_grads.2 = (bf16[256,768]{1,0:T(8,128)(2,1)}, bf16[256,768]{1,0:T(8,128)(2,1)}) custom-call(f32[512,768]{1,0:T(8,128)S(1)} %get-tuple-element.309.da_ref, bf16[512,1024]{1,0:T(8,128)(2,1)S(1)} %get-tuple-element.310.refs_2_.dq_ref, bf16[512,2048]{1,0:T(8,128)(2,1)} %get-tuple-element.234.refs_4_.dkv_ref, ...), custom_call_target="tpu_custom_call" | custom-call | flops 200000000 | bytes 1000 | tf_op jit(solution)/shard_map/input_grads/pallas_call | solution.py:931
  221.1 8.1 %collective-permute-done.29.refs_1_ = bf16[4,768,128]{2,1,0:T(8,128)(2,1)S(1)} collective-permute-done((bf16[4,768,128]{2,1,0:T(8,128)(2,1)S(1)}, bf16[4,768,128]{2,1,0:T(8,128)(2,1)S(1)}, u32[]{:S(2)}, u32[]{:S(2)}) %collective-permute-start.29) | collective-permute-done | bytes 786464 | tf_op jit(solution)/shard_map/ppermute | solution.py:367
  231.4 3.6 %collective-permute-start.34 = (bf16[1,1280,128]{2,1,0:T(8,128)(2,1)S(1)}, bf16[1,1280,128]{2,1,0:T(8,128)(2,1)S(1)}, u32[]{:S(2)}, u32[]{:S(2)}) collective-permute-start(bf16[1,1280,128]{2,1,0:T(8,128)(2,1)S(1)} %add_convert_fusion.1), channel_id=1, source_target_pairs={{0,8},{1,9},{10,2},{11,3},{12,4},{13,5},{14,6},{15,7},{16,24},{17,... | collective-permute-start | bytes 983048 | tf_op jit(solution)/shard_map/ppermute | solution.py:1362
  235.1 10.0 %collective-permute-done.35 = f32[3,1792]{1,0:T(4,128)S(1)} collective-permute-done((f32[3,1792]{1,0:T(4,128)S(1)}, f32[3,1792]{1,0:T(4,128)S(1)}, u32[]{:S(2)}, u32[]{:S(2)}) %collective-permute-start.35) | collective-permute-done | bytes 21536 | tf_op jit(solution)/shard_map/ppermute | solution.py:367
  245.1 2.0 collective-permute-done.33.refs_1_
  252.8 9.6 %collective-permute-done.40 = f32[3,1792]{1,0:T(4,128)S(1)} collective-permute-done((f32[3,1792]{1,0:T(4,128)S(1)}, f32[3,1792]{1,0:T(4,128)S(1)}, u32[]{:S(2)}, u32[]{:S(2)}) %collective-permute-start.40) | collective-permute-done | bytes 21536 | tf_op jit(solution)/shard_map/ppermute | solution.py:367
  266.0 5.9 %collective-permute-start.44 = (f32[3,1792]{1,0:T(4,128)S(1)}, f32[3,1792]{1,0:T(4,128)S(1)}, u32[]{:S(2)}, u32[]{:S(2)}) collective-permute-start(f32[3,1792]{1,0:T(4,128)S(1)} %add.64), channel_id=1, source_target_pairs={{0,1},{1,0},{2,3},{3,2},{4,5},{5,4},{6,7},{7,6},{8,9},{9,8},{10,11... | collective-permute-start | bytes 64520 | tf_op jit(solution)/shard_map/ppermute | solution.py:367
  274.2 2.1 collective-permute-start.45
  276.3 5.9 %collective-permute-done.45.refs_7_ = bf16[1,608,128]{2,1,0:T(8,128)(2,1)S(1)} collective-permute-done((bf16[1,608,128]{2,1,0:T(8,128)(2,1)S(1)}, bf16[1,608,128]{2,1,0:T(8,128)(2,1)S(1)}, u32[]{:S(2)}, u32[]{:S(2)}) %collective-permute-start.45) | collective-permute-done | bytes 155680 | tf_op jit(solution)/shard_map/ppermute | solution.py:367
  283.7 5.1 %collective-permute-done.47.refs_9_ = bf16[1,384,128]{2,1,0:T(8,128)(2,1)S(1)} collective-permute-done((bf16[1,384,128]{2,1,0:T(8,128)(2,1)S(1)}, bf16[1,384,128]{2,1,0:T(8,128)(2,1)S(1)}, u32[]{:S(2)}, u32[]{:S(2)}) %collective-permute-start.47) | collective-permute-done | bytes 98336 | tf_op jit(solution)/shard_map/ppermute | solution.py:367
  288.8 1.8 finish.1
  290.7 10.2 %collective-permute-start.48 = (f32[2528,128]{1,0:T(8,128)S(1)}, f32[2528,128]{1,0:T(8,128)S(1)}, u32[]{:S(2)}, u32[]{:S(2)}) collective-permute-start(f32[2528,128]{1,0:T(8,128)S(1)} %get-tuple-element.370), channel_id=1, source_target_pairs={{0,1},{1,0},{2,3},{3,2},{4,5},{5,4},{6,7},{7,6},{8,9},{9,8},{10,11... | collective-permute-start | bytes 3883016 | tf_op jit(solution)/shard_map/ppermute | solution.py:367
  302.1 1.4 collective-permute-done.48.far_ref
  303.5 2.2 join.1
  (305 shorter events, 57.4 us)
Async XLA Ops:
  0.6 14.2 %collective-permute-start.2 = (bf16[72,1024]{1,0:T(8,128)(2,1)}, bf16[72,1024]{1,0:T(8,128)(2,1)S(1)}, u32[]{:S(2)}, u32[]{:S(2)}) collective-permute-start(bf16[72,1024]{1,0:T(8,128)(2,1)} %param.22), channel_id=1, source_target_pairs={{0,16},{16,0},{1,17},{17,1},{2,18},{18,2},{3,19},{19,3},{4,20},{20... | collective-permute-start | bytes 442376 | tf_op jit(solution)/shard_map/ppermute | solution.py:371
  0.7 16.2 %collective-permute-start = (bf16[256,768]{1,0:T(8,128)(2,1)}, bf16[256,768]{1,0:T(8,128)(2,1)S(1)}, u32[]{:S(2)}, u32[]{:S(2)}) collective-permute-start(bf16[256,768]{1,0:T(8,128)(2,1)} %param.21), channel_id=1, source_target_pairs={{0,16},{16,0},{1,17},{17,1},{2,18},{18,2},{3,19},{19,3},{4,20},{20... | collective-permute-start | bytes 1179656 | tf_op jit(solution)/shard_map/ppermute | solution.py:371
  2.2 11.9 %collective-permute-start.1 = (s32[2]{0:T(128)}, s32[2]{0:T(128)S(1)}, u32[]{:S(2)}, u32[]{:S(2)}) collective-permute-start(s32[2]{0:T(128)} %param.23), channel_id=1, source_target_pairs={{0,16},{16,0},{1,17},{17,1},{2,18},{18,2},{3,19},{19,3},{4,20},{20... | collective-permute-start | bytes 32 | tf_op jit(solution)/shard_map/ppermute | solution.py:371
  15.2 15.7 %collective-permute-start.3 = (bf16[192,1024]{1,0:T(8,128)(2,1)S(1)}, bf16[192,1024]{1,0:T(8,128)(2,1)S(1)}, u32[]{:S(2)}, u32[]{:S(2)}) collective-permute-start(bf16[192,1024]{1,0:T(8,128)(2,1)S(1)} %fusion.o_ref.x_ref.refs_0_), channel_id=1, source_target_pairs={{0,1},{1,0},{2,3},{3,2},{4,5},{5,4},{6,7},{7,6},{8,9},{9,8},{10,11... | collective-permute-start | bytes 1179656 | tf_op jit(solution)/shard_map/ppermute | solution.py:367
  18.1 14.6 %collective-permute-start.5 = (bf16[72,1024]{1,0:T(8,128)(2,1)}, bf16[72,1024]{1,0:T(8,128)(2,1)S(1)}, u32[]{:S(2)}, u32[]{:S(2)}) collective-permute-start(bf16[72,1024]{1,0:T(8,128)(2,1)} %param.41), channel_id=1, source_target_pairs={{0,16},{16,0},{1,17},{17,1},{2,18},{18,2},{3,19},{19,3},{4,20},{20... | collective-permute-start | bytes 442376 | tf_op jit(solution)/shard_map/ppermute | solution.py:371
  30.9 6.1 %collective-permute-start.4 = (bf16[192,2048]{1,0:T(8,128)(2,1)S(1)}, bf16[192,2048]{1,0:T(8,128)(2,1)S(1)}, u32[]{:S(2)}, u32[]{:S(2)}) collective-permute-start(bf16[192,2048]{1,0:T(8,128)(2,1)S(1)} %get-tuple-element.197.pack1_ref.refs_4_), channel_id=1, source_target_pairs={{0,1},{1,0},{2,3},{3,2},{4,5},{5,4},{6,7},{7,6},{8,9},{9,8},{10,11... | collective-permute-start | bytes 2359304 | tf_op jit(solution)/shard_map/ppermute | solution.py:367
  31.9 16.3 %collective-permute-start.6 = (bf16[256,768]{1,0:T(8,128)(2,1)S(1)}, bf16[256,768]{1,0:T(8,128)(2,1)S(1)}, u32[]{:S(2)}, u32[]{:S(2)}) collective-permute-start(bf16[256,768]{1,0:T(8,128)(2,1)S(1)} %copy-done.71), channel_id=1, source_target_pairs={{0,16},{16,0},{1,17},{17,1},{2,18},{18,2},{3,19},{19,3},{4,20},{20... | collective-permute-start | bytes 1179656 | tf_op jit(solution)/shard_map/ppermute | solution.py:371
  37.0 11.2 %collective-permute-start.7 = (bf16[192,2048]{1,0:T(8,128)(2,1)S(1)}, bf16[192,2048]{1,0:T(8,128)(2,1)S(1)}, u32[]{:S(2)}, u32[]{:S(2)}) collective-permute-start(bf16[192,2048]{1,0:T(8,128)(2,1)S(1)} %get-tuple-element.208.refs_10_), channel_id=1, source_target_pairs={{0,1},{1,0},{2,3},{3,2},{4,5},{5,4},{6,7},{7,6},{8,9},{9,8},{10,11... | collective-permute-start | bytes 2359304 | tf_op jit(solution)/shard_map/ppermute | solution.py:367
  53.2 4.1 %collective-permute-start.9 = (bf16[192,2048]{1,0:T(8,128)(2,1)S(1)}, bf16[192,2048]{1,0:T(8,128)(2,1)S(1)}, u32[]{:S(2)}, u32[]{:S(2)}) collective-permute-start(bf16[192,2048]{1,0:T(8,128)(2,1)S(1)} %get-tuple-element.214.pack4_ref.refs_8_), channel_id=1, source_target_pairs={{0,1},{1,0},{2,3},{3,2},{4,5},{5,4},{6,7},{7,6},{8,9},{9,8},{10,11... | collective-permute-start | bytes 2359304 | tf_op jit(solution)/shard_map/ppermute | solution.py:367
  65.5 37.7 %collective-permute-start.13 = (bf16[512,2048]{1,0:T(8,128)(2,1)}, bf16[512,2048]{1,0:T(8,128)(2,1)}, u32[]{:S(2)}, u32[]{:S(2)}) collective-permute-start(bf16[512,2048]{1,0:T(8,128)(2,1)} %get-tuple-element.234.refs_4_.dkv_ref), channel_id=1, source_target_pairs={{0,1},{1,0},{2,3},{3,2},{4,5},{5,4},{6,7},{7,6},{8,9},{9,8},{10,11... | collective-permute-start | bytes 6291464 | tf_op jit(solution)/shard_map/ppermute | solution.py:367
  66.0 37.2 %collective-permute-start.12 = (bf16[512,768]{1,0:T(8,128)(2,1)}, bf16[512,768]{1,0:T(8,128)(2,1)S(1)}, u32[]{:S(2)}, u32[]{:S(2)}) collective-permute-start(bf16[512,768]{1,0:T(8,128)(2,1)} %copy-done.12), channel_id=1, source_target_pairs={{0,1},{1,0},{2,3},{3,2},{4,5},{5,4},{6,7},{7,6},{8,9},{9,8},{10,11... | collective-permute-start | bytes 2359304 | tf_op jit(solution)/shard_map/ppermute | solution.py:367
  66.2 29.2 %collective-permute-start.10 = (bf16[192,1024]{1,0:T(8,128)(2,1)}, bf16[192,1024]{1,0:T(8,128)(2,1)S(1)}, u32[]{:S(2)}, u32[]{:S(2)}) collective-permute-start(bf16[192,1024]{1,0:T(8,128)(2,1)} %copy-done.15), channel_id=1, source_target_pairs={{0,1},{1,0},{2,3},{3,2},{4,5},{5,4},{6,7},{7,6},{8,9},{9,8},{10,11... | collective-permute-start | bytes 1179656 | tf_op jit(solution)/shard_map/ppermute | solution.py:367
  66.5 28.9 %collective-permute-start.11 = (bf16[192,1024]{1,0:T(8,128)(2,1)}, bf16[192,1024]{1,0:T(8,128)(2,1)S(1)}, u32[]{:S(2)}, u32[]{:S(2)}) collective-permute-start(bf16[192,1024]{1,0:T(8,128)(2,1)} %copy-done.59), channel_id=1, source_target_pairs={{0,1},{1,0},{2,3},{3,2},{4,5},{5,4},{6,7},{7,6},{8,9},{9,8},{10,11... | collective-permute-start | bytes 1179656 | tf_op jit(solution)/shard_map/ppermute | solution.py:367
  103.2 17.4 %collective-permute-start.18 = (bf16[512,1792]{1,0:T(8,128)(2,1)S(1)}, bf16[512,1792]{1,0:T(8,128)(2,1)S(1)}, u32[]{:S(2)}, u32[]{:S(2)}) collective-permute-start(bf16[512,1792]{1,0:T(8,128)(2,1)S(1)} %get-tuple-element.243.pack1_ref.refs_6_), channel_id=1, source_target_pairs={{0,1},{1,0},{2,3},{3,2},{4,5},{5,4},{6,7},{7,6},{8,9},{9,8},{10,11... | collective-permute-start | bytes 5505032 | tf_op jit(solution)/shard_map/ppermute | solution.py:367
  103.6 16.1 %collective-permute-start.14 = (bf16[4,640,128]{2,1,0:T(8,128)(2,1)S(1)}, bf16[4,640,128]{2,1,0:T(8,128)(2,1)S(1)}, u32[]{:S(2)}, u32[]{:S(2)}) collective-permute-start(bf16[4,640,128]{2,1,0:T(8,128)(2,1)S(1)} %get-tuple-element.239), channel_id=1, source_target_pairs={{0,2},{1,3},{2,0},{3,1},{4,6},{5,7},{6,4},{7,5},{8,10},{9,11},{10,... | collective-permute-start | bytes 1966088 | tf_op jit(solution)/shard_map/ppermute | solution.py:367
  104.8 15.8 %collective-permute-start.15 = (bf16[4,640,128]{2,1,0:T(8,128)(2,1)S(1)}, bf16[4,640,128]{2,1,0:T(8,128)(2,1)S(1)}, u32[]{:S(2)}, u32[]{:S(2)}) collective-permute-start(bf16[4,640,128]{2,1,0:T(8,128)(2,1)S(1)} %get-tuple-element.240), channel_id=1, source_target_pairs={{0,4},{1,5},{2,6},{3,7},{4,0},{5,1},{6,2},{7,3},{8,12},{9,13},{10,... | collective-permute-start | bytes 1966088 | tf_op jit(solution)/shard_map/ppermute | solution.py:367
  120.6 18.1 %collective-permute-start.21 = (bf16[512,3840]{1,0:T(8,128)(2,1)S(1)}, bf16[512,3840]{1,0:T(8,128)(2,1)}, u32[]{:S(2)}, u32[]{:S(2)}) collective-permute-start(bf16[512,3840]{1,0:T(8,128)(2,1)S(1)} %get-tuple-element.265.refs_12_), channel_id=1, source_target_pairs={{0,1},{1,0},{2,3},{3,2},{4,5},{5,4},{6,7},{7,6},{8,9},{9,8},{10,11... | collective-permute-start | bytes 11796488 | tf_op jit(solution)/shard_map/ppermute | solution.py:367
  122.0 16.6 %collective-permute-start.16 = (bf16[4,640,128]{2,1,0:T(8,128)(2,1)}, bf16[4,640,128]{2,1,0:T(8,128)(2,1)S(1)}, u32[]{:S(2)}, u32[]{:S(2)}) collective-permute-start(bf16[4,640,128]{2,1,0:T(8,128)(2,1)} %get-tuple-element.248), channel_id=1, source_target_pairs={{0,2},{1,3},{2,0},{3,1},{4,6},{5,7},{6,4},{7,5},{8,10},{9,11},{10,... | collective-permute-start | bytes 1966088 | tf_op jit(solution)/shard_map/ppermute | solution.py:367
  122.3 16.3 %collective-permute-start.17 = (bf16[4,640,128]{2,1,0:T(8,128)(2,1)S(1)}, bf16[4,640,128]{2,1,0:T(8,128)(2,1)S(1)}, u32[]{:S(2)}, u32[]{:S(2)}) collective-permute-start(bf16[4,640,128]{2,1,0:T(8,128)(2,1)S(1)} %get-tuple-element.249), channel_id=1, source_target_pairs={{0,4},{1,5},{2,6},{3,7},{4,0},{5,1},{6,2},{7,3},{8,12},{9,13},{10,... | collective-permute-start | bytes 1966088 | tf_op jit(solution)/shard_map/ppermute | solution.py:367
  138.6 7.2 %collective-permute-start.22 = (bf16[512,3840]{1,0:T(8,128)(2,1)S(1)}, bf16[512,3840]{1,0:T(8,128)(2,1)S(1)}, u32[]{:S(2)}, u32[]{:S(2)}) collective-permute-start(bf16[512,3840]{1,0:T(8,128)(2,1)S(1)} %get-tuple-element.266.pack3_ref.refs_14_), channel_id=1, source_target_pairs={{0,1},{1,0},{2,3},{3,2},{4,5},{5,4},{6,7},{7,6},{8,9},{9,8},{10,11... | collective-permute-start | bytes 11796488 | tf_op jit(solution)/shard_map/ppermute | solution.py:367
  148.0 19.1 %collective-permute-start.23 = (bf16[512,3840]{1,0:T(8,128)(2,1)S(1)}, bf16[512,3840]{1,0:T(8,128)(2,1)S(1)}, u32[]{:S(2)}, u32[]{:S(2)}) collective-permute-start(bf16[512,3840]{1,0:T(8,128)(2,1)S(1)} %get-tuple-element.271.pack4_ref.refs_10_), channel_id=1, source_target_pairs={{0,1},{1,0},{2,3},{3,2},{4,5},{5,4},{6,7},{7,6},{8,9},{9,8},{10,11... | collective-permute-start | bytes 11796488 | tf_op jit(solution)/shard_map/ppermute | solution.py:367
  149.7 16.4 %collective-permute-start.19 = (bf16[4,640,128]{2,1,0:T(8,128)(2,1)S(1)}, bf16[4,640,128]{2,1,0:T(8,128)(2,1)S(1)}, u32[]{:S(2)}, u32[]{:S(2)}) collective-permute-start(bf16[4,640,128]{2,1,0:T(8,128)(2,1)S(1)} %get-tuple-element.262), channel_id=1, source_target_pairs={{0,4},{1,5},{2,6},{3,7},{4,0},{5,1},{6,2},{7,3},{8,12},{9,13},{10,... | collective-permute-start | bytes 1966088 | tf_op jit(solution)/shard_map/ppermute | solution.py:367
  151.0 16.0 %collective-permute-start.20 = (bf16[4,640,128]{2,1,0:T(8,128)(2,1)S(1)}, bf16[4,640,128]{2,1,0:T(8,128)(2,1)S(1)}, u32[]{:S(2)}, u32[]{:S(2)}) collective-permute-start(bf16[4,640,128]{2,1,0:T(8,128)(2,1)S(1)} %get-tuple-element.263), channel_id=1, source_target_pairs={{0,2},{1,3},{2,0},{3,1},{4,6},{5,7},{6,4},{7,5},{8,10},{9,11},{10,... | collective-permute-start | bytes 1966088 | tf_op jit(solution)/shard_map/ppermute | solution.py:367
  172.2 4.9 %collective-permute-start.24 = (bf16[192,2048]{1,0:T(8,128)(2,1)S(1)}, bf16[192,2048]{1,0:T(8,128)(2,1)S(1)}, u32[]{:S(2)}, u32[]{:S(2)}) collective-permute-start(bf16[192,2048]{1,0:T(8,128)(2,1)S(1)} %get-tuple-element.280.refs_2_.dkv_ref), channel_id=1, source_target_pairs={{0,1},{1,0},{2,3},{3,2},{4,5},{5,4},{6,7},{7,6},{8,9},{9,8},{10,11... | collective-permute-start | bytes 2359304 | tf_op jit(solution)/shard_map/ppermute | solution.py:367
  173.4 7.5 %collective-permute-start.25 = (bf16[512,1024]{1,0:T(8,128)(2,1)S(1)}, bf16[512,1024]{1,0:T(8,128)(2,1)S(1)}, u32[]{:S(2)}, u32[]{:S(2)}) collective-permute-start(bf16[512,1024]{1,0:T(8,128)(2,1)S(1)} %get-tuple-element.310.refs_2_.dq_ref), channel_id=1, source_target_pairs={{0,1},{1,0},{2,3},{3,2},{4,5},{5,4},{6,7},{7,6},{8,9},{9,8},{10,11... | collective-permute-start | bytes 3145736 | tf_op jit(solution)/shard_map/ppermute | solution.py:367
  173.4 7.4 %collective-permute-start.26 = (bf16[512,768]{1,0:T(8,128)(2,1)S(1)}, bf16[512,768]{1,0:T(8,128)(2,1)S(1)}, u32[]{:S(2)}, u32[]{:S(2)}) collective-permute-start(bf16[512,768]{1,0:T(8,128)(2,1)S(1)} %get-tuple-element.285.refs_8_), channel_id=1, source_target_pairs={{0,1},{1,0},{2,3},{3,2},{4,5},{5,4},{6,7},{7,6},{8,9},{9,8},{10,11... | collective-permute-start | bytes 2359304 | tf_op jit(solution)/shard_map/ppermute | solution.py:367
  174.7 31.6 %collective-permute-start.27 = (bf16[4,640,128]{2,1,0:T(8,128)(2,1)S(1)}, bf16[4,640,128]{2,1,0:T(8,128)(2,1)S(1)}, u32[]{:S(2)}, u32[]{:S(2)}) collective-permute-start(bf16[4,640,128]{2,1,0:T(8,128)(2,1)S(1)} %get-tuple-element.293), channel_id=1, source_target_pairs={{0,8},{1,9},{2,10},{3,11},{4,12},{5,13},{6,14},{7,15},{8,0},{9,1},... | collective-permute-start | bytes 1966088 | tf_op jit(solution)/shard_map/ppermute | solution.py:367
  179.6 26.8 %collective-permute-start.28 = (bf16[2,1280,128]{2,1,0:T(8,128)(2,1)S(1)}, bf16[2,1280,128]{2,1,0:T(8,128)(2,1)S(1)}, u32[]{:S(2)}, u32[]{:S(2)}) collective-permute-start(bf16[2,1280,128]{2,1,0:T(8,128)(2,1)S(1)} %get-tuple-element.294), channel_id=1, source_target_pairs={{0,2},{1,3},{2,0},{3,1},{4,6},{5,7},{6,4},{7,5},{8,10},{9,11},{10,... | collective-permute-start | bytes 1966088 | tf_op jit(solution)/shard_map/ppermute | solution.py:367
  210.5 18.7 %collective-permute-start.29 = (bf16[4,768,128]{2,1,0:T(8,128)(2,1)S(1)}, bf16[4,768,128]{2,1,0:T(8,128)(2,1)S(1)}, u32[]{:S(2)}, u32[]{:S(2)}) collective-permute-start(bf16[4,768,128]{2,1,0:T(8,128)(2,1)S(1)} %get-tuple-element.306), channel_id=1, source_target_pairs={{0,2},{1,3},{2,0},{3,1},{4,6},{5,7},{6,4},{7,5},{8,10},{9,11},{10,... | collective-permute-start | bytes 2359304 | tf_op jit(solution)/shard_map/ppermute | solution.py:367
  211.8 9.3 %collective-permute-start.30 = (bf16[1,1280,128]{2,1,0:T(8,128)(2,1)S(1)}, bf16[1,1280,128]{2,1,0:T(8,128)(2,1)S(1)}, u32[]{:S(2)}, u32[]{:S(2)}) collective-permute-start(bf16[1,1280,128]{2,1,0:T(8,128)(2,1)S(1)} %get-tuple-element.307), channel_id=1, source_target_pairs={{0,4},{1,5},{2,6},{3,7},{4,0},{5,1},{6,2},{7,3},{8,12},{9,13},{10,... | collective-permute-start | bytes 983048 | tf_op jit(solution)/shard_map/ppermute | solution.py:367
  212.0 9.1 %collective-permute-start.31 = (f32[3,1792]{1,0:T(4,128)S(1)}, f32[3,1792]{1,0:T(4,128)S(1)}, u32[]{:S(2)}, u32[]{:S(2)}) collective-permute-start(f32[3,1792]{1,0:T(4,128)S(1)} %maximum_maximum_fusion), channel_id=1, source_target_pairs={{0,8},{1,9},{2,10},{3,11},{4,12},{5,13},{6,14},{7,15},{8,0},{9,1},... | collective-permute-start | bytes 64520 | tf_op jit(solution)/shard_map/ppermute | solution.py:367
  230.0 15.1 %collective-permute-start.32 = (bf16[2,768,128]{2,1,0:T(8,128)(2,1)S(1)}, bf16[2,768,128]{2,1,0:T(8,128)(2,1)S(1)}, u32[]{:S(2)}, u32[]{:S(2)}) collective-permute-start(bf16[2,768,128]{2,1,0:T(8,128)(2,1)S(1)} %get-tuple-element.329), channel_id=1, source_target_pairs={{0,4},{1,5},{2,6},{3,7},{4,0},{5,1},{6,2},{7,3},{8,12},{9,13},{10,... | collective-permute-start | bytes 1179656 | tf_op jit(solution)/shard_map/ppermute | solution.py:367
  230.0 17.1 %collective-permute-start.33 = (bf16[4,736,128]{2,1,0:T(8,128)(2,1)S(1)}, bf16[4,736,128]{2,1,0:T(8,128)(2,1)S(1)}, u32[]{:S(2)}, u32[]{:S(2)}) collective-permute-start(bf16[4,736,128]{2,1,0:T(8,128)(2,1)S(1)} %get-tuple-element.330), channel_id=1, source_target_pairs={{0,2},{1,3},{2,0},{3,1},{4,6},{5,7},{6,4},{7,5},{8,10},{9,11},{10,... | collective-permute-start | bytes 2261000 | tf_op jit(solution)/shard_map/ppermute | solution.py:367
  231.4 13.7 %collective-permute-start.34 = (bf16[1,1280,128]{2,1,0:T(8,128)(2,1)S(1)}, bf16[1,1280,128]{2,1,0:T(8,128)(2,1)S(1)}, u32[]{:S(2)}, u32[]{:S(2)}) collective-permute-start(bf16[1,1280,128]{2,1,0:T(8,128)(2,1)S(1)} %add_convert_fusion.1), channel_id=1, source_target_pairs={{0,8},{1,9},{10,2},{11,3},{12,4},{13,5},{14,6},{15,7},{16,24},{17,... | collective-permute-start | bytes 983048 | tf_op jit(solution)/shard_map/ppermute | solution.py:1362
  235.0 10.1 %collective-permute-start.35 = (f32[3,1792]{1,0:T(4,128)S(1)}, f32[3,1792]{1,0:T(4,128)S(1)}, u32[]{:S(2)}, u32[]{:S(2)}) collective-permute-start(f32[3,1792]{1,0:T(4,128)S(1)} %add.60), channel_id=1, source_target_pairs={{0,4},{1,5},{2,6},{3,7},{4,0},{5,1},{6,2},{7,3},{8,12},{9,13},{10,... | collective-permute-start | bytes 64520 | tf_op jit(solution)/shard_map/ppermute | solution.py:367
  247.9 14.6 %collective-permute-start.37 = (bf16[2,736,128]{2,1,0:T(8,128)(2,1)S(1)}, bf16[2,736,128]{2,1,0:T(8,128)(2,1)S(1)}, u32[]{:S(2)}, u32[]{:S(2)}) collective-permute-start(bf16[2,736,128]{2,1,0:T(8,128)(2,1)S(1)} %get-tuple-element.340), channel_id=1, source_target_pairs={{0,4},{1,5},{2,6},{3,7},{4,0},{5,1},{6,2},{7,3},{8,12},{9,13},{10,... | collective-permute-start | bytes 1130504 | tf_op jit(solution)/shard_map/ppermute | solution.py:367
  249.1 13.4 %collective-permute-start.38 = (bf16[4,608,128]{2,1,0:T(8,128)(2,1)S(1)}, bf16[4,608,128]{2,1,0:T(8,128)(2,1)S(1)}, u32[]{:S(2)}, u32[]{:S(2)}) collective-permute-start(bf16[4,608,128]{2,1,0:T(8,128)(2,1)S(1)} %get-tuple-element.341), channel_id=1, source_target_pairs={{0,2},{1,3},{2,0},{3,1},{4,6},{5,7},{6,4},{7,5},{8,10},{9,11},{10,... | collective-permute-start | bytes 1867784 | tf_op jit(solution)/shard_map/ppermute | solution.py:367
  250.4 12.1 %collective-permute-start.39 = (bf16[1,1280,128]{2,1,0:T(8,128)(2,1)S(1)}, bf16[1,1280,128]{2,1,0:T(8,128)(2,1)S(1)}, u32[]{:S(2)}, u32[]{:S(2)}) collective-permute-start(bf16[1,1280,128]{2,1,0:T(8,128)(2,1)S(1)} %add_convert_fusion), channel_id=1, source_target_pairs={{16,0},{17,1},{18,2},{19,3},{20,4},{21,5},{22,6},{23,7},{24,8},{25... | collective-permute-start | bytes 983048 | tf_op jit(solution)/shard_map/ppermute | solution.py:1364
  252.3 10.1 %collective-permute-start.36 = (bf16[1,768,128]{2,1,0:T(8,128)(2,1)S(1)}, bf16[1,768,128]{2,1,0:T(8,128)(2,1)S(1)}, u32[]{:S(2)}, u32[]{:S(2)}) collective-permute-start(bf16[1,768,128]{2,1,0:T(8,128)(2,1)S(1)} %get-tuple-element.337), channel_id=1, source_target_pairs={{0,8},{1,9},{2,10},{3,11},{4,12},{5,13},{6,14},{7,15},{8,0},{9,1},... | collective-permute-start | bytes 589832 | tf_op jit(solution)/shard_map/ppermute | solution.py:367
  252.6 9.9 %collective-permute-start.40 = (f32[3,1792]{1,0:T(4,128)S(1)}, f32[3,1792]{1,0:T(4,128)S(1)}, u32[]{:S(2)}, u32[]{:S(2)}) collective-permute-start(f32[3,1792]{1,0:T(4,128)S(1)} %add.62), channel_id=1, source_target_pairs={{0,2},{1,3},{2,0},{3,1},{4,6},{5,7},{6,4},{7,5},{8,10},{9,11},{10,... | collective-permute-start | bytes 64520 | tf_op jit(solution)/shard_map/ppermute | solution.py:367
  262.5 10.3 %collective-permute-start.43 = (bf16[4,384,128]{2,1,0:T(8,128)(2,1)S(1)}, bf16[4,384,128]{2,1,0:T(8,128)(2,1)S(1)}, u32[]{:S(2)}, u32[]{:S(2)}) collective-permute-start(bf16[4,384,128]{2,1,0:T(8,128)(2,1)S(1)} %get-tuple-element.353), channel_id=1, source_target_pairs={{0,2},{1,3},{2,0},{3,1},{4,6},{5,7},{6,4},{7,5},{8,10},{9,11},{10,... | collective-permute-start | bytes 1179656 | tf_op jit(solution)/shard_map/ppermute | solution.py:367
  264.5 8.3 %collective-permute-start.42 = (bf16[2,608,128]{2,1,0:T(8,128)(2,1)S(1)}, bf16[2,608,128]{2,1,0:T(8,128)(2,1)S(1)}, u32[]{:S(2)}, u32[]{:S(2)}) collective-permute-start(bf16[2,608,128]{2,1,0:T(8,128)(2,1)S(1)} %get-tuple-element.352), channel_id=1, source_target_pairs={{0,4},{1,5},{2,6},{3,7},{4,0},{5,1},{6,2},{7,3},{8,12},{9,13},{10,... | collective-permute-start | bytes 933896 | tf_op jit(solution)/shard_map/ppermute | solution.py:367
  265.2 7.6 %collective-permute-start.41 = (bf16[1,736,128]{2,1,0:T(8,128)(2,1)S(1)}, bf16[1,736,128]{2,1,0:T(8,128)(2,1)S(1)}, u32[]{:S(2)}, u32[]{:S(2)}) collective-permute-start(bf16[1,736,128]{2,1,0:T(8,128)(2,1)S(1)} %get-tuple-element.349), channel_id=1, source_target_pairs={{0,8},{1,9},{2,10},{3,11},{4,12},{5,13},{6,14},{7,15},{8,0},{9,1},... | collective-permute-start | bytes 565256 | tf_op jit(solution)/shard_map/ppermute | solution.py:367
  266.0 6.7 %collective-permute-start.44 = (f32[3,1792]{1,0:T(4,128)S(1)}, f32[3,1792]{1,0:T(4,128)S(1)}, u32[]{:S(2)}, u32[]{:S(2)}) collective-permute-start(f32[3,1792]{1,0:T(4,128)S(1)} %add.64), channel_id=1, source_target_pairs={{0,1},{1,0},{2,3},{3,2},{4,5},{5,4},{6,7},{7,6},{8,9},{9,8},{10,11... | collective-permute-start | bytes 64520 | tf_op jit(solution)/shard_map/ppermute | solution.py:367
  273.4 8.8 %collective-permute-start.46 = (bf16[2,384,128]{2,1,0:T(8,128)(2,1)S(1)}, bf16[2,384,128]{2,1,0:T(8,128)(2,1)S(1)}, u32[]{:S(2)}, u32[]{:S(2)}) collective-permute-start(bf16[2,384,128]{2,1,0:T(8,128)(2,1)S(1)} %get-tuple-element.362), channel_id=1, source_target_pairs={{0,4},{1,5},{2,6},{3,7},{4,0},{5,1},{6,2},{7,3},{8,12},{9,13},{10,... | collective-permute-start | bytes 589832 | tf_op jit(solution)/shard_map/ppermute | solution.py:367
  274.2 8.0 %collective-permute-start.45 = (bf16[1,608,128]{2,1,0:T(8,128)(2,1)S(1)}, bf16[1,608,128]{2,1,0:T(8,128)(2,1)S(1)}, u32[]{:S(2)}, u32[]{:S(2)}) collective-permute-start(bf16[1,608,128]{2,1,0:T(8,128)(2,1)S(1)} %get-tuple-element.359), channel_id=1, source_target_pairs={{0,8},{1,9},{2,10},{3,11},{4,12},{5,13},{6,14},{7,15},{8,0},{9,1},... | collective-permute-start | bytes 466952 | tf_op jit(solution)/shard_map/ppermute | solution.py:367
  282.8 6.0 %collective-permute-start.47 = (bf16[1,384,128]{2,1,0:T(8,128)(2,1)S(1)}, bf16[1,384,128]{2,1,0:T(8,128)(2,1)S(1)}, u32[]{:S(2)}, u32[]{:S(2)}) collective-permute-start(bf16[1,384,128]{2,1,0:T(8,128)(2,1)S(1)} %get-tuple-element.367), channel_id=1, source_target_pairs={{0,8},{1,9},{2,10},{3,11},{4,12},{5,13},{6,14},{7,15},{8,0},{9,1},... | collective-permute-start | bytes 294920 | tf_op jit(solution)/shard_map/ppermute | solution.py:367
  290.7 12.9 %collective-permute-start.48 = (f32[2528,128]{1,0:T(8,128)S(1)}, f32[2528,128]{1,0:T(8,128)S(1)}, u32[]{:S(2)}, u32[]{:S(2)}) collective-permute-start(f32[2528,128]{1,0:T(8,128)S(1)} %get-tuple-element.370), channel_id=1, source_target_pairs={{0,1},{1,0},{2,3},{3,2},{4,5},{5,4},{6,7},{7,6},{8,9},{9,8},{10,11... | collective-permute-start | bytes 3883016 | tf_op jit(solution)/shard_map/ppermute | solution.py:367
  (98 other events, 1011.5 us)
where the time goes:
time: 310 us; the launch traced here: 306 us
  Pallas kernels  141 us (45%)
  waiting for transfers between devices  72.7 us (23%)
  starting transfers between devices  55.9 us (18%)
  local copies, waits for them, and re-layouts  28.6 us (9%)
    pallas_call x10, Pallas kernels, fused(): pl.pallas_call(kernel, in_specs=in_specs, out_specs=[vmem] * len(outs), o...  83.9 us
    ppermute x42, waiting for transfers between devices, dp_swap(): return lax.ppermute(block, 'dp', [(i, i ^ bit) for i in range(count)])  62.3 us
    ppermute x42, starting transfers between devices, dp_swap(): return lax.ppermute(block, 'dp', [(i, i ^ bit) for i in range(count)])  48.5 us
    unnamed x194, local copies, waits for them, and re-layouts  27.3 us
    pallas_call x3, Pallas kernels, flat_grads(): pl.pallas_call(functools.partial(flat_kernel, plans=plans, found=found, q...  23.8 us
    pallas_call x2, Pallas kernels, attend_back(): pl.pallas_call(functools.partial(body, pairs=pairs, blocks=blocks, cols=c...  11.7 us
    ppermute x5, waiting for transfers between devices, stream_swap(): return lax.ppermute(block, 'stream', [(0, 1), (1, 0)])  10.4 us
    pallas_call x11, Pallas kernels, add_split(): pl.pallas_call(functools.partial(add_split_kernel, plan=tuple(plan), inpu...  7.95 us
  transfers between devices with their start and end apart: 49, of which 17 were waited for; matrix products, arithmetic and copies ran while one was open for 2% of the time, Pallas kernels for 40%

commit v1 on v0

--- a/solution.py
+++ b/solution.py
@@ -115,7 +115,7 @@
         in_specs=[pl.BlockSpec(memory_space=pltpu.SMEM)] + [vmem] * (len(operands) - 1),
         out_specs=vmem,
         out_shape=jax.ShapeDtypeStruct((rows, blocks * LANES), BF16),
-        compiler_params=pltpu.CompilerParams(vmem_limit_bytes=24 * 1024 * 1024),
+        compiler_params=pltpu.CompilerParams(vmem_limit_bytes=10 * 1024 * 1024),
         cost_estimate=cost(5),
         name="attend",
     )(*operands)
@@ -224,7 +224,7 @@
         in_specs=[pl.BlockSpec(memory_space=pltpu.SMEM)] + [vmem] * (len(operands) - 1),
         out_specs=out_specs,
         out_shape=out_shape,
-        compiler_params=pltpu.CompilerParams(vmem_limit_bytes=24 * 1024 * 1024),
+        compiler_params=pltpu.CompilerParams(vmem_limit_bytes=10 * 1024 * 1024),
         cost_estimate=cost(6),
         name="attend_back",
     )(*operands)
@@ -356,7 +356,7 @@
         out_specs=pl.BlockSpec(memory_space=pltpu.VMEM),
         out_shape=jax.ShapeDtypeStruct((total_rows, LANES), BF16),
         scratch_shapes=scratch,
-        compiler_params=pltpu.CompilerParams(vmem_limit_bytes=held + 6 * 1024 * 1024),
+        compiler_params=pltpu.CompilerParams(vmem_limit_bytes=held + (7 if resident else 8) * 1024 * 1024),
         cost_estimate=cost(us),
         name="flat_grads",
     )(side, *arrays)
@@ -469,7 +469,7 @@
         ],
         out_specs=[pl.BlockSpec(memory_space=pltpu.VMEM)] * len(shapes),
         out_shape=shapes,
-        compiler_params=pltpu.CompilerParams(vmem_limit_bytes=4 * 1024 * 1024),
+        compiler_params=pltpu.CompilerParams(vmem_limit_bytes=8 * 1024 * 1024),
         cost_estimate=cost(3),
         name="split",
     )(choice, flat)
@@ -546,7 +546,7 @@
         in_specs=[pl.BlockSpec(memory_space=pltpu.SMEM)] + [vmem] * len(operands),
         out_specs=[vmem] * len(shapes),
         out_shape=shapes,
-        compiler_params=pltpu.CompilerParams(vmem_limit_bytes=4 * 1024 * 1024),
+        compiler_params=pltpu.CompilerParams(vmem_limit_bytes=8 * 1024 * 1024),
         cost_estimate=cost(1),
         name="add_split",
     )(choice, *operands)
@@ -611,7 +611,7 @@
         out_specs=[vmem] * 2,
         out_shape=[half] * 2,
         scratch_shapes=[pltpu.VMEM((rows, LANES), F32) for rows in (*sizes, sizes[0])],
-        compiler_params=pltpu.CompilerParams(vmem_limit_bytes=16 * 1024 * 1024),
+        compiler_params=pltpu.CompilerParams(vmem_limit_bytes=12 * 1024 * 1024),
         cost_estimate=cost(3),
         name="finish",
     )(choice, *operands)
@@ -620,7 +620,7 @@
         in_specs=[smem, vmem, vmem],
         out_specs=[vmem] * 2,
         out_shape=[jax.ShapeDtypeStruct((rows, LANES), F32) for rows in sizes],
-        compiler_params=pltpu.CompilerParams(vmem_limit_bytes=8 * 1024 * 1024),
+        compiler_params=pltpu.CompilerParams(vmem_limit_bytes=12 * 1024 * 1024),
         cost_estimate=cost(2),
         name="join",
     )(choice, near, dp_swap(send, 1))
@@ -673,17 +673,14 @@
 
 
 def co_kernel(
-    lens_ref, x_ref, o_ref, g_ref, wq_ref, wkv_ref, wat_ref,
-    q_ref, kv_ref, pack_ref, n_ref, inv_ref, a_ref, *, pairs, fixed, scaling,
+    lens_ref, x_ref, given_ref, source_ref, g_ref, wmade_ref, wat_ref,
+    made_ref, pack_ref, n_ref, inv_ref, a_ref, *, pairs, fixed, scaling, makes_kv,
 ):
     rows, width = x_ref.shape
     c_ref, h_ref = views(pack_ref, D_C, width)
 
-    def kv_tile(cols):
-        kv_ref[:, cols] = mm(o_ref[...], wkv_ref[:, cols]).astype(BF16)
-
-    def q_tile(cols):
-        q_ref[:, cols] = mm(x_ref[...], wq_ref[:, cols]).astype(BF16)
+    def made_tile(cols):
+        made_ref[:, cols] = mm(source_ref[...], wmade_ref[:, cols]).astype(BF16)
 
     def a_tile(cols):
         a_ref[:, cols] = x_ref[:, cols].astype(F32) + mm(c_ref[...], wat_ref[:, cols])
@@ -694,8 +691,8 @@
         inv_ref[at, :] = jnp.broadcast_to(inverse, (size, LANES))
         h_ref[at, :] = (n * g_ref[0:1, :]).astype(BF16)
 
-    tiles(kv_ref.shape[1], kv_tile)
-    tiles(q_ref.shape[1], q_tile)
+    tiles(made_ref.shape[1], made_tile)
+    q_ref, kv_ref = (given_ref, made_ref) if makes_kv else (made_ref, given_ref)
     blocks = q_ref.shape[1] // LANES
     attend_kernel(
         lens_ref, q_ref, kv_ref, kv_ref, c_ref, pairs=pairs, blocks=blocks,
@@ -836,7 +833,7 @@
     tiles(dc_ref.shape[1], dc_tile)
 
 
-def fused(kernel, operands, outs, scratch, name, us, smem_first=False, limit=14):
+def fused(kernel, operands, outs, scratch, name, us, smem_first=False, limit=11):
     vmem = pl.BlockSpec(memory_space=pltpu.VMEM)
     in_specs = [vmem] * len(operands)
     if smem_first:
@@ -853,24 +850,29 @@
     )(*operands)
 
 
-def co_forward(lens, states, other, gains, query_w, keyval_w, attend_w, pairs, fixed):
+def co_forward(lens, states, given, source, gains, made_w, attend_w, pairs, fixed):
     rows, width = states.shape
-    orows = other.shape[0]
-    return fused(
-        functools.partial(co_kernel, pairs=pairs, fixed=fixed, scaling=(D_C // H_C) ** (-0.5)),
-        (lens, states, other, gains, query_w, keyval_w, attend_w),
+    made, pack1, n1, inv1 = fused(
+        functools.partial(
+            co_kernel,
+            pairs=pairs,
+            fixed=fixed,
+            scaling=(D_C // H_C) ** (-0.5),
+            makes_kv=made_w.shape[1] == 2 * D_C,
+        ),
+        (lens, states, given, source, gains, made_w, attend_w),
         [
-            ((rows, D_C), BF16),
-            ((orows, 2 * D_C), BF16),
+            ((source.shape[0], made_w.shape[1]), BF16),
             ((rows, D_C + width), BF16),
             ((rows, width), F32),
             ((rows, LANES), F32),
         ],
         [((rows, width), F32)],
         "co_forward",
-        9,
+        7,
         True,
     )
+    return made, pack1, n1, inv1
 
 
 def mlp_forward(pack1, n1, gains, up_w, down_w, qkv_w):
@@ -995,11 +997,11 @@
 
 
 def stream_forward(
-    lens, states, other, cot, weights, gains, heads, fixed, other_fixed, pairs, moves, hook
+    lens, states, given, source, cot, weights, gains, heads, fixed, other_fixed, pairs, moves, hook
 ):
-    query_w, other_keyval_w, attend_w, up_w, down_w, qkv_w, output_w = weights
-    q, kv, pack1, n1, inv1 = co_forward(
-        lens, states, other, gains, query_w, other_keyval_w, attend_w, pairs, other_fixed
+    made_w, attend_w, up_w, down_w, qkv_w, output_w = weights
+    made, pack1, n1, inv1 = co_forward(
+        lens, states, given, source, gains, made_w, attend_w, pairs, other_fixed
     )
     pack1 = moves.settle(hook("co", pack1))
     moves.send(pack1=pack1)
@@ -1013,11 +1015,10 @@
     pack4 = moves.settle(hook("mid", pack4))
     moves.send(pack4=pack4)
     da_low, da, dc, dg0 = context_back(pack4, db, n1, inv1, gains, up_w, attend_w)
-    dc, da_low = tied(moves.settle(hook("back", dc)), da_low)
-    moves.send(da=da_low)
+    dc = moves.settle(hook("back", dc))
     width, hidden = up_w.shape
 
-    def sides(dq):
+    def sides(dq, da_low):
         def side(number, start, count):
             pack = (pack1, pack2, pack3, pack4)[number - 1]
             return moves.pair("pack%d" % number, pack, start, count)
@@ -1031,7 +1032,7 @@
             "output": (side(3, 0, width), side(3, width, width)),
         }
 
-    return result, da, dc, q, kv, sides, jnp.concatenate([dg0, dg1, dg2])
+    return result, (da, da_low), dc, made, sides, jnp.concatenate([dg0, dg1, dg2])
 
 
 NAMES = ("query", "keyval", "attend", "up", "down", "qkv", "output")
@@ -1045,7 +1046,7 @@
         for plan, low, high in ((plans[0], 0, room), (plans[1], room, m)):
             if low < high and name in both:
                 start = filled + low * n - (0 if plan is plans[0] else total // 2)
-                step = 1536 if (high - low) > 1536 else high - low
+                step = min(high - low, 1024)
                 for at in range(low, high, step):
                     place = (start + (at - low) * n) // UNIT
                     plan.append(Job(*both[name], at, at + step, place))
@@ -1103,9 +1104,13 @@
 
     choice = choices(stream)
     image_all = both_images(image_states)
-    far_text = stream_swap(text_states)
+    image_q = mm(image_all, image_query).astype(BF16)
+    image_kv = mm(image_all, image_keyval).astype(BF16)
+    far_text, far_lens, image_q, image_kv = tied(
+        stream_swap(text_states), stream_swap(caption_lengths), image_q, image_kv
+    )
     text_all = jnp.concatenate([text_states, far_text])
-    lens = jnp.concatenate([caption_lengths, stream_swap(caption_lengths)])
+    lens = jnp.concatenate([caption_lengths, far_lens])
     image_cotangent, text_cotangent, text_all = tied(image_cotangent, text_cotangent, text_all)
     image_cot = both_images(image_cotangent)
     far_text_cot = stream_swap(text_cotangent)
@@ -1123,12 +1128,13 @@
             value, cots[0] = tied(value, cots[0])
         return value
 
-    image_out, image_da, image_dc, image_q, text_kv, image_sides, image_dg = stream_forward(
+    image_out, (image_da, image_da_low), image_dc, text_kv, image_sides, image_dg = stream_forward(
         lens,
         image_all,
+        image_q,
         text_all,
         image_cot,
-        (image_query, text_keyval, image_attend, image_up, image_down, image_qkv, image_output),
+        (text_keyval, image_attend, image_up, image_down, image_qkv, image_output),
         image_gains,
         H_I,
         regions,
@@ -1138,10 +1144,10 @@
         image_hook,
     )
     image_dq, text_dkv = attend_back(
-        lens, image_q, text_kv, text_kv, image_dc, co_cols, pairs, co_blocks, 1, None, co_scale, False
-    )
-    image_moves.send(dq=image_dq)
-    image_sides = image_sides(image_dq)
+        lens, image_q, text_kv, text_kv, image_dc, co_cols, pairs, co_blocks, 1, None, co_scale, False,
+    )
+    image_moves.send(dq=image_dq, da=image_da_low)
+    image_sides = image_sides(image_dq, image_da_low)
     text_moves.send(states=text_all, dkv=text_dkv)
 
     def sizes_of(*weights):
@@ -1184,18 +1190,15 @@
             pieces[:] = add_split(choice, ((2, pieces[0::2]), (1, pieces[1::2])))
             for piece in pieces:
                 piece.send()
-        if name == "back":
-            (value,) = paced(pieces, (), (value,))
-            pieces[:] = add_split(choice, ((3, pieces),))
-            pieces[0].send()
         return value
 
-    text_out, text_da, text_dc, text_q, image_kv, text_sides, text_dg = stream_forward(
+    text_out, (text_da, text_da_low), text_dc, text_q, text_sides, text_dg = stream_forward(
         lens,
         text_all,
-        image_all,
+        image_kv,
+        text_all,
         jnp.concatenate([text_cotangent, cots[0]]),
-        (text_query, image_keyval, text_attend, text_up, text_down, text_qkv, text_output),
+        (text_query, text_attend, text_up, text_down, text_qkv, text_output),
         text_gains,
         H_T,
         None,
@@ -1210,9 +1213,13 @@
         lens, text_q, image_kv, image_kv, text_dc, co_cols, pairs, co_blocks, 1, regions, co_scale, False
     )
 
+    if early:
+        image_dkv, text_dq, text_da_low = paced(pieces, (), (image_dkv, text_dq, text_da_low))
+        pieces[:] = add_split(choice, ((3, pieces[:1]), (3, pieces[1:])))
+        pieces[0].send()
     image_moves.send(dkv=image_dkv)
-    text_moves.send(dq=text_dq)
-    text_sides = text_sides(text_dq)
+    text_moves.send(dq=text_dq, da=text_da_low)
+    text_sides = text_sides(text_dq, text_da_low)
     text_sides["keyval"] = (text_moves.pair("states", text_all), text_moves.pair("dkv", text_dkv))
 
     def all_input_grads(text_dq, image_dq):
@@ -1244,18 +1251,19 @@
         text_sides["query"] = (text_sides["query"][0], (near_dq, *rest))
         late.send()
         text_flat = gather_half(text_sides, text_sizes)
-        text_flat = after(text_flat, pieces + [late])
+        text_flat = after(text_flat, [late, pieces[0]])
         text_pieces = piece_set(choice, text_flat, (1, 1, 1, 1), TEXT_SHARES)
         one, two, three, four = text_pieces
         late.turn()
-        one.out, late.out, text_dq, image_dq, gains = tied(
-            one.out, late.out, text_dq, image_dq, gains
+        one.out, late.out, pieces[1].out, text_dq, image_dq, gains = tied(
+            one.out, late.out, pieces[1].out, text_dq, image_dq, gains
         )
         one.send()
         late.send()
+        pieces[1].send()
         gains = gain_step(gains, bits.pop())
         grads = all_input_grads(text_dq, image_dq)
-        *grads, gains = paced((one, late), (two,), (*grads, gains))
+        *grads, gains = paced((one, late, pieces[1]), (two,), (*grads, gains))
         (one,) = add_split(choice, ((2, (one,)),))
         late.add(gather=True)
         two.send()
@@ -1292,7 +1300,7 @@
         image_share, text_share = finished(
             choice,
             (pieces, (one, two, three, four)),
-            (((0, 2 * unit, unit, 3 * unit),), tuple(starts)),
+            (((0, 2 * unit), (unit, 3 * unit)), tuple(starts)),
             (late.keep[0], late.far[0]),
         )
     else:

time: 310 us -> 275 us (0.89)
  waiting for transfers between devices: 72.7 us -> 60.5 us
  Pallas kernels: 141 us -> 129 us
  local copies, waits for them, and re-layouts: 28.6 us -> 18.1 us
  matrix products: 2.55 us -> 6.66 us
    pallas_call x10, Pallas kernels: 83.9 us -> 70.6 us  [fused(): pl.pallas_call(kernel, in_specs=in_specs, out_specs=[vmem] * len(outs), o...]
    unnamed x194 -> x182, local copies, waits for them, and re-layouts: 27.3 us -> 16.8 us
    ppermute x5, waiting for transfers between devices: 10.4 us -> 2.99 us  [stream_swap(): return lax.ppermute(block, 'stream', [(0, 1), (1, 0)])]
    ppermute x42 -> x43, waiting for transfers between devices: 62.3 us -> 57.6 us  [dp_swap(): return lax.ppermute(block, 'dp', [(i, i ^ bit) for i in range(count)])]
    dot_general x4 -> x6, matrix products: 2.55 us -> 6.66 us  [mm(): return jnp.dot(a, b, preferred_element_type=F32)]
    ppermute x42 -> x43, starting transfers between devices: 48.5 us -> 47.5 us  [dp_swap(): return lax.ppermute(block, 'dp', [(i, i ^ bit) for i in range(count)])]
  transfers between devices with their start and end apart: 49 -> 50, of which waited for: 17 -> 19; matrix products, arithmetic and copies ran while one was open for 2% -> 3% of each run, Pallas kernels for 40% -> 42%
where the time goes in v1:
time: 275 us; the launch traced here: 272 us
  Pallas kernels  129 us (47%)
  waiting for transfers between devices  60.5 us (22%)
  starting transfers between devices  54.6 us (20%)
  local copies, waits for them, and re-layouts  18.1 us (7%)
  matrix products  6.66 us (2%)
    pallas_call x10, Pallas kernels, fused(): pl.pallas_call(kernel, in_specs=in_specs, out_specs=[vmem] * len(outs), o...  70.6 us
    ppermute x43, waiting for transfers between devices, dp_swap(): return lax.ppermute(block, 'dp', [(i, i ^ bit) for i in range(count)])  57.6 us
    ppermute x43, starting transfers between devices, dp_swap(): return lax.ppermute(block, 'dp', [(i, i ^ bit) for i in range(count)])  47.5 us
    pallas_call x3, Pallas kernels, flat_grads(): pl.pallas_call(functools.partial(flat_kernel, plans=plans, found=found, q...  25.9 us
    unnamed x182, local copies, waits for them, and re-layouts  16.8 us
    pallas_call x2, Pallas kernels, attend_back(): pl.pallas_call(functools.partial(body, pairs=pairs, blocks=blocks, cols=c...  11.7 us
    pallas_call x11, Pallas kernels, add_split(): pl.pallas_call(functools.partial(add_split_kernel, plan=tuple(plan), inpu...  7.99 us
    pallas_call x2, Pallas kernels, input_grads(): pl.pallas_call(functools.partial(input_kernel, first=first), in_specs=[vm...  6.77 us
  transfers between devices with their start and end apart: 50, of which 19 were waited for; matrix products, arithmetic and copies ran while one was open for 3% of the time, Pallas kernels for 42%

profile of v1, /device:TPU:3, one launch (start us, length us, event | category | flops | bytes accessed | tf_op | source)
XLA Modules:
  0.0 272.2 jit_solution(8085554877832453899)
XLA Ops:
  0.7 1.5 collective-permute-start
  3.7 1.9 collective-permute-done.2
  6.0 2.8 %collective-permute-start.3 = (bf16[192,1024]{1,0:T(8,128)(2,1)S(1)}, bf16[192,1024]{1,0:T(8,128)(2,1)S(1)}, u32[]{:S(2)}, u32[]{:S(2)}) collective-permute-start(bf16[192,1024]{1,0:T(8,128)(2,1)S(1)} %fusion.x_ref.refs_0_), channel_id=1, source_target_pairs={{0,1},{1,0},{2,3},{3,2},{4,5},{5,4},{6,7},{7,6},{8,9},{9,8},{10,11... | collective-permute-start | bytes 1179656 | tf_op jit(solution)/shard_map/ppermute | solution.py:367
  8.8 2.2 convolution_convert_fusion.1.given_ref.refs_0_
  11.1 1.9 convolution_convert_fusion.given_ref.refs_1_
  14.6 7.8 %co_forward.3 = (bf16[512,2048]{1,0:T(8,128)(2,1)S(1)}, bf16[192,2048]{1,0:T(8,128)(2,1)S(1)}, f32[192,1024]{1,0:T(8,128)S(1)}, f32[192,128]{1,0:T(8,128)S(1)}) custom-call(s32[4]{0:T(128)S(1)} %pad_add_fusion.1.lens_ref, bf16[192,1024]{1,0:T(8,128)(2,1)S(1)} %fusion.x_ref.refs_0_, bf16[192,1024]{1,0:T(8,128)(2,1)S(1)} %convolution_convert_fusion.1.given_ref.refs_0_, ...), custom_call_target="tpu_custom_call" | custom-call | flops 7000000000 | bytes 1000 | tf_op jit(solution)/shard_map/co_forward/pallas_call | solution.py:841
  23.3 1.6 collective-permute-start.4
  25.3 1.5 collective-permute-start.6
  27.4 3.7 %mlp_forward.2 = (bf16[192,2048]{1,0:T(8,128)(2,1)S(1)}, bf16[192,1024]{1,0:T(8,128)(2,1)S(1)}, f32[192,1024]{1,0:T(8,128)S(1)}, f32[192,128]{1,0:T(8,128)S(1)}, bf16[192,3072]{1,0:T(8,128)(2,1)S(1)}) custom-call(bf16[192,2048]{1,0:T(8,128)(2,1)S(1)} %get-tuple-element.204.pack1_ref.refs_4_, f32[192,1024]{1,0:T(8,128)S(1)} %get-tuple-element.205.n1_ref, ...), custom_call_target="tpu_custom_call" | custom-call | flops 4800000000 | bytes 1000 | tf_op jit(solution)/shard_map/mlp_forward/pallas_call | solution.py:841
  31.5 10.5 %self_turn.2 = (bf16[192,5120]{1,0:T(8,128)(2,1)S(1)}, bf16[192,1024]{1,0:T(8,128)(2,1)S(1)}, f32[192,1024]{1,0:T(8,128)S(1)}, f32[1,1024]{1,0:T(1,128)S(1)}) custom-call(s32[4]{0:T(128)S(1)} %pad_add_fusion.1.lens_ref, bf16[192,3072]{1,0:T(8,128)(2,1)S(1)} %get-tuple-element.209.r_ref, f32[192,1024]{1,0:T(8,128)S(1)} %get-tuple-element.210.n2_ref, ...), custom_call_target="tpu_custom_call" | custom-call | flops 10499999744 | bytes 1000 | tf_op jit(solution)/shard_map/self_turn/pallas_call | solution.py:841
  43.3 3.6 %mlp_back.2 = (bf16[192,2048]{1,0:T(8,128)(2,1)S(1)}, f32[192,1024]{1,0:T(8,128)S(1)}, f32[1,1024]{1,0:T(1,128)S(1)}) custom-call(bf16[192,5120]{1,0:T(8,128)(2,1)S(1)} %get-tuple-element.216.pack3_ref.refs_12_, f32[192,1024]{1,0:T(8,128)S(1)} %get-tuple-element.217.de_ref, f32[192,1024]{1,0:T(8,128)S(1)} %get-tuple-element.210.n2_ref, ...), custom_call_target="tpu_custom_call" | custom-call | flops 2742857216 | bytes 1000 | tf_op jit(solution)/shard_map/mlp_back/pallas_call | solution.py:841
  47.3 2.2 context_back.2
  50.3 6.6 %attend_back.2 = (bf16[192,1024]{1,0:T(8,128)(2,1)S(1)}, bf16[512,2048]{1,0:T(8,128)(2,1)}) custom-call(s32[4]{0:T(128)S(1)} %pad_add_fusion.1.lens_ref, bf16[192,1024]{1,0:T(8,128)(2,1)S(1)} %convolution_convert_fusion.1.given_ref.refs_0_, bf16[512,2048]{1,0:T(8,128)(2,1)S(1)} %get-tuple-element.203.refs_1_, bf16[192,1024]{1,0:T(8,128)(2,1)S(1)} %get-tuple-element.225.refs_2_), custom_call_target="tpu_custom_call" | custom-call | flops 6000000000 | bytes 1000 | tf_op jit(solution)/shard_map/attend_back/pallas_call | solution.py:213
  58.8 1.5 copy-done.7
  62.6 1.4 copy-done.36
  65.5 7.4 %co_forward.2 = (bf16[512,1024]{1,0:T(8,128)(2,1)S(1)}, bf16[512,1792]{1,0:T(8,128)(2,1)S(1)}, f32[512,768]{1,0:T(8,128)S(1)}, f32[512,128]{1,0:T(8,128)S(1)}) custom-call(s32[4]{0:T(128)S(1)} %copy-done.61, bf16[512,768]{1,0:T(8,128)(2,1)S(1)} %copy-done.12, bf16[192,2048]{1,0:T(8,128)(2,1)S(1)} %copy-done.14, bf16[512,768]{1,0:T(8,128)(2,1)S(1)} %copy-done.12, ...), custom_call_target="tpu_custom_call" | custom-call | flops 7000000000 | bytes 1000 | tf_op jit(solution)/shard_map/co_forward/pallas_call | solution.py:841
  73.0 6.3 %flat_grads.3.flat_ref = bf16[20480,128]{1,0:T(8,128)(2,1)S(1)} custom-call(s32[2]{0:T(128)S(1)} %pad_add_fusion.side_ref, bf16[192,1024]{1,0:T(8,128)(2,1)S(1)} %fusion.x_ref.refs_0_, bf16[192,1024]{1,0:T(8,128)(2,1)S(1)} %copy-done.54, bf16[192,1024]{1,0:T(8,128)(2,1)S(1)} %copy-done.19, bf16[192,1024]{1,0:T(8,128)(2,1)S(1)} %collective-permute-done.10.refs_3_, ...), custom_call_target="tpu_custom_call" | custom-call | flops 6000000000 | bytes 1000 | tf_op jit(solution)/shard_map/flat_grads/pallas_call | solution.py:350
  83.2 10.6 %mlp_forward.3 = (bf16[512,3840]{1,0:T(8,128)(2,1)S(1)}, bf16[512,3072]{1,0:T(8,128)(2,1)S(1)}, f32[512,768]{1,0:T(8,128)S(1)}, f32[512,128]{1,0:T(8,128)S(1)}, bf16[512,2304]{1,0:T(8,128)(2,1)S(1)}) custom-call(bf16[512,1792]{1,0:T(8,128)(2,1)S(1)} %get-tuple-element.246.pack1_ref.refs_6_, f32[512,768]{1,0:T(8,128)S(1)} %get-tuple-element.247.n1_ref, ...), custom_call_target="tpu_custom_call" | custom-call | flops 12800000000 | bytes 1000 | tf_op jit(solution)/shard_map/mlp_forward/pallas_call | solution.py:841
  93.9 2.9 %collective-permute-done.14.refs_1_ = bf16[4,640,128]{2,1,0:T(8,128)(2,1)S(1)} collective-permute-done((bf16[4,640,128]{2,1,0:T(8,128)(2,1)S(1)}, bf16[4,640,128]{2,1,0:T(8,128)(2,1)S(1)}, u32[]{:S(2)}, u32[]{:S(2)}) %collective-permute-start.14) | collective-permute-done | bytes 655392 | tf_op jit(solution)/shard_map/ppermute | solution.py:367
  100.6 12.5 %self_turn.3 = (bf16[512,3840]{1,0:T(8,128)(2,1)S(1)}, bf16[512,768]{1,0:T(8,128)(2,1)S(1)}, f32[512,768]{1,0:T(8,128)S(1)}, f32[1,768]{1,0:T(1,128)S(1)}) custom-call(s32[4]{0:T(128)S(1)} %copy-done.61, bf16[512,2304]{1,0:T(8,128)(2,1)S(1)} %get-tuple-element.256.r_ref, f32[512,768]{1,0:T(8,128)S(1)} %get-tuple-element.257.n2_ref, f32[3,768]{1,0:T(4,128)S(1)} %copy-done.59, ...), custom_call_target="tpu_custom_call" | custom-call | flops 12999999488 | bytes 1000 | tf_op jit(solution)/shard_map/self_turn/pallas_call | solution.py:841
  113.2 2.3 collective-permute-done.16.refs_3_
  116.5 6.0 %mlp_back.3 = (bf16[512,3840]{1,0:T(8,128)(2,1)S(1)}, f32[512,768]{1,0:T(8,128)S(1)}, f32[1,768]{1,0:T(1,128)S(1)}) custom-call(bf16[512,3840]{1,0:T(8,128)(2,1)S(1)} %get-tuple-element.270.pack3_ref.refs_14_, f32[512,768]{1,0:T(8,128)S(1)} %get-tuple-element.271.de_ref, f32[512,768]{1,0:T(8,128)S(1)} %get-tuple-element.257.n2_ref, ...), custom_call_target="tpu_custom_call" | custom-call | flops 7314285568 | bytes 1000 | tf_op jit(solution)/shard_map/mlp_back/pallas_call | solution.py:841
  122.9 2.1 copy-done.83
  129.3 6.3 %context_back.3 = (bf16[512,768]{1,0:T(8,128)(2,1)S(1)}, f32[512,768]{1,0:T(8,128)S(1)}, bf16[512,1024]{1,0:T(8,128)(2,1)S(1)}, f32[1,768]{1,0:T(1,128)S(1)}) custom-call(bf16[512,3840]{1,0:T(8,128)(2,1)S(1)} %get-tuple-element.275.pack4_ref.refs_10_, f32[512,768]{1,0:T(8,128)S(1)} %get-tuple-element.276.db_ref, f32[512,768]{1,0:T(8,128)S(1)} %get-tuple-element.247.n1_ref, ...), custom_call_target="tpu_custom_call" | custom-call | flops 6400000000 | bytes 1000 | tf_op jit(solution)/shard_map/context_back/pallas_call | solution.py:841
  135.6 5.1 %attend_back.3 = (bf16[512,1024]{1,0:T(8,128)(2,1)S(1)}, bf16[192,2048]{1,0:T(8,128)(2,1)S(1)}) custom-call(s32[4]{0:T(128)S(1)} %copy-done.61, bf16[512,1024]{1,0:T(8,128)(2,1)S(1)} %get-tuple-element.267.refs_0_, bf16[192,2048]{1,0:T(8,128)(2,1)S(1)} %copy-done.15, bf16[512,1024]{1,0:T(8,128)(2,1)S(1)} %get-tuple-element.279.refs_2_), custom_call_target="tpu_custom_call" | custom-call | flops 6000000000 | bytes 1000 | tf_op jit(solution)/shard_map/attend_back/pallas_call | solution.py:213
  140.7 2.4 collective-permute-done.19.refs_1_
  146.6 2.4 collective-permute-start.28
  149.0 1.7 flat_grads.4.flat_ref
  154.8 17.9 %flat_grads.5.flat_ref = bf16[19968,128]{1,0:T(8,128)(2,1)} custom-call(s32[2]{0:T(128)S(1)} %pad_add_fusion.side_ref, bf16[512,768]{1,0:T(8,128)(2,1)S(1)} %copy-done.13, bf16[512,768]{1,0:T(8,128)(2,1)S(1)} %copy-done.40, bf16[512,1024]{1,0:T(8,128)(2,1)S(1)} %get-tuple-element.316.refs_2_.dq_ref, bf16[512,1024]{1,0:T(8,128)(2,1)S(1)} %collective-permute-done.25.refs_3_, ...), custom_call_target="tpu_custom_call" | custom-call | flops 14000000000 | bytes 1000 | tf_op jit(solution)/shard_map/flat_grads/pallas_call | solution.py:350
  172.7 2.4 copy-done.62
  179.0 2.0 collective-permute-start.32
  181.0 2.9 %input_grads.3 = (bf16[72,1024]{1,0:T(8,128)(2,1)}, bf16[72,1024]{1,0:T(8,128)(2,1)}) custom-call(f32[192,1024]{1,0:T(8,128)S(1)} %copy-done.10, bf16[192,1024]{1,0:T(8,128)(2,1)S(1)} %copy-done.19, bf16[192,2048]{1,0:T(8,128)(2,1)S(1)} %get-tuple-element.284.refs_2_.dkv_ref, bf16[192,1024]{1,0:T(8,128)(2,1)S(1)} %copy-done.17, ...), custom_call_target="tpu_custom_call" | custom-call | flops 200000000 | bytes 1000 | tf_op jit(solution)/shard_map/input_grads/pallas_call | solution.py:933
  184.0 3.9 %input_grads.2 = (bf16[256,768]{1,0:T(8,128)(2,1)}, bf16[256,768]{1,0:T(8,128)(2,1)}) custom-call(f32[512,768]{1,0:T(8,128)S(1)} %get-tuple-element.315.da_ref, bf16[512,1024]{1,0:T(8,128)(2,1)S(1)} %get-tuple-element.316.refs_2_.dq_ref, bf16[512,2048]{1,0:T(8,128)(2,1)} %get-tuple-element.239.refs_4_.dkv_ref, ...), custom_call_target="tpu_custom_call" | custom-call | flops 200000000 | bytes 1000 | tf_op jit(solution)/shard_map/input_grads/pallas_call | solution.py:933
  187.8 8.2 %collective-permute-done.32 = f32[3,1792]{1,0:T(4,128)S(1)} collective-permute-done((f32[3,1792]{1,0:T(4,128)S(1)}, f32[3,1792]{1,0:T(4,128)S(1)}, u32[]{:S(2)}, u32[]{:S(2)}) %collective-permute-start.32) | collective-permute-done | bytes 21536 | tf_op jit(solution)/shard_map/ppermute | solution.py:367
  198.1 2.3 collective-permute-start.35
  200.8 10.7 %collective-permute-done.36 = f32[3,1792]{1,0:T(4,128)S(1)} collective-permute-done((f32[3,1792]{1,0:T(4,128)S(1)}, f32[3,1792]{1,0:T(4,128)S(1)}, u32[]{:S(2)}, u32[]{:S(2)}) %collective-permute-start.36) | collective-permute-done | bytes 21536 | tf_op jit(solution)/shard_map/ppermute | solution.py:367
  211.5 2.0 collective-permute-done.34.refs_1_
  215.5 1.6 collective-permute-start.39
  219.4 9.3 %collective-permute-done.41 = f32[3,1792]{1,0:T(4,128)S(1)} collective-permute-done((f32[3,1792]{1,0:T(4,128)S(1)}, f32[3,1792]{1,0:T(4,128)S(1)}, u32[]{:S(2)}, u32[]{:S(2)}) %collective-permute-start.41) | collective-permute-done | bytes 21536 | tf_op jit(solution)/shard_map/ppermute | solution.py:367
  228.8 2.0 collective-permute-start.44
  232.6 5.3 %collective-permute-start.45 = (f32[3,1792]{1,0:T(4,128)S(1)}, f32[3,1792]{1,0:T(4,128)S(1)}, u32[]{:S(2)}, u32[]{:S(2)}) collective-permute-start(f32[3,1792]{1,0:T(4,128)S(1)} %add.64), channel_id=1, source_target_pairs={{0,1},{1,0},{2,3},{3,2},{4,5},{5,4},{6,7},{7,6},{8,9},{9,8},{10,11... | collective-permute-start | bytes 64520 | tf_op jit(solution)/shard_map/ppermute | solution.py:367
  241.5 1.4 collective-permute-start.46
  242.9 6.2 %collective-permute-done.46.refs_9_ = bf16[1,608,128]{2,1,0:T(8,128)(2,1)S(1)} collective-permute-done((bf16[1,608,128]{2,1,0:T(8,128)(2,1)S(1)}, bf16[1,608,128]{2,1,0:T(8,128)(2,1)S(1)}, u32[]{:S(2)}, u32[]{:S(2)}) %collective-permute-start.46) | collective-permute-done | bytes 155680 | tf_op jit(solution)/shard_map/ppermute | solution.py:367
  250.5 7.5 %collective-permute-done.48.refs_11_ = bf16[1,384,128]{2,1,0:T(8,128)(2,1)S(1)} collective-permute-done((bf16[1,384,128]{2,1,0:T(8,128)(2,1)S(1)}, bf16[1,384,128]{2,1,0:T(8,128)(2,1)S(1)}, u32[]{:S(2)}, u32[]{:S(2)}) %collective-permute-start.48) | collective-permute-done | bytes 98336 | tf_op jit(solution)/shard_map/ppermute | solution.py:367
  258.1 1.8 finish.1
  259.9 7.2 %collective-permute-start.49 = (f32[2528,128]{1,0:T(8,128)S(1)}, f32[2528,128]{1,0:T(8,128)S(1)}, u32[]{:S(2)}, u32[]{:S(2)}) collective-permute-start(f32[2528,128]{1,0:T(8,128)S(1)} %get-tuple-element.378), channel_id=1, source_target_pairs={{0,1},{1,0},{2,3},{3,2},{4,5},{5,4},{6,7},{7,6},{8,9},{9,8},{10,11... | collective-permute-start | bytes 3883016 | tf_op jit(solution)/shard_map/ppermute | solution.py:367
  268.3 1.4 collective-permute-done.49.far_ref
  269.8 2.2 join.1
  (297 shorter events, 53.1 us)
Async XLA Ops:
  0.6 5.0 %collective-permute-start.2 = (bf16[72,1024]{1,0:T(8,128)(2,1)}, bf16[72,1024]{1,0:T(8,128)(2,1)S(1)}, u32[]{:S(2)}, u32[]{:S(2)}) collective-permute-start(bf16[72,1024]{1,0:T(8,128)(2,1)} %param.22), channel_id=1, source_target_pairs={{0,16},{16,0},{1,17},{17,1},{2,18},{18,2},{3,19},{19,3},{4,20},{20... | collective-permute-start | bytes 442376 | tf_op jit(solution)/shard_map/ppermute | solution.py:371
  0.7 13.3 %collective-permute-start = (bf16[256,768]{1,0:T(8,128)(2,1)}, bf16[256,768]{1,0:T(8,128)(2,1)S(1)}, u32[]{:S(2)}, u32[]{:S(2)}) collective-permute-start(bf16[256,768]{1,0:T(8,128)(2,1)} %param.21), channel_id=1, source_target_pairs={{0,16},{16,0},{1,17},{17,1},{2,18},{18,2},{3,19},{19,3},{4,20},{20... | collective-permute-start | bytes 1179656 | tf_op jit(solution)/shard_map/ppermute | solution.py:371
  2.2 11.9 %collective-permute-start.1 = (s32[2]{0:T(128)}, s32[2]{0:T(128)S(1)}, u32[]{:S(2)}, u32[]{:S(2)}) collective-permute-start(s32[2]{0:T(128)} %param.23), channel_id=1, source_target_pairs={{0,16},{16,0},{1,17},{17,1},{2,18},{18,2},{3,19},{19,3},{4,20},{20... | collective-permute-start | bytes 32 | tf_op jit(solution)/shard_map/ppermute | solution.py:371
  6.0 16.5 %collective-permute-start.3 = (bf16[192,1024]{1,0:T(8,128)(2,1)S(1)}, bf16[192,1024]{1,0:T(8,128)(2,1)S(1)}, u32[]{:S(2)}, u32[]{:S(2)}) collective-permute-start(bf16[192,1024]{1,0:T(8,128)(2,1)S(1)} %fusion.x_ref.refs_0_), channel_id=1, source_target_pairs={{0,1},{1,0},{2,3},{3,2},{4,5},{5,4},{6,7},{7,6},{8,9},{9,8},{10,11... | collective-permute-start | bytes 1179656 | tf_op jit(solution)/shard_map/ppermute | solution.py:367
  14.2 12.6 %collective-permute-start.5 = (bf16[72,1024]{1,0:T(8,128)(2,1)S(1)}, bf16[72,1024]{1,0:T(8,128)(2,1)S(1)}, u32[]{:S(2)}, u32[]{:S(2)}) collective-permute-start(bf16[72,1024]{1,0:T(8,128)(2,1)S(1)} %copy-done.68), channel_id=1, source_target_pairs={{0,16},{16,0},{1,17},{17,1},{2,18},{18,2},{3,19},{19,3},{4,20},{20... | collective-permute-start | bytes 442376 | tf_op jit(solution)/shard_map/ppermute | solution.py:371
  23.3 7.8 %collective-permute-start.4 = (bf16[192,2048]{1,0:T(8,128)(2,1)S(1)}, bf16[192,2048]{1,0:T(8,128)(2,1)S(1)}, u32[]{:S(2)}, u32[]{:S(2)}) collective-permute-start(bf16[192,2048]{1,0:T(8,128)(2,1)S(1)} %get-tuple-element.204.pack1_ref.refs_4_), channel_id=1, source_target_pairs={{0,1},{1,0},{2,3},{3,2},{4,5},{5,4},{6,7},{7,6},{8,9},{9,8},{10,11... | collective-permute-start | bytes 2359304 | tf_op jit(solution)/shard_map/ppermute | solution.py:367
  25.3 16.8 %collective-permute-start.6 = (bf16[256,768]{1,0:T(8,128)(2,1)S(1)}, bf16[256,768]{1,0:T(8,128)(2,1)S(1)}, u32[]{:S(2)}, u32[]{:S(2)}) collective-permute-start(bf16[256,768]{1,0:T(8,128)(2,1)S(1)} %copy-done.64), channel_id=1, source_target_pairs={{0,16},{16,0},{1,17},{17,1},{2,18},{18,2},{3,19},{19,3},{4,20},{20... | collective-permute-start | bytes 1179656 | tf_op jit(solution)/shard_map/ppermute | solution.py:371
  31.1 11.0 %collective-permute-start.7 = (bf16[192,2048]{1,0:T(8,128)(2,1)S(1)}, bf16[192,2048]{1,0:T(8,128)(2,1)S(1)}, u32[]{:S(2)}, u32[]{:S(2)}) collective-permute-start(bf16[192,2048]{1,0:T(8,128)(2,1)S(1)} %get-tuple-element.215.refs_10_), channel_id=1, source_target_pairs={{0,1},{1,0},{2,3},{3,2},{4,5},{5,4},{6,7},{7,6},{8,9},{9,8},{10,11... | collective-permute-start | bytes 2359304 | tf_op jit(solution)/shard_map/ppermute | solution.py:367
  57.6 22.6 %collective-permute-start.13 = (bf16[512,2048]{1,0:T(8,128)(2,1)}, bf16[512,2048]{1,0:T(8,128)(2,1)}, u32[]{:S(2)}, u32[]{:S(2)}) collective-permute-start(bf16[512,2048]{1,0:T(8,128)(2,1)} %get-tuple-element.239.refs_4_.dkv_ref), channel_id=1, source_target_pairs={{0,1},{1,0},{2,3},{3,2},{4,5},{5,4},{6,7},{7,6},{8,9},{9,8},{10,11... | collective-permute-start | bytes 6291464 | tf_op jit(solution)/shard_map/ppermute | solution.py:367
  58.1 22.1 %collective-permute-start.12 = (bf16[512,768]{1,0:T(8,128)(2,1)}, bf16[512,768]{1,0:T(8,128)(2,1)S(1)}, u32[]{:S(2)}, u32[]{:S(2)}) collective-permute-start(bf16[512,768]{1,0:T(8,128)(2,1)} %copy-done.11), channel_id=1, source_target_pairs={{0,1},{1,0},{2,3},{3,2},{4,5},{5,4},{6,7},{7,6},{8,9},{9,8},{10,11... | collective-permute-start | bytes 2359304 | tf_op jit(solution)/shard_map/ppermute | solution.py:367
  58.3 14.6 %collective-permute-start.11 = (bf16[192,1024]{1,0:T(8,128)(2,1)}, bf16[192,1024]{1,0:T(8,128)(2,1)S(1)}, u32[]{:S(2)}, u32[]{:S(2)}) collective-permute-start(bf16[192,1024]{1,0:T(8,128)(2,1)} %copy-done.56), channel_id=1, source_target_pairs={{0,1},{1,0},{2,3},{3,2},{4,5},{5,4},{6,7},{7,6},{8,9},{9,8},{10,11... | collective-permute-start | bytes 1179656 | tf_op jit(solution)/shard_map/ppermute | solution.py:367
  58.6 14.3 %collective-permute-start.10 = (bf16[192,1024]{1,0:T(8,128)(2,1)}, bf16[192,1024]{1,0:T(8,128)(2,1)S(1)}, u32[]{:S(2)}, u32[]{:S(2)}) collective-permute-start(bf16[192,1024]{1,0:T(8,128)(2,1)} %copy-done.18), channel_id=1, source_target_pairs={{0,1},{1,0},{2,3},{3,2},{4,5},{5,4},{6,7},{7,6},{8,9},{9,8},{10,11... | collective-permute-start | bytes 1179656 | tf_op jit(solution)/shard_map/ppermute | solution.py:367
  80.2 17.5 %collective-permute-start.18 = (bf16[512,1792]{1,0:T(8,128)(2,1)S(1)}, bf16[512,1792]{1,0:T(8,128)(2,1)S(1)}, u32[]{:S(2)}, u32[]{:S(2)}) collective-permute-start(bf16[512,1792]{1,0:T(8,128)(2,1)S(1)} %get-tuple-element.246.pack1_ref.refs_6_), channel_id=1, source_target_pairs={{0,1},{1,0},{2,3},{3,2},{4,5},{5,4},{6,7},{7,6},{8,9},{9,8},{10,11... | collective-permute-start | bytes 5505032 | tf_op jit(solution)/shard_map/ppermute | solution.py:367
  80.6 16.2 %collective-permute-start.14 = (bf16[4,640,128]{2,1,0:T(8,128)(2,1)S(1)}, bf16[4,640,128]{2,1,0:T(8,128)(2,1)S(1)}, u32[]{:S(2)}, u32[]{:S(2)}) collective-permute-start(bf16[4,640,128]{2,1,0:T(8,128)(2,1)S(1)} %get-tuple-element.242), channel_id=1, source_target_pairs={{0,2},{1,3},{2,0},{3,1},{4,6},{5,7},{6,4},{7,5},{8,10},{9,11},{10,... | collective-permute-start | bytes 1966088 | tf_op jit(solution)/shard_map/ppermute | solution.py:367
  81.8 15.9 %collective-permute-start.15 = (bf16[4,640,128]{2,1,0:T(8,128)(2,1)S(1)}, bf16[4,640,128]{2,1,0:T(8,128)(2,1)S(1)}, u32[]{:S(2)}, u32[]{:S(2)}) collective-permute-start(bf16[4,640,128]{2,1,0:T(8,128)(2,1)S(1)} %get-tuple-element.243), channel_id=1, source_target_pairs={{0,4},{1,5},{2,6},{3,7},{4,0},{5,1},{6,2},{7,3},{8,12},{9,13},{10,... | collective-permute-start | bytes 1966088 | tf_op jit(solution)/shard_map/ppermute | solution.py:367
  97.7 17.8 %collective-permute-start.21 = (bf16[512,3840]{1,0:T(8,128)(2,1)S(1)}, bf16[512,3840]{1,0:T(8,128)(2,1)}, u32[]{:S(2)}, u32[]{:S(2)}) collective-permute-start(bf16[512,3840]{1,0:T(8,128)(2,1)S(1)} %get-tuple-element.269.refs_12_), channel_id=1, source_target_pairs={{0,1},{1,0},{2,3},{3,2},{4,5},{5,4},{6,7},{7,6},{8,9},{9,8},{10,11... | collective-permute-start | bytes 11796488 | tf_op jit(solution)/shard_map/ppermute | solution.py:367
  99.1 16.4 %collective-permute-start.16 = (bf16[4,640,128]{2,1,0:T(8,128)(2,1)S(1)}, bf16[4,640,128]{2,1,0:T(8,128)(2,1)S(1)}, u32[]{:S(2)}, u32[]{:S(2)}) collective-permute-start(bf16[4,640,128]{2,1,0:T(8,128)(2,1)S(1)} %get-tuple-element.251), channel_id=1, source_target_pairs={{0,2},{1,3},{2,0},{3,1},{4,6},{5,7},{6,4},{7,5},{8,10},{9,11},{10,... | collective-permute-start | bytes 1966088 | tf_op jit(solution)/shard_map/ppermute | solution.py:367
  99.4 16.1 %collective-permute-start.17 = (bf16[4,640,128]{2,1,0:T(8,128)(2,1)S(1)}, bf16[4,640,128]{2,1,0:T(8,128)(2,1)S(1)}, u32[]{:S(2)}, u32[]{:S(2)}) collective-permute-start(bf16[4,640,128]{2,1,0:T(8,128)(2,1)S(1)} %get-tuple-element.252), channel_id=1, source_target_pairs={{0,4},{1,5},{2,6},{3,7},{4,0},{5,1},{6,2},{7,3},{8,12},{9,13},{10,... | collective-permute-start | bytes 1966088 | tf_op jit(solution)/shard_map/ppermute | solution.py:367
  115.5 7.5 %collective-permute-start.22 = (bf16[512,3840]{1,0:T(8,128)(2,1)S(1)}, bf16[512,3840]{1,0:T(8,128)(2,1)S(1)}, u32[]{:S(2)}, u32[]{:S(2)}) collective-permute-start(bf16[512,3840]{1,0:T(8,128)(2,1)S(1)} %get-tuple-element.270.pack3_ref.refs_14_), channel_id=1, source_target_pairs={{0,1},{1,0},{2,3},{3,2},{4,5},{5,4},{6,7},{7,6},{8,9},{9,8},{10,11... | collective-permute-start | bytes 11796488 | tf_op jit(solution)/shard_map/ppermute | solution.py:367
  125.1 10.6 %collective-permute-start.23 = (bf16[512,3840]{1,0:T(8,128)(2,1)S(1)}, bf16[512,3840]{1,0:T(8,128)(2,1)S(1)}, u32[]{:S(2)}, u32[]{:S(2)}) collective-permute-start(bf16[512,3840]{1,0:T(8,128)(2,1)S(1)} %get-tuple-element.275.pack4_ref.refs_10_), channel_id=1, source_target_pairs={{0,1},{1,0},{2,3},{3,2},{4,5},{5,4},{6,7},{7,6},{8,9},{9,8},{10,11... | collective-permute-start | bytes 11796488 | tf_op jit(solution)/shard_map/ppermute | solution.py:367
  126.7 16.4 %collective-permute-start.19 = (bf16[4,640,128]{2,1,0:T(8,128)(2,1)S(1)}, bf16[4,640,128]{2,1,0:T(8,128)(2,1)S(1)}, u32[]{:S(2)}, u32[]{:S(2)}) collective-permute-start(bf16[4,640,128]{2,1,0:T(8,128)(2,1)S(1)} %get-tuple-element.265), channel_id=1, source_target_pairs={{0,4},{1,5},{2,6},{3,7},{4,0},{5,1},{6,2},{7,3},{8,12},{9,13},{10,... | collective-permute-start | bytes 1966088 | tf_op jit(solution)/shard_map/ppermute | solution.py:367
  128.1 16.0 %collective-permute-start.20 = (bf16[4,640,128]{2,1,0:T(8,128)(2,1)S(1)}, bf16[4,640,128]{2,1,0:T(8,128)(2,1)S(1)}, u32[]{:S(2)}, u32[]{:S(2)}) collective-permute-start(bf16[4,640,128]{2,1,0:T(8,128)(2,1)S(1)} %get-tuple-element.266), channel_id=1, source_target_pairs={{0,2},{1,3},{2,0},{3,1},{4,6},{5,7},{6,4},{7,5},{8,10},{9,11},{10,... | collective-permute-start | bytes 1966088 | tf_op jit(solution)/shard_map/ppermute | solution.py:367
  144.1 4.8 %collective-permute-start.24 = (bf16[192,2048]{1,0:T(8,128)(2,1)S(1)}, bf16[192,2048]{1,0:T(8,128)(2,1)S(1)}, u32[]{:S(2)}, u32[]{:S(2)}) collective-permute-start(bf16[192,2048]{1,0:T(8,128)(2,1)S(1)} %get-tuple-element.284.refs_2_.dkv_ref), channel_id=1, source_target_pairs={{0,1},{1,0},{2,3},{3,2},{4,5},{5,4},{6,7},{7,6},{8,9},{9,8},{10,11... | collective-permute-start | bytes 2359304 | tf_op jit(solution)/shard_map/ppermute | solution.py:367
  145.2 7.5 %collective-permute-start.25 = (bf16[512,1024]{1,0:T(8,128)(2,1)S(1)}, bf16[512,1024]{1,0:T(8,128)(2,1)S(1)}, u32[]{:S(2)}, u32[]{:S(2)}) collective-permute-start(bf16[512,1024]{1,0:T(8,128)(2,1)S(1)} %get-tuple-element.316.refs_2_.dq_ref), channel_id=1, source_target_pairs={{0,1},{1,0},{2,3},{3,2},{4,5},{5,4},{6,7},{7,6},{8,9},{9,8},{10,11... | collective-permute-start | bytes 3145736 | tf_op jit(solution)/shard_map/ppermute | solution.py:367
  145.2 7.5 %collective-permute-start.26 = (bf16[512,768]{1,0:T(8,128)(2,1)S(1)}, bf16[512,768]{1,0:T(8,128)(2,1)S(1)}, u32[]{:S(2)}, u32[]{:S(2)}) collective-permute-start(bf16[512,768]{1,0:T(8,128)(2,1)S(1)} %get-tuple-element.289.refs_8_), channel_id=1, source_target_pairs={{0,1},{1,0},{2,3},{3,2},{4,5},{5,4},{6,7},{7,6},{8,9},{9,8},{10,11... | collective-permute-start | bytes 2359304 | tf_op jit(solution)/shard_map/ppermute | solution.py:367
  146.6 26.0 %collective-permute-start.28 = (bf16[2,640,128]{2,1,0:T(8,128)(2,1)S(1)}, bf16[2,640,128]{2,1,0:T(8,128)(2,1)S(1)}, u32[]{:S(2)}, u32[]{:S(2)}) collective-permute-start(bf16[2,640,128]{2,1,0:T(8,128)(2,1)S(1)} %get-tuple-element.298), channel_id=1, source_target_pairs={{0,8},{1,9},{2,10},{3,11},{4,12},{5,13},{6,14},{7,15},{8,0},{9,1},... | collective-permute-start | bytes 983048 | tf_op jit(solution)/shard_map/ppermute | solution.py:367
  151.4 21.3 %collective-permute-start.27 = (bf16[2,1280,128]{2,1,0:T(8,128)(2,1)S(1)}, bf16[2,1280,128]{2,1,0:T(8,128)(2,1)S(1)}, u32[]{:S(2)}, u32[]{:S(2)}) collective-permute-start(bf16[2,1280,128]{2,1,0:T(8,128)(2,1)S(1)} %get-tuple-element.293), channel_id=1, source_target_pairs={{0,2},{1,3},{2,0},{3,1},{4,6},{5,7},{6,4},{7,5},{8,10},{9,11},{10,... | collective-permute-start | bytes 1966088 | tf_op jit(solution)/shard_map/ppermute | solution.py:367
  176.8 19.2 %collective-permute-start.29 = (bf16[4,768,128]{2,1,0:T(8,128)(2,1)S(1)}, bf16[4,768,128]{2,1,0:T(8,128)(2,1)S(1)}, u32[]{:S(2)}, u32[]{:S(2)}) collective-permute-start(bf16[4,768,128]{2,1,0:T(8,128)(2,1)S(1)} %get-tuple-element.311), channel_id=1, source_target_pairs={{0,2},{1,3},{2,0},{3,1},{4,6},{5,7},{6,4},{7,5},{8,10},{9,11},{10,... | collective-permute-start | bytes 2359304 | tf_op jit(solution)/shard_map/ppermute | solution.py:367
  178.1 17.8 %collective-permute-start.30 = (bf16[1,1280,128]{2,1,0:T(8,128)(2,1)S(1)}, bf16[1,1280,128]{2,1,0:T(8,128)(2,1)S(1)}, u32[]{:S(2)}, u32[]{:S(2)}) collective-permute-start(bf16[1,1280,128]{2,1,0:T(8,128)(2,1)S(1)} %get-tuple-element.312), channel_id=1, source_target_pairs={{0,4},{1,5},{2,6},{3,7},{4,0},{5,1},{6,2},{7,3},{8,12},{9,13},{10,... | collective-permute-start | bytes 983048 | tf_op jit(solution)/shard_map/ppermute | solution.py:367
  178.3 17.7 %collective-permute-start.31 = (bf16[2,640,128]{2,1,0:T(8,128)(2,1)S(1)}, bf16[2,640,128]{2,1,0:T(8,128)(2,1)S(1)}, u32[]{:S(2)}, u32[]{:S(2)}) collective-permute-start(bf16[2,640,128]{2,1,0:T(8,128)(2,1)S(1)} %get-tuple-element.313), channel_id=1, source_target_pairs={{0,8},{1,9},{2,10},{3,11},{4,12},{5,13},{6,14},{7,15},{8,0},{9,1},... | collective-permute-start | bytes 983048 | tf_op jit(solution)/shard_map/ppermute | solution.py:367
  179.0 16.9 %collective-permute-start.32 = (f32[3,1792]{1,0:T(4,128)S(1)}, f32[3,1792]{1,0:T(4,128)S(1)}, u32[]{:S(2)}, u32[]{:S(2)}) collective-permute-start(f32[3,1792]{1,0:T(4,128)S(1)} %maximum_maximum_fusion), channel_id=1, source_target_pairs={{0,8},{1,9},{2,10},{3,11},{4,12},{5,13},{6,14},{7,15},{8,0},{9,1},... | collective-permute-start | bytes 64520 | tf_op jit(solution)/shard_map/ppermute | solution.py:367
  196.8 14.7 %collective-permute-start.33 = (bf16[2,768,128]{2,1,0:T(8,128)(2,1)S(1)}, bf16[2,768,128]{2,1,0:T(8,128)(2,1)S(1)}, u32[]{:S(2)}, u32[]{:S(2)}) collective-permute-start(bf16[2,768,128]{2,1,0:T(8,128)(2,1)S(1)} %get-tuple-element.337), channel_id=1, source_target_pairs={{0,4},{1,5},{2,6},{3,7},{4,0},{5,1},{6,2},{7,3},{8,12},{9,13},{10,... | collective-permute-start | bytes 1179656 | tf_op jit(solution)/shard_map/ppermute | solution.py:367
  196.8 16.7 %collective-permute-start.34 = (bf16[4,736,128]{2,1,0:T(8,128)(2,1)S(1)}, bf16[4,736,128]{2,1,0:T(8,128)(2,1)S(1)}, u32[]{:S(2)}, u32[]{:S(2)}) collective-permute-start(bf16[4,736,128]{2,1,0:T(8,128)(2,1)S(1)} %get-tuple-element.338), channel_id=1, source_target_pairs={{0,2},{1,3},{2,0},{3,1},{4,6},{5,7},{6,4},{7,5},{8,10},{9,11},{10,... | collective-permute-start | bytes 2261000 | tf_op jit(solution)/shard_map/ppermute | solution.py:367
  198.1 13.4 %collective-permute-start.35 = (bf16[1,1280,128]{2,1,0:T(8,128)(2,1)S(1)}, bf16[1,1280,128]{2,1,0:T(8,128)(2,1)S(1)}, u32[]{:S(2)}, u32[]{:S(2)}) collective-permute-start(bf16[1,1280,128]{2,1,0:T(8,128)(2,1)S(1)} %add_convert_fusion.1), channel_id=1, source_target_pairs={{0,8},{1,9},{10,2},{11,3},{12,4},{13,5},{14,6},{15,7},{16,24},{17,... | collective-permute-start | bytes 983048 | tf_op jit(solution)/shard_map/ppermute | solution.py:1370
  200.4 11.1 %collective-permute-start.36 = (f32[3,1792]{1,0:T(4,128)S(1)}, f32[3,1792]{1,0:T(4,128)S(1)}, u32[]{:S(2)}, u32[]{:S(2)}) collective-permute-start(f32[3,1792]{1,0:T(4,128)S(1)} %add.60), channel_id=1, source_target_pairs={{0,4},{1,5},{2,6},{3,7},{4,0},{5,1},{6,2},{7,3},{8,12},{9,13},{10,... | collective-permute-start | bytes 64520 | tf_op jit(solution)/shard_map/ppermute | solution.py:367
  214.3 14.5 %collective-permute-start.38 = (bf16[2,736,128]{2,1,0:T(8,128)(2,1)S(1)}, bf16[2,736,128]{2,1,0:T(8,128)(2,1)S(1)}, u32[]{:S(2)}, u32[]{:S(2)}) collective-permute-start(bf16[2,736,128]{2,1,0:T(8,128)(2,1)S(1)} %get-tuple-element.348), channel_id=1, source_target_pairs={{0,4},{1,5},{2,6},{3,7},{4,0},{5,1},{6,2},{7,3},{8,12},{9,13},{10,... | collective-permute-start | bytes 1130504 | tf_op jit(solution)/shard_map/ppermute | solution.py:367
  215.5 13.3 %collective-permute-start.39 = (bf16[4,608,128]{2,1,0:T(8,128)(2,1)S(1)}, bf16[4,608,128]{2,1,0:T(8,128)(2,1)S(1)}, u32[]{:S(2)}, u32[]{:S(2)}) collective-permute-start(bf16[4,608,128]{2,1,0:T(8,128)(2,1)S(1)} %get-tuple-element.349), channel_id=1, source_target_pairs={{0,2},{1,3},{2,0},{3,1},{4,6},{5,7},{6,4},{7,5},{8,10},{9,11},{10,... | collective-permute-start | bytes 1867784 | tf_op jit(solution)/shard_map/ppermute | solution.py:367
  217.2 11.6 %collective-permute-start.40 = (bf16[1,1280,128]{2,1,0:T(8,128)(2,1)S(1)}, bf16[1,1280,128]{2,1,0:T(8,128)(2,1)S(1)}, u32[]{:S(2)}, u32[]{:S(2)}) collective-permute-start(bf16[1,1280,128]{2,1,0:T(8,128)(2,1)S(1)} %add_convert_fusion), channel_id=1, source_target_pairs={{16,0},{17,1},{18,2},{19,3},{20,4},{21,5},{22,6},{23,7},{24,8},{25... | collective-permute-start | bytes 983048 | tf_op jit(solution)/shard_map/ppermute | solution.py:1372
  219.1 9.6 %collective-permute-start.37 = (bf16[1,768,128]{2,1,0:T(8,128)(2,1)S(1)}, bf16[1,768,128]{2,1,0:T(8,128)(2,1)S(1)}, u32[]{:S(2)}, u32[]{:S(2)}) collective-permute-start(bf16[1,768,128]{2,1,0:T(8,128)(2,1)S(1)} %get-tuple-element.345), channel_id=1, source_target_pairs={{0,8},{1,9},{2,10},{3,11},{4,12},{5,13},{6,14},{7,15},{8,0},{9,1},... | collective-permute-start | bytes 589832 | tf_op jit(solution)/shard_map/ppermute | solution.py:367
  219.4 9.3 %collective-permute-start.41 = (f32[3,1792]{1,0:T(4,128)S(1)}, f32[3,1792]{1,0:T(4,128)S(1)}, u32[]{:S(2)}, u32[]{:S(2)}) collective-permute-start(f32[3,1792]{1,0:T(4,128)S(1)} %add.62), channel_id=1, source_target_pairs={{0,2},{1,3},{2,0},{3,1},{4,6},{5,7},{6,4},{7,5},{8,10},{9,11},{10,... | collective-permute-start | bytes 64520 | tf_op jit(solution)/shard_map/ppermute | solution.py:367
  228.8 11.3 %collective-permute-start.44 = (bf16[4,384,128]{2,1,0:T(8,128)(2,1)S(1)}, bf16[4,384,128]{2,1,0:T(8,128)(2,1)S(1)}, u32[]{:S(2)}, u32[]{:S(2)}) collective-permute-start(bf16[4,384,128]{2,1,0:T(8,128)(2,1)S(1)} %get-tuple-element.361), channel_id=1, source_target_pairs={{0,2},{1,3},{2,0},{3,1},{4,6},{5,7},{6,4},{7,5},{8,10},{9,11},{10,... | collective-permute-start | bytes 1179656 | tf_op jit(solution)/shard_map/ppermute | solution.py:367
  231.5 8.6 %collective-permute-start.43 = (bf16[2,608,128]{2,1,0:T(8,128)(2,1)S(1)}, bf16[2,608,128]{2,1,0:T(8,128)(2,1)S(1)}, u32[]{:S(2)}, u32[]{:S(2)}) collective-permute-start(bf16[2,608,128]{2,1,0:T(8,128)(2,1)S(1)} %get-tuple-element.360), channel_id=1, source_target_pairs={{0,4},{1,5},{2,6},{3,7},{4,0},{5,1},{6,2},{7,3},{8,12},{9,13},{10,... | collective-permute-start | bytes 933896 | tf_op jit(solution)/shard_map/ppermute | solution.py:367
  232.2 7.2 %collective-permute-start.42 = (bf16[1,736,128]{2,1,0:T(8,128)(2,1)S(1)}, bf16[1,736,128]{2,1,0:T(8,128)(2,1)S(1)}, u32[]{:S(2)}, u32[]{:S(2)}) collective-permute-start(bf16[1,736,128]{2,1,0:T(8,128)(2,1)S(1)} %get-tuple-element.357), channel_id=1, source_target_pairs={{0,8},{1,9},{2,10},{3,11},{4,12},{5,13},{6,14},{7,15},{8,0},{9,1},... | collective-permute-start | bytes 565256 | tf_op jit(solution)/shard_map/ppermute | solution.py:367
  232.6 6.1 %collective-permute-start.45 = (f32[3,1792]{1,0:T(4,128)S(1)}, f32[3,1792]{1,0:T(4,128)S(1)}, u32[]{:S(2)}, u32[]{:S(2)}) collective-permute-start(f32[3,1792]{1,0:T(4,128)S(1)} %add.64), channel_id=1, source_target_pairs={{0,1},{1,0},{2,3},{3,2},{4,5},{5,4},{6,7},{7,6},{8,9},{9,8},{10,11... | collective-permute-start | bytes 64520 | tf_op jit(solution)/shard_map/ppermute | solution.py:367
  240.7 8.3 %collective-permute-start.47 = (bf16[2,384,128]{2,1,0:T(8,128)(2,1)S(1)}, bf16[2,384,128]{2,1,0:T(8,128)(2,1)S(1)}, u32[]{:S(2)}, u32[]{:S(2)}) collective-permute-start(bf16[2,384,128]{2,1,0:T(8,128)(2,1)S(1)} %get-tuple-element.370), channel_id=1, source_target_pairs={{0,4},{1,5},{2,6},{3,7},{4,0},{5,1},{6,2},{7,3},{8,12},{9,13},{10,... | collective-permute-start | bytes 589832 | tf_op jit(solution)/shard_map/ppermute | solution.py:367
  241.5 7.5 %collective-permute-start.46 = (bf16[1,608,128]{2,1,0:T(8,128)(2,1)S(1)}, bf16[1,608,128]{2,1,0:T(8,128)(2,1)S(1)}, u32[]{:S(2)}, u32[]{:S(2)}) collective-permute-start(bf16[1,608,128]{2,1,0:T(8,128)(2,1)S(1)} %get-tuple-element.367), channel_id=1, source_target_pairs={{0,8},{1,9},{2,10},{3,11},{4,12},{5,13},{6,14},{7,15},{8,0},{9,1},... | collective-permute-start | bytes 466952 | tf_op jit(solution)/shard_map/ppermute | solution.py:367
  249.7 8.4 %collective-permute-start.48 = (bf16[1,384,128]{2,1,0:T(8,128)(2,1)S(1)}, bf16[1,384,128]{2,1,0:T(8,128)(2,1)S(1)}, u32[]{:S(2)}, u32[]{:S(2)}) collective-permute-start(bf16[1,384,128]{2,1,0:T(8,128)(2,1)S(1)} %get-tuple-element.375), channel_id=1, source_target_pairs={{0,8},{1,9},{2,10},{3,11},{4,12},{5,13},{6,14},{7,15},{8,0},{9,1},... | collective-permute-start | bytes 294920 | tf_op jit(solution)/shard_map/ppermute | solution.py:367
  259.9 9.9 %collective-permute-start.49 = (f32[2528,128]{1,0:T(8,128)S(1)}, f32[2528,128]{1,0:T(8,128)S(1)}, u32[]{:S(2)}, u32[]{:S(2)}) collective-permute-start(f32[2528,128]{1,0:T(8,128)S(1)} %get-tuple-element.378), channel_id=1, source_target_pairs={{0,1},{1,0},{2,3},{3,2},{4,5},{5,4},{6,7},{7,6},{8,9},{9,8},{10,11... | collective-permute-start | bytes 3883016 | tf_op jit(solution)/shard_map/ppermute | solution.py:367
  (93 other events, 748.1 us)

commit v2 on v1

--- a/solution.py
+++ b/solution.py
@@ -31,7 +31,7 @@
 
 
 def cost(us):
-    return pl.CostEstimate(flops=int(us * 1e9), bytes_accessed=1000, transcendentals=0)
+    return pl.CostEstimate(flops=int(us * 10e9), bytes_accessed=1000, transcendentals=0)
 
 
 def lane_block(ref, rows, block):
@@ -296,8 +296,8 @@
             def _(i, job=job, units=units, bm=bm, rows=rows, a_refs=a_refs, a_first=a_first):
                 columns = pl.ds(pl.multiple_of(a_first + i * bm, LANES), bm)
                 a = jnp.concatenate([a_ref[:, columns] for a_ref in a_refs], axis=0).T
-                for u0 in range(0, units, 4):
-                    u1 = min(u0 + 4, units)
+                for u0 in range(0, units, 12):
+                    u1 = min(u0 + 12, units)
                     total = mm(a, chosen_ref[:, u0 * LANES : u1 * LANES])
                     for u in range(u0, u1):
                         stage_ref[pl.ds(u, bm, stride=units), :] = total[
@@ -356,7 +356,7 @@
         out_specs=pl.BlockSpec(memory_space=pltpu.VMEM),
         out_shape=jax.ShapeDtypeStruct((total_rows, LANES), BF16),
         scratch_shapes=scratch,
-        compiler_params=pltpu.CompilerParams(vmem_limit_bytes=held + (7 if resident else 8) * 1024 * 1024),
+        compiler_params=pltpu.CompilerParams(vmem_limit_bytes=held + (8 if resident else 10) * 1024 * 1024),
         cost_estimate=cost(us),
         name="flat_grads",
     )(side, *arrays)

time: 275 us -> 270 us (0.982)
  waiting for transfers between devices: 60.5 us -> 57 us
  starting transfers between devices: 54.6 us -> 51.3 us
  other arithmetic: 0.73 us -> 3.9 us
    ppermute x43, waiting for transfers between devices: 57.6 us -> 53.3 us  [dp_swap(): return lax.ppermute(block, 'dp', [(i, i ^ bit) for i in range(count)])]
    unnamed x182 -> x188, local copies, waits for them, and re-layouts: 16.8 us -> 14.4 us
  transfers between devices with their start and end apart: 50 -> 50, of which waited for: 19 -> 15; matrix products, arithmetic and copies ran while one was open for 3% -> 4% of each run, Pallas kernels for 42% -> 46%
where the time goes in v2:
time: 270 us; the launch traced here: 267 us
  Pallas kernels  131 us (49%)
  waiting for transfers between devices  57 us (21%)
  starting transfers between devices  51.3 us (19%)
  local copies, waits for them, and re-layouts  15.7 us (6%)
  matrix products  5.8 us (2%)
  other arithmetic  3.9 us (1%)
    pallas_call x10, Pallas kernels, fused(): pl.pallas_call(kernel, in_specs=in_specs, out_specs=[vmem] * len(outs), o...  73.2 us
    ppermute x43, waiting for transfers between devices, dp_swap(): return lax.ppermute(block, 'dp', [(i, i ^ bit) for i in range(count)])  53.3 us
    ppermute x43, starting transfers between devices, dp_swap(): return lax.ppermute(block, 'dp', [(i, i ^ bit) for i in range(count)])  44.9 us
    pallas_call x3, Pallas kernels, flat_grads(): pl.pallas_call(functools.partial(flat_kernel, plans=plans, found=found, q...  25.2 us
    unnamed x188, local copies, waits for them, and re-layouts  14.4 us
    pallas_call x11, Pallas kernels, add_split(): pl.pallas_call(functools.partial(add_split_kernel, plan=tuple(plan), inpu...  10.5 us
    pallas_call x2, Pallas kernels, attend_back(): pl.pallas_call(functools.partial(body, pairs=pairs, blocks=blocks, cols=c...  10.3 us
    dot_general x6, matrix products, mm(): return jnp.dot(a, b, preferred_element_type=F32)  5.8 us
  transfers between devices with their start and end apart: 50, of which 15 were waited for; matrix products, arithmetic and copies ran while one was open for 4% of the time, Pallas kernels for 46%

profile of v2, /device:TPU:3, one launch (start us, length us, event | category | flops | bytes accessed | tf_op | source)
XLA Modules:
  0.0 267.3 jit_solution(145959018251944114)
XLA Ops:
  0.7 1.5 collective-permute-start
  3.9 1.8 collective-permute-done.2
  6.1 2.8 %collective-permute-start.3 = (bf16[192,1024]{1,0:T(8,128)(2,1)S(1)}, bf16[192,1024]{1,0:T(8,128)(2,1)S(1)}, u32[]{:S(2)}, u32[]{:S(2)}) collective-permute-start(bf16[192,1024]{1,0:T(8,128)(2,1)S(1)} %fusion.x_ref.refs_0_), channel_id=1, source_target_pairs={{0,1},{1,0},{2,3},{3,2},{4,5},{5,4},{6,7},{7,6},{8,9},{9,8},{10,11... | collective-permute-start | bytes 1179656 | tf_op jit(solution)/shard_map/ppermute | solution.py:367
  8.8 2.2 convolution_convert_fusion.1.given_ref.refs_0_
  12.2 1.9 collective-permute-done.1
  16.6 2.2 collective-permute-start.12
  18.8 8.4 %co_forward.3 = (bf16[512,2048]{1,0:T(8,128)(2,1)S(1)}, bf16[192,2048]{1,0:T(8,128)(2,1)S(1)}, f32[192,1024]{1,0:T(8,128)S(1)}, f32[192,128]{1,0:T(8,128)S(1)}) custom-call(s32[4]{0:T(128)S(1)} %pad_add_fusion.1.lens_ref, bf16[192,1024]{1,0:T(8,128)(2,1)S(1)} %fusion.x_ref.refs_0_, bf16[192,1024]{1,0:T(8,128)(2,1)S(1)} %convolution_convert_fusion.1.given_ref.refs_0_, ...), custom_call_target="tpu_custom_call" | custom-call | flops 70000001024 | bytes 1000 | tf_op jit(solution)/shard_map/co_forward/pallas_call | solution.py:841
  29.3 3.7 %mlp_forward.2 = (bf16[192,2048]{1,0:T(8,128)(2,1)S(1)}, bf16[192,1024]{1,0:T(8,128)(2,1)S(1)}, f32[192,1024]{1,0:T(8,128)S(1)}, f32[192,128]{1,0:T(8,128)S(1)}, bf16[192,3072]{1,0:T(8,128)(2,1)S(1)}) custom-call(bf16[192,2048]{1,0:T(8,128)(2,1)S(1)} %get-tuple-element.204.pack1_ref.refs_4_, f32[192,1024]{1,0:T(8,128)S(1)} %get-tuple-element.205.n1_ref, ...), custom_call_target="tpu_custom_call" | custom-call | flops 48000000000 | bytes 1000 | tf_op jit(solution)/shard_map/mlp_forward/pallas_call | solution.py:841
  33.6 10.5 %self_turn.2 = (bf16[192,5120]{1,0:T(8,128)(2,1)S(1)}, bf16[192,1024]{1,0:T(8,128)(2,1)S(1)}, f32[192,1024]{1,0:T(8,128)S(1)}, f32[1,1024]{1,0:T(1,128)S(1)}) custom-call(s32[4]{0:T(128)S(1)} %pad_add_fusion.1.lens_ref, bf16[192,3072]{1,0:T(8,128)(2,1)S(1)} %get-tuple-element.209.r_ref, f32[192,1024]{1,0:T(8,128)S(1)} %get-tuple-element.210.n2_ref, ...), custom_call_target="tpu_custom_call" | custom-call | flops 105000001536 | bytes 1000 | tf_op jit(solution)/shard_map/self_turn/pallas_call | solution.py:841
  44.8 3.6 %mlp_back.2 = (bf16[192,2048]{1,0:T(8,128)(2,1)S(1)}, f32[192,1024]{1,0:T(8,128)S(1)}, f32[1,1024]{1,0:T(1,128)S(1)}) custom-call(bf16[192,5120]{1,0:T(8,128)(2,1)S(1)} %get-tuple-element.216.pack3_ref.refs_12_, f32[192,1024]{1,0:T(8,128)S(1)} %get-tuple-element.217.de_ref, f32[192,1024]{1,0:T(8,128)S(1)} %get-tuple-element.210.n2_ref, ...), custom_call_target="tpu_custom_call" | custom-call | flops 27428571136 | bytes 1000 | tf_op jit(solution)/shard_map/mlp_back/pallas_call | solution.py:841
  48.8 2.2 context_back.2
  51.3 5.2 %attend_back.2 = (bf16[192,1024]{1,0:T(8,128)(2,1)S(1)}, bf16[512,2048]{1,0:T(8,128)(2,1)S(1)}) custom-call(s32[4]{0:T(128)S(1)} %pad_add_fusion.1.lens_ref, bf16[192,1024]{1,0:T(8,128)(2,1)S(1)} %copy-done.19, bf16[512,2048]{1,0:T(8,128)(2,1)S(1)} %get-tuple-element.203.refs_1_, bf16[192,1024]{1,0:T(8,128)(2,1)S(1)} %get-tuple-element.225.refs_2_), custom_call_target="tpu_custom_call" | custom-call | flops 60000002048 | bytes 1000 | tf_op jit(solution)/shard_map/attend_back/pallas_call | solution.py:213
  57.0 9.3 %co_forward.2 = (bf16[512,1024]{1,0:T(8,128)(2,1)S(1)}, bf16[512,1792]{1,0:T(8,128)(2,1)S(1)}, f32[512,768]{1,0:T(8,128)S(1)}, f32[512,128]{1,0:T(8,128)S(1)}) custom-call(s32[4]{0:T(128)S(1)} %pad_add_fusion.1.lens_ref, bf16[512,768]{1,0:T(8,128)(2,1)} %pad_maximum_fusion.x_ref.source_ref.refs_0_, ...), custom_call_target="tpu_custom_call" | custom-call | flops 70000001024 | bytes 1000 | tf_op jit(solution)/shard_map/co_forward/pallas_call | solution.py:841
  67.3 1.7 pad_maximum_fusion.1.cot_ref
  69.3 6.2 %flat_grads.3.flat_ref = bf16[20480,128]{1,0:T(8,128)(2,1)S(1)} custom-call(s32[2]{0:T(128)S(1)} %pad_add_fusion.side_ref, bf16[192,1024]{1,0:T(8,128)(2,1)S(1)} %copy-done.4, bf16[192,1024]{1,0:T(8,128)(2,1)S(1)} %copy-done.54, bf16[192,1024]{1,0:T(8,128)(2,1)S(1)} %get-tuple-element.321.refs_2_.dq_ref, ...), custom_call_target="tpu_custom_call" | custom-call | flops 60000002048 | bytes 1000 | tf_op jit(solution)/shard_map/flat_grads/pallas_call | solution.py:350
  80.9 10.7 %mlp_forward.3 = (bf16[512,3840]{1,0:T(8,128)(2,1)S(1)}, bf16[512,3072]{1,0:T(8,128)(2,1)S(1)}, f32[512,768]{1,0:T(8,128)S(1)}, f32[512,128]{1,0:T(8,128)S(1)}, bf16[512,2304]{1,0:T(8,128)(2,1)S(1)}) custom-call(bf16[512,1792]{1,0:T(8,128)(2,1)S(1)} %get-tuple-element.246.pack1_ref.refs_6_, f32[512,768]{1,0:T(8,128)S(1)} %get-tuple-element.247.n1_ref, ...), custom_call_target="tpu_custom_call" | custom-call | flops 128000000000 | bytes 1000 | tf_op jit(solution)/shard_map/mlp_forward/pallas_call | solution.py:841
  91.6 1.4 copy-done.68
  98.3 1.7 copy-done.69
  99.9 12.4 %self_turn.3 = (bf16[512,3840]{1,0:T(8,128)(2,1)S(1)}, bf16[512,768]{1,0:T(8,128)(2,1)S(1)}, f32[512,768]{1,0:T(8,128)S(1)}, f32[1,768]{1,0:T(1,128)S(1)}) custom-call(s32[4]{0:T(128)S(1)} %copy-done.61, bf16[512,2304]{1,0:T(8,128)(2,1)S(1)} %copy-done.69, f32[512,768]{1,0:T(8,128)S(1)} %get-tuple-element.257.n2_ref, f32[3,768]{1,0:T(4,128)S(1)} %copy-done.57, ...), custom_call_target="tpu_custom_call" | custom-call | flops 130000003072 | bytes 1000 | tf_op jit(solution)/shard_map/self_turn/pallas_call | solution.py:841
  112.5 2.2 add_split.11
  116.6 6.0 %mlp_back.3 = (bf16[512,3840]{1,0:T(8,128)(2,1)S(1)}, f32[512,768]{1,0:T(8,128)S(1)}, f32[1,768]{1,0:T(1,128)S(1)}) custom-call(bf16[512,3840]{1,0:T(8,128)(2,1)S(1)} %get-tuple-element.270.pack3_ref.refs_14_, f32[512,768]{1,0:T(8,128)S(1)} %get-tuple-element.271.de_ref, f32[512,768]{1,0:T(8,128)S(1)} %get-tuple-element.257.n2_ref, ...), custom_call_target="tpu_custom_call" | custom-call | flops 73142853632 | bytes 1000 | tf_op jit(solution)/shard_map/mlp_back/pallas_call | solution.py:841
  123.4 1.9 copy-done.88
  125.4 6.3 %context_back.3 = (bf16[512,768]{1,0:T(8,128)(2,1)S(1)}, f32[512,768]{1,0:T(8,128)S(1)}, bf16[512,1024]{1,0:T(8,128)(2,1)S(1)}, f32[1,768]{1,0:T(1,128)S(1)}) custom-call(bf16[512,3840]{1,0:T(8,128)(2,1)S(1)} %get-tuple-element.275.pack4_ref.refs_10_, f32[512,768]{1,0:T(8,128)S(1)} %get-tuple-element.276.db_ref, f32[512,768]{1,0:T(8,128)S(1)} %copy-done.65, ...), custom_call_target="tpu_custom_call" | custom-call | flops 64000000000 | bytes 1000 | tf_op jit(solution)/shard_map/context_back/pallas_call | solution.py:841
  132.4 5.1 %attend_back.3 = (bf16[512,1024]{1,0:T(8,128)(2,1)S(1)}, bf16[192,2048]{1,0:T(8,128)(2,1)S(1)}) custom-call(s32[4]{0:T(128)S(1)} %copy-done.62, bf16[512,1024]{1,0:T(8,128)(2,1)S(1)} %copy-done.67, bf16[192,2048]{1,0:T(8,128)(2,1)S(1)} %copy-done.15, bf16[512,1024]{1,0:T(8,128)(2,1)S(1)} %get-tuple-element.279.refs_2_), custom_call_target="tpu_custom_call" | custom-call | flops 60000002048 | bytes 1000 | tf_op jit(solution)/shard_map/attend_back/pallas_call | solution.py:213
  138.2 2.3 add_split.12
  140.6 2.3 collective-permute-start.28
  143.4 1.7 flat_grads.4.flat_ref
  149.6 17.2 %flat_grads.5.flat_ref = bf16[19968,128]{1,0:T(8,128)(2,1)} custom-call(s32[2]{0:T(128)S(1)} %copy-done.59, bf16[512,768]{1,0:T(8,128)(2,1)} %pad_maximum_fusion.x_ref.source_ref.refs_0_, bf16[512,768]{1,0:T(8,128)(2,1)} %collective-permute-done.12.refs_1_, bf16[512,1024]{1,0:T(8,128)(2,1)S(1)} %get-tuple-element.316.refs_2_.dq_ref, ...), custom_call_target="tpu_custom_call" | custom-call | flops 140000002048 | bytes 1000 | tf_op jit(solution)/shard_map/flat_grads/pallas_call | solution.py:350
  166.9 2.4 copy-done.63
  173.0 2.3 collective-permute-start.31
  175.3 2.9 %input_grads.3 = (bf16[72,1024]{1,0:T(8,128)(2,1)}, bf16[72,1024]{1,0:T(8,128)(2,1)}) custom-call(f32[192,1024]{1,0:T(8,128)S(1)} %get-tuple-element.320.da_ref, bf16[192,1024]{1,0:T(8,128)(2,1)S(1)} %copy-done.17, bf16[192,2048]{1,0:T(8,128)(2,1)S(1)} %copy-done.13, bf16[192,1024]{1,0:T(8,128)(2,1)S(1)} %get-tuple-element.322.y_ref, ...), custom_call_target="tpu_custom_call" | custom-call | flops 2000000000 | bytes 1000 | tf_op jit(solution)/shard_map/input_grads/pallas_call | solution.py:933
  178.3 2.3 input_grads.2
  180.6 7.7 %collective-permute-done.30 = bf16[1,1280,128]{2,1,0:T(8,128)(2,1)S(1)} collective-permute-done((bf16[1,1280,128]{2,1,0:T(8,128)(2,1)S(1)}, bf16[1,1280,128]{2,1,0:T(8,128)(2,1)S(1)}, u32[]{:S(2)}, u32[]{:S(2)}) %collective-permute-start.30) | collective-permute-done | bytes 327712 | tf_op jit(solution)/shard_map/ppermute | solution.py:367
  188.2 1.6 collective-permute-done.29.refs_1_
  192.2 2.0 collective-permute-start.35
  194.3 12.4 %collective-permute-done.36 = f32[3,1792]{1,0:T(4,128)S(1)} collective-permute-done((f32[3,1792]{1,0:T(4,128)S(1)}, f32[3,1792]{1,0:T(4,128)S(1)}, u32[]{:S(2)}, u32[]{:S(2)}) %collective-permute-start.36) | collective-permute-done | bytes 21536 | tf_op jit(solution)/shard_map/ppermute | solution.py:367
  206.7 2.0 collective-permute-done.34.refs_1_
  211.2 2.7 collective-permute-start.39
  214.6 12.3 %collective-permute-done.41 = f32[3,1792]{1,0:T(4,128)S(1)} collective-permute-done((f32[3,1792]{1,0:T(4,128)S(1)}, f32[3,1792]{1,0:T(4,128)S(1)}, u32[]{:S(2)}, u32[]{:S(2)}) %collective-permute-start.41) | collective-permute-done | bytes 21536 | tf_op jit(solution)/shard_map/ppermute | solution.py:367
  230.7 3.7 %collective-permute-start.45 = (f32[3,1792]{1,0:T(4,128)S(1)}, f32[3,1792]{1,0:T(4,128)S(1)}, u32[]{:S(2)}, u32[]{:S(2)}) collective-permute-start(f32[3,1792]{1,0:T(4,128)S(1)} %add.64), channel_id=1, source_target_pairs={{0,1},{1,0},{2,3},{3,2},{4,5},{5,4},{6,7},{7,6},{8,9},{9,8},{10,11... | collective-permute-start | bytes 64520 | tf_op jit(solution)/shard_map/ppermute | solution.py:367
  235.3 5.2 %collective-permute-done.42.refs_7_ = bf16[1,736,128]{2,1,0:T(8,128)(2,1)S(1)} collective-permute-done((bf16[1,736,128]{2,1,0:T(8,128)(2,1)S(1)}, bf16[1,736,128]{2,1,0:T(8,128)(2,1)S(1)}, u32[]{:S(2)}, u32[]{:S(2)}) %collective-permute-start.42) | collective-permute-done | bytes 188448 | tf_op jit(solution)/shard_map/ppermute | solution.py:367
  241.9 6.0 %collective-permute-done.46.refs_9_ = bf16[1,608,128]{2,1,0:T(8,128)(2,1)S(1)} collective-permute-done((bf16[1,608,128]{2,1,0:T(8,128)(2,1)S(1)}, bf16[1,608,128]{2,1,0:T(8,128)(2,1)S(1)}, u32[]{:S(2)}, u32[]{:S(2)}) %collective-permute-start.46) | collective-permute-done | bytes 155680 | tf_op jit(solution)/shard_map/ppermute | solution.py:367
  248.5 1.7 collective-permute-start.48
  250.1 2.9 %collective-permute-done.48.refs_11_ = bf16[1,384,128]{2,1,0:T(8,128)(2,1)S(1)} collective-permute-done((bf16[1,384,128]{2,1,0:T(8,128)(2,1)S(1)}, bf16[1,384,128]{2,1,0:T(8,128)(2,1)S(1)}, u32[]{:S(2)}, u32[]{:S(2)}) %collective-permute-start.48) | collective-permute-done | bytes 98336 | tf_op jit(solution)/shard_map/ppermute | solution.py:367
  253.0 2.3 finish.1
  255.3 6.9 %collective-permute-start.49 = (f32[2528,128]{1,0:T(8,128)S(1)}, f32[2528,128]{1,0:T(8,128)S(1)}, u32[]{:S(2)}, u32[]{:S(2)}) collective-permute-start(f32[2528,128]{1,0:T(8,128)S(1)} %get-tuple-element.378), channel_id=1, source_target_pairs={{0,1},{1,0},{2,3},{3,2},{4,5},{5,4},{6,7},{7,6},{8,9},{9,8},{10,11... | collective-permute-start | bytes 3883016 | tf_op jit(solution)/shard_map/ppermute | solution.py:367
  263.4 1.4 collective-permute-done.49.far_ref
  264.8 2.2 join.1
  (302 shorter events, 47.8 us)
Async XLA Ops:
  0.6 5.0 %collective-permute-start.2 = (bf16[72,1024]{1,0:T(8,128)(2,1)}, bf16[72,1024]{1,0:T(8,128)(2,1)S(1)}, u32[]{:S(2)}, u32[]{:S(2)}) collective-permute-start(bf16[72,1024]{1,0:T(8,128)(2,1)} %param.22), channel_id=1, source_target_pairs={{0,16},{16,0},{1,17},{17,1},{2,18},{18,2},{3,19},{19,3},{4,20},{20... | collective-permute-start | bytes 442376 | tf_op jit(solution)/shard_map/ppermute | solution.py:371
  0.7 13.3 %collective-permute-start = (bf16[256,768]{1,0:T(8,128)(2,1)}, bf16[256,768]{1,0:T(8,128)(2,1)S(1)}, u32[]{:S(2)}, u32[]{:S(2)}) collective-permute-start(bf16[256,768]{1,0:T(8,128)(2,1)} %param.21), channel_id=1, source_target_pairs={{0,16},{16,0},{1,17},{17,1},{2,18},{18,2},{3,19},{19,3},{4,20},{20... | collective-permute-start | bytes 1179656 | tf_op jit(solution)/shard_map/ppermute | solution.py:371
  2.2 11.9 %collective-permute-start.1 = (s32[2]{0:T(128)}, s32[2]{0:T(128)S(1)}, u32[]{:S(2)}, u32[]{:S(2)}) collective-permute-start(s32[2]{0:T(128)} %param.23), channel_id=1, source_target_pairs={{0,16},{16,0},{1,17},{17,1},{2,18},{18,2},{3,19},{19,3},{4,20},{20... | collective-permute-start | bytes 32 | tf_op jit(solution)/shard_map/ppermute | solution.py:371
  6.1 21.7 %collective-permute-start.3 = (bf16[192,1024]{1,0:T(8,128)(2,1)S(1)}, bf16[192,1024]{1,0:T(8,128)(2,1)S(1)}, u32[]{:S(2)}, u32[]{:S(2)}) collective-permute-start(bf16[192,1024]{1,0:T(8,128)(2,1)S(1)} %fusion.x_ref.refs_0_), channel_id=1, source_target_pairs={{0,1},{1,0},{2,3},{3,2},{4,5},{5,4},{6,7},{7,6},{8,9},{9,8},{10,11... | collective-permute-start | bytes 1179656 | tf_op jit(solution)/shard_map/ppermute | solution.py:367
  15.1 17.9 %collective-permute-start.5 = (bf16[72,1024]{1,0:T(8,128)(2,1)S(1)}, bf16[72,1024]{1,0:T(8,128)(2,1)S(1)}, u32[]{:S(2)}, u32[]{:S(2)}) collective-permute-start(bf16[72,1024]{1,0:T(8,128)(2,1)S(1)} %copy-done.71), channel_id=1, source_target_pairs={{0,16},{16,0},{1,17},{17,1},{2,18},{18,2},{3,19},{19,3},{4,20},{20... | collective-permute-start | bytes 442376 | tf_op jit(solution)/shard_map/ppermute | solution.py:371
  15.5 28.7 %collective-permute-start.6 = (bf16[256,768]{1,0:T(8,128)(2,1)}, bf16[256,768]{1,0:T(8,128)(2,1)}, u32[]{:S(2)}, u32[]{:S(2)}) collective-permute-start(bf16[256,768]{1,0:T(8,128)(2,1)} %param.40), channel_id=1, source_target_pairs={{0,16},{16,0},{1,17},{17,1},{2,18},{18,2},{3,19},{19,3},{4,20},{20... | collective-permute-start | bytes 1179656 | tf_op jit(solution)/shard_map/ppermute | solution.py:371
  16.6 62.5 %collective-permute-start.12 = (bf16[512,768]{1,0:T(8,128)(2,1)}, bf16[512,768]{1,0:T(8,128)(2,1)}, u32[]{:S(2)}, u32[]{:S(2)}) collective-permute-start(bf16[512,768]{1,0:T(8,128)(2,1)} %pad_maximum_fusion.x_ref.source_ref.refs_0_), channel_id=1, source_target_pairs={{0,1},{1,0},{2,3},{3,2},{4,5},{5,4},{6,7},{7,6},{8,9},{9,8},{10,11... | collective-permute-start | bytes 2359304 | tf_op jit(solution)/shard_map/ppermute | solution.py:367
  28.5 5.0 %collective-permute-start.4 = (bf16[192,2048]{1,0:T(8,128)(2,1)S(1)}, bf16[192,2048]{1,0:T(8,128)(2,1)S(1)}, u32[]{:S(2)}, u32[]{:S(2)}) collective-permute-start(bf16[192,2048]{1,0:T(8,128)(2,1)S(1)} %get-tuple-element.204.pack1_ref.refs_4_), channel_id=1, source_target_pairs={{0,1},{1,0},{2,3},{3,2},{4,5},{5,4},{6,7},{7,6},{8,9},{9,8},{10,11... | collective-permute-start | bytes 2359304 | tf_op jit(solution)/shard_map/ppermute | solution.py:367
  33.5 10.7 %collective-permute-start.7 = (bf16[192,2048]{1,0:T(8,128)(2,1)S(1)}, bf16[192,2048]{1,0:T(8,128)(2,1)S(1)}, u32[]{:S(2)}, u32[]{:S(2)}) collective-permute-start(bf16[192,2048]{1,0:T(8,128)(2,1)S(1)} %get-tuple-element.215.refs_10_), channel_id=1, source_target_pairs={{0,1},{1,0},{2,3},{3,2},{4,5},{5,4},{6,7},{7,6},{8,9},{9,8},{10,11... | collective-permute-start | bytes 2359304 | tf_op jit(solution)/shard_map/ppermute | solution.py:367
  44.2 4.2 %collective-permute-start.8 = (bf16[192,5120]{1,0:T(8,128)(2,1)S(1)}, bf16[192,5120]{1,0:T(8,128)(2,1)S(1)}, u32[]{:S(2)}, u32[]{:S(2)}) collective-permute-start(bf16[192,5120]{1,0:T(8,128)(2,1)S(1)} %get-tuple-element.216.pack3_ref.refs_12_), channel_id=1, source_target_pairs={{0,1},{1,0},{2,3},{3,2},{4,5},{5,4},{6,7},{7,6},{8,9},{9,8},{10,11... | collective-permute-start | bytes 5898248 | tf_op jit(solution)/shard_map/ppermute | solution.py:367
  51.0 18.3 %collective-permute-start.11 = (bf16[192,1024]{1,0:T(8,128)(2,1)S(1)}, bf16[192,1024]{1,0:T(8,128)(2,1)S(1)}, u32[]{:S(2)}, u32[]{:S(2)}) collective-permute-start(bf16[192,1024]{1,0:T(8,128)(2,1)S(1)} %get-tuple-element.228.refs_6_), channel_id=1, source_target_pairs={{0,1},{1,0},{2,3},{3,2},{4,5},{5,4},{6,7},{7,6},{8,9},{9,8},{10,11... | collective-permute-start | bytes 1179656 | tf_op jit(solution)/shard_map/ppermute | solution.py:367
  56.6 12.7 %collective-permute-start.10 = (bf16[192,1024]{1,0:T(8,128)(2,1)S(1)}, bf16[192,1024]{1,0:T(8,128)(2,1)S(1)}, u32[]{:S(2)}, u32[]{:S(2)}) collective-permute-start(bf16[192,1024]{1,0:T(8,128)(2,1)S(1)} %get-tuple-element.321.refs_2_.dq_ref), channel_id=1, source_target_pairs={{0,1},{1,0},{2,3},{3,2},{4,5},{5,4},{6,7},{7,6},{8,9},{9,8},{10,11... | collective-permute-start | bytes 1179656 | tf_op jit(solution)/shard_map/ppermute | solution.py:367
  69.0 10.1 %collective-permute-start.13 = (bf16[512,2048]{1,0:T(8,128)(2,1)S(1)}, bf16[512,2048]{1,0:T(8,128)(2,1)S(1)}, u32[]{:S(2)}, u32[]{:S(2)}) collective-permute-start(bf16[512,2048]{1,0:T(8,128)(2,1)S(1)} %get-tuple-element.239.refs_4_.dkv_ref), channel_id=1, source_target_pairs={{0,1},{1,0},{2,3},{3,2},{4,5},{5,4},{6,7},{7,6},{8,9},{9,8},{10,11... | collective-permute-start | bytes 6291464 | tf_op jit(solution)/shard_map/ppermute | solution.py:367
  76.5 16.5 %collective-permute-start.14 = (bf16[4,640,128]{2,1,0:T(8,128)(2,1)S(1)}, bf16[4,640,128]{2,1,0:T(8,128)(2,1)S(1)}, u32[]{:S(2)}, u32[]{:S(2)}) collective-permute-start(bf16[4,640,128]{2,1,0:T(8,128)(2,1)S(1)} %get-tuple-element.242), channel_id=1, source_target_pairs={{0,2},{1,3},{2,0},{3,1},{4,6},{5,7},{6,4},{7,5},{8,10},{9,11},{10,... | collective-permute-start | bytes 1966088 | tf_op jit(solution)/shard_map/ppermute | solution.py:367
  77.8 15.6 %collective-permute-start.15 = (bf16[4,640,128]{2,1,0:T(8,128)(2,1)S(1)}, bf16[4,640,128]{2,1,0:T(8,128)(2,1)S(1)}, u32[]{:S(2)}, u32[]{:S(2)}) collective-permute-start(bf16[4,640,128]{2,1,0:T(8,128)(2,1)S(1)} %get-tuple-element.243), channel_id=1, source_target_pairs={{0,4},{1,5},{2,6},{3,7},{4,0},{5,1},{6,2},{7,3},{8,12},{9,13},{10,... | collective-permute-start | bytes 1966088 | tf_op jit(solution)/shard_map/ppermute | solution.py:367
  79.1 16.7 %collective-permute-start.18 = (bf16[512,1792]{1,0:T(8,128)(2,1)S(1)}, bf16[512,1792]{1,0:T(8,128)(2,1)S(1)}, u32[]{:S(2)}, u32[]{:S(2)}) collective-permute-start(bf16[512,1792]{1,0:T(8,128)(2,1)S(1)} %get-tuple-element.246.pack1_ref.refs_6_), channel_id=1, source_target_pairs={{0,1},{1,0},{2,3},{3,2},{4,5},{5,4},{6,7},{7,6},{8,9},{9,8},{10,11... | collective-permute-start | bytes 5505032 | tf_op jit(solution)/shard_map/ppermute | solution.py:367
  93.4 19.0 %collective-permute-start.16 = (bf16[4,640,128]{2,1,0:T(8,128)(2,1)S(1)}, bf16[4,640,128]{2,1,0:T(8,128)(2,1)S(1)}, u32[]{:S(2)}, u32[]{:S(2)}) collective-permute-start(bf16[4,640,128]{2,1,0:T(8,128)(2,1)S(1)} %get-tuple-element.251), channel_id=1, source_target_pairs={{0,2},{1,3},{2,0},{3,1},{4,6},{5,7},{6,4},{7,5},{8,10},{9,11},{10,... | collective-permute-start | bytes 1966088 | tf_op jit(solution)/shard_map/ppermute | solution.py:367
  94.5 17.9 %collective-permute-start.17 = (bf16[4,640,128]{2,1,0:T(8,128)(2,1)S(1)}, bf16[4,640,128]{2,1,0:T(8,128)(2,1)S(1)}, u32[]{:S(2)}, u32[]{:S(2)}) collective-permute-start(bf16[4,640,128]{2,1,0:T(8,128)(2,1)S(1)} %get-tuple-element.252), channel_id=1, source_target_pairs={{0,4},{1,5},{2,6},{3,7},{4,0},{5,1},{6,2},{7,3},{8,12},{9,13},{10,... | collective-permute-start | bytes 1966088 | tf_op jit(solution)/shard_map/ppermute | solution.py:367
  97.1 19.0 %collective-permute-start.21 = (bf16[512,3840]{1,0:T(8,128)(2,1)S(1)}, bf16[512,3840]{1,0:T(8,128)(2,1)S(1)}, u32[]{:S(2)}, u32[]{:S(2)}) collective-permute-start(bf16[512,3840]{1,0:T(8,128)(2,1)S(1)} %get-tuple-element.269.refs_12_), channel_id=1, source_target_pairs={{0,1},{1,0},{2,3},{3,2},{4,5},{5,4},{6,7},{7,6},{8,9},{9,8},{10,11... | collective-permute-start | bytes 11796488 | tf_op jit(solution)/shard_map/ppermute | solution.py:367
  114.7 22.8 %collective-permute-start.19 = (bf16[4,640,128]{2,1,0:T(8,128)(2,1)}, bf16[4,640,128]{2,1,0:T(8,128)(2,1)}, u32[]{:S(2)}, u32[]{:S(2)}) collective-permute-start(bf16[4,640,128]{2,1,0:T(8,128)(2,1)} %get-tuple-element.265), channel_id=1, source_target_pairs={{0,4},{1,5},{2,6},{3,7},{4,0},{5,1},{6,2},{7,3},{8,12},{9,13},{10,... | collective-permute-start | bytes 1966088 | tf_op jit(solution)/shard_map/ppermute | solution.py:367
  114.8 22.7 %collective-permute-start.20 = (bf16[4,640,128]{2,1,0:T(8,128)(2,1)}, bf16[4,640,128]{2,1,0:T(8,128)(2,1)}, u32[]{:S(2)}, u32[]{:S(2)}) collective-permute-start(bf16[4,640,128]{2,1,0:T(8,128)(2,1)} %get-tuple-element.266), channel_id=1, source_target_pairs={{0,2},{1,3},{2,0},{3,1},{4,6},{5,7},{6,4},{7,5},{8,10},{9,11},{10,... | collective-permute-start | bytes 1966088 | tf_op jit(solution)/shard_map/ppermute | solution.py:367
  116.0 7.0 %collective-permute-start.22 = (bf16[512,3840]{1,0:T(8,128)(2,1)S(1)}, bf16[512,3840]{1,0:T(8,128)(2,1)S(1)}, u32[]{:S(2)}, u32[]{:S(2)}) collective-permute-start(bf16[512,3840]{1,0:T(8,128)(2,1)S(1)} %get-tuple-element.270.pack3_ref.refs_14_), channel_id=1, source_target_pairs={{0,1},{1,0},{2,3},{3,2},{4,5},{5,4},{6,7},{7,6},{8,9},{9,8},{10,11... | collective-permute-start | bytes 11796488 | tf_op jit(solution)/shard_map/ppermute | solution.py:367
  123.0 9.3 %collective-permute-start.23 = (bf16[512,3840]{1,0:T(8,128)(2,1)S(1)}, bf16[512,3840]{1,0:T(8,128)(2,1)S(1)}, u32[]{:S(2)}, u32[]{:S(2)}) collective-permute-start(bf16[512,3840]{1,0:T(8,128)(2,1)S(1)} %get-tuple-element.275.pack4_ref.refs_10_), channel_id=1, source_target_pairs={{0,1},{1,0},{2,3},{3,2},{4,5},{5,4},{6,7},{7,6},{8,9},{9,8},{10,11... | collective-permute-start | bytes 11796488 | tf_op jit(solution)/shard_map/ppermute | solution.py:367
  137.5 5.9 %collective-permute-start.24 = (bf16[192,2048]{1,0:T(8,128)(2,1)S(1)}, bf16[192,2048]{1,0:T(8,128)(2,1)S(1)}, u32[]{:S(2)}, u32[]{:S(2)}) collective-permute-start(bf16[192,2048]{1,0:T(8,128)(2,1)S(1)} %get-tuple-element.284.refs_2_.dkv_ref), channel_id=1, source_target_pairs={{0,1},{1,0},{2,3},{3,2},{4,5},{5,4},{6,7},{7,6},{8,9},{9,8},{10,11... | collective-permute-start | bytes 2359304 | tf_op jit(solution)/shard_map/ppermute | solution.py:367
  140.6 26.3 %collective-permute-start.28 = (bf16[2,640,128]{2,1,0:T(8,128)(2,1)}, bf16[2,640,128]{2,1,0:T(8,128)(2,1)}, u32[]{:S(2)}, u32[]{:S(2)}) collective-permute-start(bf16[2,640,128]{2,1,0:T(8,128)(2,1)} %get-tuple-element.298), channel_id=1, source_target_pairs={{0,8},{1,9},{2,10},{3,11},{4,12},{5,13},{6,14},{7,15},{8,0},{9,1},... | collective-permute-start | bytes 983048 | tf_op jit(solution)/shard_map/ppermute | solution.py:367
  142.9 3.9 %collective-permute-start.25 = (bf16[512,1024]{1,0:T(8,128)(2,1)S(1)}, bf16[512,1024]{1,0:T(8,128)(2,1)S(1)}, u32[]{:S(2)}, u32[]{:S(2)}) collective-permute-start(bf16[512,1024]{1,0:T(8,128)(2,1)S(1)} %get-tuple-element.316.refs_2_.dq_ref), channel_id=1, source_target_pairs={{0,1},{1,0},{2,3},{3,2},{4,5},{5,4},{6,7},{7,6},{8,9},{9,8},{10,11... | collective-permute-start | bytes 3145736 | tf_op jit(solution)/shard_map/ppermute | solution.py:367
  145.9 21.0 %collective-permute-start.27 = (bf16[2,1280,128]{2,1,0:T(8,128)(2,1)S(1)}, bf16[2,1280,128]{2,1,0:T(8,128)(2,1)S(1)}, u32[]{:S(2)}, u32[]{:S(2)}) collective-permute-start(bf16[2,1280,128]{2,1,0:T(8,128)(2,1)S(1)} %get-tuple-element.293), channel_id=1, source_target_pairs={{0,2},{1,3},{2,0},{3,1},{4,6},{5,7},{6,4},{7,5},{8,10},{9,11},{10,... | collective-permute-start | bytes 1966088 | tf_op jit(solution)/shard_map/ppermute | solution.py:367
  171.0 18.8 %collective-permute-start.29 = (bf16[4,768,128]{2,1,0:T(8,128)(2,1)S(1)}, bf16[4,768,128]{2,1,0:T(8,128)(2,1)S(1)}, u32[]{:S(2)}, u32[]{:S(2)}) collective-permute-start(bf16[4,768,128]{2,1,0:T(8,128)(2,1)S(1)} %get-tuple-element.311), channel_id=1, source_target_pairs={{0,2},{1,3},{2,0},{3,1},{4,6},{5,7},{6,4},{7,5},{8,10},{9,11},{10,... | collective-permute-start | bytes 2359304 | tf_op jit(solution)/shard_map/ppermute | solution.py:367
  171.9 8.6 %collective-permute-start.32 = (f32[3,1792]{1,0:T(4,128)S(1)}, f32[3,1792]{1,0:T(4,128)S(1)}, u32[]{:S(2)}, u32[]{:S(2)}) collective-permute-start(f32[3,1792]{1,0:T(4,128)S(1)} %copy-done.72), channel_id=1, source_target_pairs={{0,8},{1,9},{2,10},{3,11},{4,12},{5,13},{6,14},{7,15},{8,0},{9,1},... | collective-permute-start | bytes 64520 | tf_op jit(solution)/shard_map/ppermute | solution.py:367
  172.1 16.2 %collective-permute-start.30 = (bf16[1,1280,128]{2,1,0:T(8,128)(2,1)S(1)}, bf16[1,1280,128]{2,1,0:T(8,128)(2,1)S(1)}, u32[]{:S(2)}, u32[]{:S(2)}) collective-permute-start(bf16[1,1280,128]{2,1,0:T(8,128)(2,1)S(1)} %get-tuple-element.312), channel_id=1, source_target_pairs={{0,4},{1,5},{2,6},{3,7},{4,0},{5,1},{6,2},{7,3},{8,12},{9,13},{10,... | collective-permute-start | bytes 983048 | tf_op jit(solution)/shard_map/ppermute | solution.py:367
  173.0 15.2 %collective-permute-start.31 = (bf16[2,640,128]{2,1,0:T(8,128)(2,1)S(1)}, bf16[2,640,128]{2,1,0:T(8,128)(2,1)S(1)}, u32[]{:S(2)}, u32[]{:S(2)}) collective-permute-start(bf16[2,640,128]{2,1,0:T(8,128)(2,1)S(1)} %get-tuple-element.313), channel_id=1, source_target_pairs={{0,8},{1,9},{2,10},{3,11},{4,12},{5,13},{6,14},{7,15},{8,0},{9,1},... | collective-permute-start | bytes 983048 | tf_op jit(solution)/shard_map/ppermute | solution.py:367
  190.6 16.2 %collective-permute-start.33 = (bf16[2,768,128]{2,1,0:T(8,128)(2,1)S(1)}, bf16[2,768,128]{2,1,0:T(8,128)(2,1)S(1)}, u32[]{:S(2)}, u32[]{:S(2)}) collective-permute-start(bf16[2,768,128]{2,1,0:T(8,128)(2,1)S(1)} %get-tuple-element.337), channel_id=1, source_target_pairs={{0,4},{1,5},{2,6},{3,7},{4,0},{5,1},{6,2},{7,3},{8,12},{9,13},{10,... | collective-permute-start | bytes 1179656 | tf_op jit(solution)/shard_map/ppermute | solution.py:367
  191.9 16.8 %collective-permute-start.34 = (bf16[4,736,128]{2,1,0:T(8,128)(2,1)S(1)}, bf16[4,736,128]{2,1,0:T(8,128)(2,1)S(1)}, u32[]{:S(2)}, u32[]{:S(2)}) collective-permute-start(bf16[4,736,128]{2,1,0:T(8,128)(2,1)S(1)} %get-tuple-element.338), channel_id=1, source_target_pairs={{0,2},{1,3},{2,0},{3,1},{4,6},{5,7},{6,4},{7,5},{8,10},{9,11},{10,... | collective-permute-start | bytes 2261000 | tf_op jit(solution)/shard_map/ppermute | solution.py:367
  192.2 14.5 %collective-permute-start.35 = (bf16[1,1280,128]{2,1,0:T(8,128)(2,1)S(1)}, bf16[1,1280,128]{2,1,0:T(8,128)(2,1)S(1)}, u32[]{:S(2)}, u32[]{:S(2)}) collective-permute-start(bf16[1,1280,128]{2,1,0:T(8,128)(2,1)S(1)} %add_convert_fusion.1), channel_id=1, source_target_pairs={{0,8},{1,9},{10,2},{11,3},{12,4},{13,5},{14,6},{15,7},{16,24},{17,... | collective-permute-start | bytes 983048 | tf_op jit(solution)/shard_map/ppermute | solution.py:1370
  194.2 12.5 %collective-permute-start.36 = (f32[3,1792]{1,0:T(4,128)S(1)}, f32[3,1792]{1,0:T(4,128)S(1)}, u32[]{:S(2)}, u32[]{:S(2)}) collective-permute-start(f32[3,1792]{1,0:T(4,128)S(1)} %add.60), channel_id=1, source_target_pairs={{0,4},{1,5},{2,6},{3,7},{4,0},{5,1},{6,2},{7,3},{8,12},{9,13},{10,... | collective-permute-start | bytes 64520 | tf_op jit(solution)/shard_map/ppermute | solution.py:367
  208.8 18.1 %collective-permute-start.40 = (bf16[1,1280,128]{2,1,0:T(8,128)(2,1)S(1)}, bf16[1,1280,128]{2,1,0:T(8,128)(2,1)S(1)}, u32[]{:S(2)}, u32[]{:S(2)}) collective-permute-start(bf16[1,1280,128]{2,1,0:T(8,128)(2,1)S(1)} %add_convert_fusion), channel_id=1, source_target_pairs={{16,0},{17,1},{18,2},{19,3},{20,4},{21,5},{22,6},{23,7},{24,8},{25... | collective-permute-start | bytes 983048 | tf_op jit(solution)/shard_map/ppermute | solution.py:1372
  210.8 16.1 %collective-permute-start.38 = (bf16[2,736,128]{2,1,0:T(8,128)(2,1)S(1)}, bf16[2,736,128]{2,1,0:T(8,128)(2,1)S(1)}, u32[]{:S(2)}, u32[]{:S(2)}) collective-permute-start(bf16[2,736,128]{2,1,0:T(8,128)(2,1)S(1)} %get-tuple-element.348), channel_id=1, source_target_pairs={{0,4},{1,5},{2,6},{3,7},{4,0},{5,1},{6,2},{7,3},{8,12},{9,13},{10,... | collective-permute-start | bytes 1130504 | tf_op jit(solution)/shard_map/ppermute | solution.py:367
  211.2 15.8 %collective-permute-start.39 = (bf16[4,608,128]{2,1,0:T(8,128)(2,1)S(1)}, bf16[4,608,128]{2,1,0:T(8,128)(2,1)S(1)}, u32[]{:S(2)}, u32[]{:S(2)}) collective-permute-start(bf16[4,608,128]{2,1,0:T(8,128)(2,1)S(1)} %get-tuple-element.349), channel_id=1, source_target_pairs={{0,2},{1,3},{2,0},{3,1},{4,6},{5,7},{6,4},{7,5},{8,10},{9,11},{10,... | collective-permute-start | bytes 1867784 | tf_op jit(solution)/shard_map/ppermute | solution.py:367
  214.5 12.5 %collective-permute-start.37 = (bf16[1,768,128]{2,1,0:T(8,128)(2,1)S(1)}, bf16[1,768,128]{2,1,0:T(8,128)(2,1)S(1)}, u32[]{:S(2)}, u32[]{:S(2)}) collective-permute-start(bf16[1,768,128]{2,1,0:T(8,128)(2,1)S(1)} %get-tuple-element.345), channel_id=1, source_target_pairs={{0,8},{1,9},{2,10},{3,11},{4,12},{5,13},{6,14},{7,15},{8,0},{9,1},... | collective-permute-start | bytes 589832 | tf_op jit(solution)/shard_map/ppermute | solution.py:367
  214.5 12.4 %collective-permute-start.41 = (f32[3,1792]{1,0:T(4,128)S(1)}, f32[3,1792]{1,0:T(4,128)S(1)}, u32[]{:S(2)}, u32[]{:S(2)}) collective-permute-start(f32[3,1792]{1,0:T(4,128)S(1)} %add.62), channel_id=1, source_target_pairs={{0,2},{1,3},{2,0},{3,1},{4,6},{5,7},{6,4},{7,5},{8,10},{9,11},{10,... | collective-permute-start | bytes 64520 | tf_op jit(solution)/shard_map/ppermute | solution.py:367
  227.7 12.8 %collective-permute-start.43 = (bf16[2,608,128]{2,1,0:T(8,128)(2,1)S(1)}, bf16[2,608,128]{2,1,0:T(8,128)(2,1)S(1)}, u32[]{:S(2)}, u32[]{:S(2)}) collective-permute-start(bf16[2,608,128]{2,1,0:T(8,128)(2,1)S(1)} %get-tuple-element.360), channel_id=1, source_target_pairs={{0,4},{1,5},{2,6},{3,7},{4,0},{5,1},{6,2},{7,3},{8,12},{9,13},{10,... | collective-permute-start | bytes 933896 | tf_op jit(solution)/shard_map/ppermute | solution.py:367
  228.8 11.6 %collective-permute-start.44 = (bf16[4,384,128]{2,1,0:T(8,128)(2,1)S(1)}, bf16[4,384,128]{2,1,0:T(8,128)(2,1)S(1)}, u32[]{:S(2)}, u32[]{:S(2)}) collective-permute-start(bf16[4,384,128]{2,1,0:T(8,128)(2,1)S(1)} %get-tuple-element.361), channel_id=1, source_target_pairs={{0,2},{1,3},{2,0},{3,1},{4,6},{5,7},{6,4},{7,5},{8,10},{9,11},{10,... | collective-permute-start | bytes 1179656 | tf_op jit(solution)/shard_map/ppermute | solution.py:367
  230.7 9.8 %collective-permute-start.42 = (bf16[1,736,128]{2,1,0:T(8,128)(2,1)S(1)}, bf16[1,736,128]{2,1,0:T(8,128)(2,1)S(1)}, u32[]{:S(2)}, u32[]{:S(2)}) collective-permute-start(bf16[1,736,128]{2,1,0:T(8,128)(2,1)S(1)} %get-tuple-element.357), channel_id=1, source_target_pairs={{0,8},{1,9},{2,10},{3,11},{4,12},{5,13},{6,14},{7,15},{8,0},{9,1},... | collective-permute-start | bytes 565256 | tf_op jit(solution)/shard_map/ppermute | solution.py:367
  230.7 4.6 %collective-permute-start.45 = (f32[3,1792]{1,0:T(4,128)S(1)}, f32[3,1792]{1,0:T(4,128)S(1)}, u32[]{:S(2)}, u32[]{:S(2)}) collective-permute-start(f32[3,1792]{1,0:T(4,128)S(1)} %add.64), channel_id=1, source_target_pairs={{0,1},{1,0},{2,3},{3,2},{4,5},{5,4},{6,7},{7,6},{8,9},{9,8},{10,11... | collective-permute-start | bytes 64520 | tf_op jit(solution)/shard_map/ppermute | solution.py:367
  241.1 6.8 %collective-permute-start.47 = (bf16[2,384,128]{2,1,0:T(8,128)(2,1)S(1)}, bf16[2,384,128]{2,1,0:T(8,128)(2,1)S(1)}, u32[]{:S(2)}, u32[]{:S(2)}) collective-permute-start(bf16[2,384,128]{2,1,0:T(8,128)(2,1)S(1)} %get-tuple-element.370), channel_id=1, source_target_pairs={{0,4},{1,5},{2,6},{3,7},{4,0},{5,1},{6,2},{7,3},{8,12},{9,13},{10,... | collective-permute-start | bytes 589832 | tf_op jit(solution)/shard_map/ppermute | solution.py:367
  241.8 6.0 %collective-permute-start.46 = (bf16[1,608,128]{2,1,0:T(8,128)(2,1)S(1)}, bf16[1,608,128]{2,1,0:T(8,128)(2,1)S(1)}, u32[]{:S(2)}, u32[]{:S(2)}) collective-permute-start(bf16[1,608,128]{2,1,0:T(8,128)(2,1)S(1)} %get-tuple-element.367), channel_id=1, source_target_pairs={{0,8},{1,9},{2,10},{3,11},{4,12},{5,13},{6,14},{7,15},{8,0},{9,1},... | collective-permute-start | bytes 466952 | tf_op jit(solution)/shard_map/ppermute | solution.py:367
  248.5 4.6 %collective-permute-start.48 = (bf16[1,384,128]{2,1,0:T(8,128)(2,1)S(1)}, bf16[1,384,128]{2,1,0:T(8,128)(2,1)S(1)}, u32[]{:S(2)}, u32[]{:S(2)}) collective-permute-start(bf16[1,384,128]{2,1,0:T(8,128)(2,1)S(1)} %get-tuple-element.375), channel_id=1, source_target_pairs={{0,8},{1,9},{2,10},{3,11},{4,12},{5,13},{6,14},{7,15},{8,0},{9,1},... | collective-permute-start | bytes 294920 | tf_op jit(solution)/shard_map/ppermute | solution.py:367
  255.3 9.5 %collective-permute-start.49 = (f32[2528,128]{1,0:T(8,128)S(1)}, f32[2528,128]{1,0:T(8,128)S(1)}, u32[]{:S(2)}, u32[]{:S(2)}) collective-permute-start(f32[2528,128]{1,0:T(8,128)S(1)} %get-tuple-element.378), channel_id=1, source_target_pairs={{0,1},{1,0},{2,3},{3,2},{4,5},{5,4},{6,7},{7,6},{8,9},{9,8},{10,11... | collective-permute-start | bytes 3883016 | tf_op jit(solution)/shard_map/ppermute | solution.py:367
  (96 other events, 955.1 us)

commit v3 on v2

--- a/solution.py
+++ b/solution.py
@@ -70,7 +70,7 @@
     else:
         masks = [keys < fixed] * pairs
 
-    @pl.loop(0, blocks)
+    @pl.loop(0, blocks, unroll=4 if blocks % 4 == 0 else 3)
     def _(j):
         scores = []
         for p in range(pairs):
@@ -149,7 +149,7 @@
     else:
         masks = [keys < fixed] * pairs
 
-    @pl.loop(0, blocks)
+    @pl.loop(0, blocks, unroll=4 if blocks % 4 == 0 else 3)
     def _(j):
         scores, slopes = [], []
         for p in range(pairs):
@@ -738,12 +738,16 @@
 
 
 def self_kernel(
-    lens_ref, r_ref, n2_ref, g_ref, wout_ref, cot_ref,
+    lens_ref, r_ref, n2_ref, g_ref, wout_ref, cot_ref, far_cot_ref,
     pack_ref, y_ref, de_ref, dg_ref, a_ref, dz_ref,
     *, pairs, heads_in, fixed, scaling,
 ):
     rows, width = n2_ref.shape
     z_ref, de_low_ref, dr_ref = views(pack_ref, width, width, 3 * width)
+    near = cot_ref.shape[0]
+    dz_ref[:near, :] = cot_ref[...]
+    if near < rows:
+        dz_ref[near:, :] = far_cot_ref[...]
     blocks = width // LANES
     cols = (0, blocks, 2 * blocks)
     shared = dict(
@@ -756,7 +760,7 @@
     def last(start, at, size):
         n, inverse = normed_chunk(a_ref[at, :])
         y = n * g_ref[2:3, :]
-        grad = cot_ref[at, :].astype(F32)
+        grad = dz_ref[at, :].astype(F32)
         if fixed is None:
             slots = rows // pairs
             place = lax.broadcasted_iota(jnp.int32, (size, 1), 0) + lax.rem(start, slots)
@@ -894,14 +898,14 @@
     )
 
 
-def self_turn(lens, r, n2, gains, output_w, cot, pairs, heads, fixed):
+def self_turn(lens, r, n2, gains, output_w, cots, pairs, heads, fixed):
     rows, width = n2.shape
     size = width // heads
     return fused(
         functools.partial(
             self_kernel, pairs=pairs, heads_in=LANES // size, fixed=fixed, scaling=size ** (-0.5)
         ),
-        (lens, r, n2, gains, output_w, cot),
+        (lens, r, n2, gains, output_w, *cots),
         [
             ((rows, 5 * width), BF16),
             ((rows, width), BF16),
@@ -1008,7 +1012,9 @@
     pack2, slope, n2, inv2, r = mlp_forward(pack1, n1, gains, up_w, down_w, qkv_w)
     r, pack2 = tied(moves.settle(hook("mlp", r)), pack2)
     moves.send(pack2=pack2)
-    pack3, result, de, dg2 = self_turn(lens, r, n2, gains, output_w, cot, pairs, heads, fixed)
+    near_cot, far_cot = cot
+    cots = (near_cot, far_cot[0] if far_cot else near_cot)
+    pack3, result, de, dg2 = self_turn(lens, r, n2, gains, output_w, cots, pairs, heads, fixed)
     pack3 = moves.settle(hook("self", pack3))
     moves.send(pack3=pack3)
     pack4, db, dg1 = mlp_back(pack3, de, n2, inv2, gains, slope, qkv_w, down_w)
@@ -1133,7 +1139,7 @@
         image_all,
         image_q,
         text_all,
-        image_cot,
+        (image_cot, None),
         (text_keyval, image_attend, image_up, image_down, image_qkv, image_output),
         image_gains,
         H_I,
@@ -1197,7 +1203,7 @@
         text_all,
         image_kv,
         text_all,
-        jnp.concatenate([text_cotangent, cots[0]]),
+        (text_cotangent, cots),
         (text_query, text_attend, text_up, text_down, text_qkv, text_output),
         text_gains,
         H_T,

time: 270 us -> 261 us (0.967)
  starting transfers between devices: 51.3 us -> 56.6 us
  Pallas kernels: 131 us -> 126 us
  local copies, waits for them, and re-layouts: 15.7 us -> 11.1 us
  waiting for transfers between devices: 57 us -> 54.1 us
    unnamed x188 -> x184, local copies, waits for them, and re-layouts: 14.4 us -> 9.75 us
    ppermute x43, starting transfers between devices: 44.9 us -> 48.8 us  [dp_swap(): return lax.ppermute(block, 'dp', [(i, i ^ bit) for i in range(count)])]
    pallas_call x10, Pallas kernels: 73.2 us -> 69.8 us  [fused(): pl.pallas_call(kernel, in_specs=in_specs, out_specs=[vmem] * len(outs), o...]
    ppermute x43, waiting for transfers between devices: 53.3 us -> 50.5 us  [dp_swap(): return lax.ppermute(block, 'dp', [(i, i ^ bit) for i in range(count)])]
  transfers between devices with their start and end apart: 50 -> 50, of which waited for: 15 -> 14; matrix products, arithmetic and copies ran while one was open for 4% -> 4% of each run, Pallas kernels for 46% -> 45%
where the time goes in v3:
time: 261 us; the launch traced here: 258 us
  Pallas kernels  126 us (48%)
  starting transfers between devices  56.6 us (22%)
  waiting for transfers between devices  54.1 us (21%)
  local copies, waits for them, and re-layouts  11.1 us (4%)
  matrix products  5.8 us (2%)
    pallas_call x10, Pallas kernels, fused(): pl.pallas_call(kernel, in_specs=in_specs, out_specs=[vmem] * len(outs), o...  69.8 us
    ppermute x43, waiting for transfers between devices, dp_swap(): return lax.ppermute(block, 'dp', [(i, i ^ bit) for i in range(count)])  50.5 us
    ppermute x43, starting transfers between devices, dp_swap(): return lax.ppermute(block, 'dp', [(i, i ^ bit) for i in range(count)])  48.8 us
    pallas_call x3, Pallas kernels, flat_grads(): pl.pallas_call(functools.partial(flat_kernel, plans=plans, found=found, q...  24.8 us
    pallas_call x11, Pallas kernels, add_split(): pl.pallas_call(functools.partial(add_split_kernel, plan=tuple(plan), inpu...  10.6 us
    unnamed x184, local copies, waits for them, and re-layouts  9.75 us
    pallas_call x2, Pallas kernels, attend_back(): pl.pallas_call(functools.partial(body, pairs=pairs, blocks=blocks, cols=c...  8.42 us
    dot_general x6, matrix products, mm(): return jnp.dot(a, b, preferred_element_type=F32)  5.8 us
  transfers between devices with their start and end apart: 50, of which 14 were waited for; matrix products, arithmetic and copies ran while one was open for 4% of the time, Pallas kernels for 45%

profile of v3, /device:TPU:3, one launch (start us, length us, event | category | flops | bytes accessed | tf_op | source)
XLA Modules:
  0.0 257.8 jit_solution(558879311945986193)
XLA Ops:
  0.7 1.5 collective-permute-start
  2.4 1.3 fusion.9
  3.9 1.8 collective-permute-done.2
  6.1 2.8 %collective-permute-start.3 = (bf16[192,1024]{1,0:T(8,128)(2,1)S(1)}, bf16[192,1024]{1,0:T(8,128)(2,1)S(1)}, u32[]{:S(2)}, u32[]{:S(2)}) collective-permute-start(bf16[192,1024]{1,0:T(8,128)(2,1)S(1)} %fusion.x_ref.refs_0_), channel_id=1, source_target_pairs={{0,1},{1,0},{2,3},{3,2},{4,5},{5,4},{6,7},{7,6},{8,9},{9,8},{10,11... | collective-permute-start | bytes 1179656 | tf_op jit(solution)/shard_map/ppermute | solution.py:367
  8.8 2.2 convolution_convert_fusion.1.given_ref.refs_0_
  12.2 1.9 collective-permute-done.1
  16.6 2.2 collective-permute-start.12
  18.8 7.8 %co_forward.3 = (bf16[512,2048]{1,0:T(8,128)(2,1)S(1)}, bf16[192,2048]{1,0:T(8,128)(2,1)S(1)}, f32[192,1024]{1,0:T(8,128)S(1)}, f32[192,128]{1,0:T(8,128)S(1)}) custom-call(s32[4]{0:T(128)S(1)} %pad_add_fusion.1.lens_ref, bf16[192,1024]{1,0:T(8,128)(2,1)S(1)} %fusion.x_ref.refs_0_, bf16[192,1024]{1,0:T(8,128)(2,1)S(1)} %convolution_convert_fusion.1.given_ref.refs_0_, ...), custom_call_target="tpu_custom_call" | custom-call | flops 70000001024 | bytes 1000 | tf_op jit(solution)/shard_map/co_forward/pallas_call | solution.py:845
  28.7 3.7 %mlp_forward.2 = (bf16[192,2048]{1,0:T(8,128)(2,1)S(1)}, bf16[192,1024]{1,0:T(8,128)(2,1)S(1)}, f32[192,1024]{1,0:T(8,128)S(1)}, f32[192,128]{1,0:T(8,128)S(1)}, bf16[192,3072]{1,0:T(8,128)(2,1)S(1)}) custom-call(bf16[192,2048]{1,0:T(8,128)(2,1)S(1)} %get-tuple-element.204.pack1_ref.refs_4_, f32[192,1024]{1,0:T(8,128)S(1)} %get-tuple-element.205.n1_ref, ...), custom_call_target="tpu_custom_call" | custom-call | flops 48000000000 | bytes 1000 | tf_op jit(solution)/shard_map/mlp_forward/pallas_call | solution.py:845
  33.0 8.9 %self_turn.2 = (bf16[192,5120]{1,0:T(8,128)(2,1)S(1)}, bf16[192,1024]{1,0:T(8,128)(2,1)S(1)}, f32[192,1024]{1,0:T(8,128)S(1)}, f32[1,1024]{1,0:T(1,128)S(1)}) custom-call(s32[4]{0:T(128)S(1)} %pad_add_fusion.1.lens_ref, bf16[192,3072]{1,0:T(8,128)(2,1)S(1)} %get-tuple-element.209.r_ref, f32[192,1024]{1,0:T(8,128)S(1)} %get-tuple-element.210.n2_ref, ...), custom_call_target="tpu_custom_call" | custom-call | flops 105000001536 | bytes 1000 | tf_op jit(solution)/shard_map/self_turn/pallas_call | solution.py:845
  42.5 3.6 %mlp_back.2 = (bf16[192,2048]{1,0:T(8,128)(2,1)S(1)}, f32[192,1024]{1,0:T(8,128)S(1)}, f32[1,1024]{1,0:T(1,128)S(1)}) custom-call(bf16[192,5120]{1,0:T(8,128)(2,1)S(1)} %get-tuple-element.216.pack3_ref.refs_12_, f32[192,1024]{1,0:T(8,128)S(1)} %get-tuple-element.217.de_ref, f32[192,1024]{1,0:T(8,128)S(1)} %get-tuple-element.210.n2_ref, ...), custom_call_target="tpu_custom_call" | custom-call | flops 27428571136 | bytes 1000 | tf_op jit(solution)/shard_map/mlp_back/pallas_call | solution.py:845
  46.5 2.2 context_back.2
  49.0 4.4 %attend_back.2 = (bf16[192,1024]{1,0:T(8,128)(2,1)S(1)}, bf16[512,2048]{1,0:T(8,128)(2,1)S(1)}) custom-call(s32[4]{0:T(128)S(1)} %pad_add_fusion.1.lens_ref, bf16[192,1024]{1,0:T(8,128)(2,1)S(1)} %copy-done.19, bf16[512,2048]{1,0:T(8,128)(2,1)S(1)} %get-tuple-element.203.refs_1_, bf16[192,1024]{1,0:T(8,128)(2,1)S(1)} %get-tuple-element.225.refs_2_), custom_call_target="tpu_custom_call" | custom-call | flops 60000002048 | bytes 1000 | tf_op jit(solution)/shard_map/attend_back/pallas_call | solution.py:213
  53.9 8.5 %co_forward.2 = (bf16[512,1024]{1,0:T(8,128)(2,1)S(1)}, bf16[512,1792]{1,0:T(8,128)(2,1)S(1)}, f32[512,768]{1,0:T(8,128)S(1)}, f32[512,128]{1,0:T(8,128)S(1)}) custom-call(s32[4]{0:T(128)S(1)} %pad_add_fusion.1.lens_ref, bf16[512,768]{1,0:T(8,128)(2,1)} %pad_maximum_fusion.x_ref.source_ref.refs_0_, ...), custom_call_target="tpu_custom_call" | custom-call | flops 70000001024 | bytes 1000 | tf_op jit(solution)/shard_map/co_forward/pallas_call | solution.py:845
  62.8 5.8 %flat_grads.3.flat_ref = bf16[20480,128]{1,0:T(8,128)(2,1)S(1)} custom-call(s32[2]{0:T(128)S(1)} %pad_add_fusion.side_ref, bf16[192,1024]{1,0:T(8,128)(2,1)S(1)} %copy-done.4, bf16[192,1024]{1,0:T(8,128)(2,1)S(1)} %copy-done.54, bf16[192,1024]{1,0:T(8,128)(2,1)S(1)} %get-tuple-element.321.refs_2_.dq_ref, ...), custom_call_target="tpu_custom_call" | custom-call | flops 60000002048 | bytes 1000 | tf_op jit(solution)/shard_map/flat_grads/pallas_call | solution.py:350
  73.9 11.1 %mlp_forward.3 = (bf16[512,3840]{1,0:T(8,128)(2,1)S(1)}, bf16[512,3072]{1,0:T(8,128)(2,1)S(1)}, f32[512,768]{1,0:T(8,128)S(1)}, f32[512,128]{1,0:T(8,128)S(1)}, bf16[512,2304]{1,0:T(8,128)(2,1)S(1)}) custom-call(bf16[512,1792]{1,0:T(8,128)(2,1)S(1)} %get-tuple-element.246.pack1_ref.refs_6_, f32[512,768]{1,0:T(8,128)S(1)} %get-tuple-element.247.n1_ref, ...), custom_call_target="tpu_custom_call" | custom-call | flops 128000000000 | bytes 1000 | tf_op jit(solution)/shard_map/mlp_forward/pallas_call | solution.py:845
  85.0 1.7 copy-done.64
  86.8 1.6 collective-permute-start.16
  91.8 11.8 %self_turn.3 = (bf16[512,3840]{1,0:T(8,128)(2,1)S(1)}, bf16[512,768]{1,0:T(8,128)(2,1)S(1)}, f32[512,768]{1,0:T(8,128)S(1)}, f32[1,768]{1,0:T(1,128)S(1)}) custom-call(s32[4]{0:T(128)S(1)} %copy-done.61, bf16[512,2304]{1,0:T(8,128)(2,1)S(1)} %get-tuple-element.256.r_ref, f32[512,768]{1,0:T(8,128)S(1)} %get-tuple-element.257.n2_ref, f32[3,768]{1,0:T(4,128)S(1)} %copy-done.57, ...), custom_call_target="tpu_custom_call" | custom-call | flops 130000003072 | bytes 1000 | tf_op jit(solution)/shard_map/self_turn/pallas_call | solution.py:845
  104.0 2.2 add_split.11
  107.8 2.0 collective-permute-start.22
  109.8 6.2 %mlp_back.3 = (bf16[512,3840]{1,0:T(8,128)(2,1)S(1)}, f32[512,768]{1,0:T(8,128)S(1)}, f32[1,768]{1,0:T(1,128)S(1)}) custom-call(bf16[512,3840]{1,0:T(8,128)(2,1)S(1)} %get-tuple-element.270.pack3_ref.refs_14_, f32[512,768]{1,0:T(8,128)S(1)} %get-tuple-element.271.de_ref, f32[512,768]{1,0:T(8,128)S(1)} %get-tuple-element.257.n2_ref, ...), custom_call_target="tpu_custom_call" | custom-call | flops 73142853632 | bytes 1000 | tf_op jit(solution)/shard_map/mlp_back/pallas_call | solution.py:845
  116.1 1.8 collective-permute-start.23
  118.0 6.2 %context_back.3 = (bf16[512,768]{1,0:T(8,128)(2,1)S(1)}, f32[512,768]{1,0:T(8,128)S(1)}, bf16[512,1024]{1,0:T(8,128)(2,1)S(1)}, f32[1,768]{1,0:T(1,128)S(1)}) custom-call(bf16[512,3840]{1,0:T(8,128)(2,1)S(1)} %get-tuple-element.275.pack4_ref.refs_10_, f32[512,768]{1,0:T(8,128)S(1)} %get-tuple-element.276.db_ref, f32[512,768]{1,0:T(8,128)S(1)} %copy-done.67, ...), custom_call_target="tpu_custom_call" | custom-call | flops 64000000000 | bytes 1000 | tf_op jit(solution)/shard_map/context_back/pallas_call | solution.py:845
  124.9 4.0 %attend_back.3 = (bf16[512,1024]{1,0:T(8,128)(2,1)S(1)}, bf16[192,2048]{1,0:T(8,128)(2,1)S(1)}) custom-call(s32[4]{0:T(128)S(1)} %copy-done.62, bf16[512,1024]{1,0:T(8,128)(2,1)S(1)} %get-tuple-element.267.refs_0_, bf16[192,2048]{1,0:T(8,128)(2,1)S(1)} %copy-done.15, bf16[512,1024]{1,0:T(8,128)(2,1)S(1)} %get-tuple-element.279.refs_2_), custom_call_target="tpu_custom_call" | custom-call | flops 60000002048 | bytes 1000 | tf_op jit(solution)/shard_map/attend_back/pallas_call | solution.py:213
  129.0 2.4 add_split.12
  131.4 2.3 collective-permute-start.28
  134.4 1.7 flat_grads.4.flat_ref
  140.6 17.3 %flat_grads.5.flat_ref = bf16[19968,128]{1,0:T(8,128)(2,1)} custom-call(s32[2]{0:T(128)S(1)} %copy-done.59, bf16[512,768]{1,0:T(8,128)(2,1)} %pad_maximum_fusion.x_ref.source_ref.refs_0_, bf16[512,768]{1,0:T(8,128)(2,1)} %collective-permute-done.12.refs_1_, bf16[512,1024]{1,0:T(8,128)(2,1)S(1)} %get-tuple-element.316.refs_2_.dq_ref, ...), custom_call_target="tpu_custom_call" | custom-call | flops 140000002048 | bytes 1000 | tf_op jit(solution)/shard_map/flat_grads/pallas_call | solution.py:350
  157.9 2.4 copy-done.63
  163.9 2.3 collective-permute-start.31
  166.3 2.9 %input_grads.3 = (bf16[72,1024]{1,0:T(8,128)(2,1)}, bf16[72,1024]{1,0:T(8,128)(2,1)}) custom-call(f32[192,1024]{1,0:T(8,128)S(1)} %get-tuple-element.320.da_ref, bf16[192,1024]{1,0:T(8,128)(2,1)S(1)} %copy-done.17, bf16[192,2048]{1,0:T(8,128)(2,1)S(1)} %copy-done.13, bf16[192,1024]{1,0:T(8,128)(2,1)S(1)} %get-tuple-element.322.y_ref, ...), custom_call_target="tpu_custom_call" | custom-call | flops 2000000000 | bytes 1000 | tf_op jit(solution)/shard_map/input_grads/pallas_call | solution.py:937
  169.2 2.3 input_grads.2
  171.5 8.5 %collective-permute-done.30 = bf16[1,1280,128]{2,1,0:T(8,128)(2,1)S(1)} collective-permute-done((bf16[1,1280,128]{2,1,0:T(8,128)(2,1)S(1)}, bf16[1,1280,128]{2,1,0:T(8,128)(2,1)S(1)}, u32[]{:S(2)}, u32[]{:S(2)}) %collective-permute-start.30) | collective-permute-done | bytes 327712 | tf_op jit(solution)/shard_map/ppermute | solution.py:367
  183.1 3.4 %collective-permute-start.35 = (bf16[1,1280,128]{2,1,0:T(8,128)(2,1)S(1)}, bf16[1,1280,128]{2,1,0:T(8,128)(2,1)S(1)}, u32[]{:S(2)}, u32[]{:S(2)}) collective-permute-start(bf16[1,1280,128]{2,1,0:T(8,128)(2,1)S(1)} %add_convert_fusion.1), channel_id=1, source_target_pairs={{0,8},{1,9},{10,2},{11,3},{12,4},{13,5},{14,6},{15,7},{16,24},{17,... | collective-permute-start | bytes 983048 | tf_op jit(solution)/shard_map/ppermute | solution.py:1376
  186.6 10.2 %collective-permute-done.36 = f32[3,1792]{1,0:T(4,128)S(1)} collective-permute-done((f32[3,1792]{1,0:T(4,128)S(1)}, f32[3,1792]{1,0:T(4,128)S(1)}, u32[]{:S(2)}, u32[]{:S(2)}) %collective-permute-start.36) | collective-permute-done | bytes 21536 | tf_op jit(solution)/shard_map/ppermute | solution.py:367
  196.9 2.0 collective-permute-done.34.refs_1_
  202.0 1.6 collective-permute-start.39
  204.9 10.7 %collective-permute-done.41 = f32[3,1792]{1,0:T(4,128)S(1)} collective-permute-done((f32[3,1792]{1,0:T(4,128)S(1)}, f32[3,1792]{1,0:T(4,128)S(1)}, u32[]{:S(2)}, u32[]{:S(2)}) %collective-permute-start.41) | collective-permute-done | bytes 21536 | tf_op jit(solution)/shard_map/ppermute | solution.py:367
  216.4 1.4 collective-permute-start.43
  219.6 4.6 %collective-permute-start.45 = (f32[3,1792]{1,0:T(4,128)S(1)}, f32[3,1792]{1,0:T(4,128)S(1)}, u32[]{:S(2)}, u32[]{:S(2)}) collective-permute-start(f32[3,1792]{1,0:T(4,128)S(1)} %add.64), channel_id=1, source_target_pairs={{0,1},{1,0},{2,3},{3,2},{4,5},{5,4},{6,7},{7,6},{8,9},{9,8},{10,11... | collective-permute-start | bytes 64520 | tf_op jit(solution)/shard_map/ppermute | solution.py:367
  225.1 1.9 collective-permute-done.42.refs_7_
  229.2 6.2 %collective-permute-done.46.refs_9_ = bf16[1,608,128]{2,1,0:T(8,128)(2,1)S(1)} collective-permute-done((bf16[1,608,128]{2,1,0:T(8,128)(2,1)S(1)}, bf16[1,608,128]{2,1,0:T(8,128)(2,1)S(1)}, u32[]{:S(2)}, u32[]{:S(2)}) %collective-permute-start.46) | collective-permute-done | bytes 155680 | tf_op jit(solution)/shard_map/ppermute | solution.py:367
  236.3 7.2 %collective-permute-done.48.refs_11_ = bf16[1,384,128]{2,1,0:T(8,128)(2,1)S(1)} collective-permute-done((bf16[1,384,128]{2,1,0:T(8,128)(2,1)S(1)}, bf16[1,384,128]{2,1,0:T(8,128)(2,1)S(1)}, u32[]{:S(2)}, u32[]{:S(2)}) %collective-permute-start.48) | collective-permute-done | bytes 98336 | tf_op jit(solution)/shard_map/ppermute | solution.py:367
  243.5 2.3 finish.1
  245.8 6.9 %collective-permute-start.49 = (f32[2528,128]{1,0:T(8,128)S(1)}, f32[2528,128]{1,0:T(8,128)S(1)}, u32[]{:S(2)}, u32[]{:S(2)}) collective-permute-start(f32[2528,128]{1,0:T(8,128)S(1)} %get-tuple-element.378), channel_id=1, source_target_pairs={{0,1},{1,0},{2,3},{3,2},{4,5},{5,4},{6,7},{7,6},{8,9},{9,8},{10,11... | collective-permute-start | bytes 3883016 | tf_op jit(solution)/shard_map/ppermute | solution.py:367
  253.9 1.4 collective-permute-done.49.far_ref
  255.3 2.2 join.1
  (297 shorter events, 44.6 us)
Async XLA Ops:
  0.6 5.0 %collective-permute-start.2 = (bf16[72,1024]{1,0:T(8,128)(2,1)}, bf16[72,1024]{1,0:T(8,128)(2,1)S(1)}, u32[]{:S(2)}, u32[]{:S(2)}) collective-permute-start(bf16[72,1024]{1,0:T(8,128)(2,1)} %param.22), channel_id=1, source_target_pairs={{0,16},{16,0},{1,17},{17,1},{2,18},{18,2},{3,19},{19,3},{4,20},{20... | collective-permute-start | bytes 442376 | tf_op jit(solution)/shard_map/ppermute | solution.py:371
  0.7 13.3 %collective-permute-start = (bf16[256,768]{1,0:T(8,128)(2,1)}, bf16[256,768]{1,0:T(8,128)(2,1)S(1)}, u32[]{:S(2)}, u32[]{:S(2)}) collective-permute-start(bf16[256,768]{1,0:T(8,128)(2,1)} %param.21), channel_id=1, source_target_pairs={{0,16},{16,0},{1,17},{17,1},{2,18},{18,2},{3,19},{19,3},{4,20},{20... | collective-permute-start | bytes 1179656 | tf_op jit(solution)/shard_map/ppermute | solution.py:371
  2.2 11.9 %collective-permute-start.1 = (s32[2]{0:T(128)}, s32[2]{0:T(128)S(1)}, u32[]{:S(2)}, u32[]{:S(2)}) collective-permute-start(s32[2]{0:T(128)} %param.23), channel_id=1, source_target_pairs={{0,16},{16,0},{1,17},{17,1},{2,18},{18,2},{3,19},{19,3},{4,20},{20... | collective-permute-start | bytes 32 | tf_op jit(solution)/shard_map/ppermute | solution.py:371
  6.1 21.0 %collective-permute-start.3 = (bf16[192,1024]{1,0:T(8,128)(2,1)S(1)}, bf16[192,1024]{1,0:T(8,128)(2,1)S(1)}, u32[]{:S(2)}, u32[]{:S(2)}) collective-permute-start(bf16[192,1024]{1,0:T(8,128)(2,1)S(1)} %fusion.x_ref.refs_0_), channel_id=1, source_target_pairs={{0,1},{1,0},{2,3},{3,2},{4,5},{5,4},{6,7},{7,6},{8,9},{9,8},{10,11... | collective-permute-start | bytes 1179656 | tf_op jit(solution)/shard_map/ppermute | solution.py:367
  15.1 17.3 %collective-permute-start.5 = (bf16[72,1024]{1,0:T(8,128)(2,1)S(1)}, bf16[72,1024]{1,0:T(8,128)(2,1)S(1)}, u32[]{:S(2)}, u32[]{:S(2)}) collective-permute-start(bf16[72,1024]{1,0:T(8,128)(2,1)S(1)} %copy-done.69), channel_id=1, source_target_pairs={{0,16},{16,0},{1,17},{17,1},{2,18},{18,2},{3,19},{19,3},{4,20},{20... | collective-permute-start | bytes 442376 | tf_op jit(solution)/shard_map/ppermute | solution.py:371
  15.5 26.4 %collective-permute-start.6 = (bf16[256,768]{1,0:T(8,128)(2,1)}, bf16[256,768]{1,0:T(8,128)(2,1)}, u32[]{:S(2)}, u32[]{:S(2)}) collective-permute-start(bf16[256,768]{1,0:T(8,128)(2,1)} %cot_ref), channel_id=1, source_target_pairs={{0,16},{16,0},{1,17},{17,1},{2,18},{18,2},{3,19},{19,3},{4,20},{20... | collective-permute-start | bytes 1179656 | tf_op jit(solution)/shard_map/ppermute | solution.py:371
  16.6 55.5 %collective-permute-start.12 = (bf16[512,768]{1,0:T(8,128)(2,1)}, bf16[512,768]{1,0:T(8,128)(2,1)}, u32[]{:S(2)}, u32[]{:S(2)}) collective-permute-start(bf16[512,768]{1,0:T(8,128)(2,1)} %pad_maximum_fusion.x_ref.source_ref.refs_0_), channel_id=1, source_target_pairs={{0,1},{1,0},{2,3},{3,2},{4,5},{5,4},{6,7},{7,6},{8,9},{9,8},{10,11... | collective-permute-start | bytes 2359304 | tf_op jit(solution)/shard_map/ppermute | solution.py:367
  27.8 5.0 %collective-permute-start.4 = (bf16[192,2048]{1,0:T(8,128)(2,1)S(1)}, bf16[192,2048]{1,0:T(8,128)(2,1)S(1)}, u32[]{:S(2)}, u32[]{:S(2)}) collective-permute-start(bf16[192,2048]{1,0:T(8,128)(2,1)S(1)} %get-tuple-element.204.pack1_ref.refs_4_), channel_id=1, source_target_pairs={{0,1},{1,0},{2,3},{3,2},{4,5},{5,4},{6,7},{7,6},{8,9},{9,8},{10,11... | collective-permute-start | bytes 2359304 | tf_op jit(solution)/shard_map/ppermute | solution.py:367
  32.9 9.0 %collective-permute-start.7 = (bf16[192,2048]{1,0:T(8,128)(2,1)S(1)}, bf16[192,2048]{1,0:T(8,128)(2,1)S(1)}, u32[]{:S(2)}, u32[]{:S(2)}) collective-permute-start(bf16[192,2048]{1,0:T(8,128)(2,1)S(1)} %get-tuple-element.215.refs_10_), channel_id=1, source_target_pairs={{0,1},{1,0},{2,3},{3,2},{4,5},{5,4},{6,7},{7,6},{8,9},{9,8},{10,11... | collective-permute-start | bytes 2359304 | tf_op jit(solution)/shard_map/ppermute | solution.py:367
  41.9 4.2 %collective-permute-start.8 = (bf16[192,5120]{1,0:T(8,128)(2,1)S(1)}, bf16[192,5120]{1,0:T(8,128)(2,1)S(1)}, u32[]{:S(2)}, u32[]{:S(2)}) collective-permute-start(bf16[192,5120]{1,0:T(8,128)(2,1)S(1)} %get-tuple-element.216.pack3_ref.refs_12_), channel_id=1, source_target_pairs={{0,1},{1,0},{2,3},{3,2},{4,5},{5,4},{6,7},{7,6},{8,9},{9,8},{10,11... | collective-permute-start | bytes 5898248 | tf_op jit(solution)/shard_map/ppermute | solution.py:367
  48.7 14.0 %collective-permute-start.11 = (bf16[192,1024]{1,0:T(8,128)(2,1)S(1)}, bf16[192,1024]{1,0:T(8,128)(2,1)S(1)}, u32[]{:S(2)}, u32[]{:S(2)}) collective-permute-start(bf16[192,1024]{1,0:T(8,128)(2,1)S(1)} %get-tuple-element.228.refs_6_), channel_id=1, source_target_pairs={{0,1},{1,0},{2,3},{3,2},{4,5},{5,4},{6,7},{7,6},{8,9},{9,8},{10,11... | collective-permute-start | bytes 1179656 | tf_op jit(solution)/shard_map/ppermute | solution.py:367
  53.5 9.2 %collective-permute-start.10 = (bf16[192,1024]{1,0:T(8,128)(2,1)S(1)}, bf16[192,1024]{1,0:T(8,128)(2,1)S(1)}, u32[]{:S(2)}, u32[]{:S(2)}) collective-permute-start(bf16[192,1024]{1,0:T(8,128)(2,1)S(1)} %get-tuple-element.321.refs_2_.dq_ref), channel_id=1, source_target_pairs={{0,1},{1,0},{2,3},{3,2},{4,5},{5,4},{6,7},{7,6},{8,9},{9,8},{10,11... | collective-permute-start | bytes 1179656 | tf_op jit(solution)/shard_map/ppermute | solution.py:367
  62.4 9.7 %collective-permute-start.13 = (bf16[512,2048]{1,0:T(8,128)(2,1)S(1)}, bf16[512,2048]{1,0:T(8,128)(2,1)S(1)}, u32[]{:S(2)}, u32[]{:S(2)}) collective-permute-start(bf16[512,2048]{1,0:T(8,128)(2,1)S(1)} %get-tuple-element.239.refs_4_.dkv_ref), channel_id=1, source_target_pairs={{0,1},{1,0},{2,3},{3,2},{4,5},{5,4},{6,7},{7,6},{8,9},{9,8},{10,11... | collective-permute-start | bytes 6291464 | tf_op jit(solution)/shard_map/ppermute | solution.py:367
  69.5 17.2 %collective-permute-start.14 = (bf16[4,640,128]{2,1,0:T(8,128)(2,1)S(1)}, bf16[4,640,128]{2,1,0:T(8,128)(2,1)S(1)}, u32[]{:S(2)}, u32[]{:S(2)}) collective-permute-start(bf16[4,640,128]{2,1,0:T(8,128)(2,1)S(1)} %get-tuple-element.242), channel_id=1, source_target_pairs={{0,2},{1,3},{2,0},{3,1},{4,6},{5,7},{6,4},{7,5},{8,10},{9,11},{10,... | collective-permute-start | bytes 1966088 | tf_op jit(solution)/shard_map/ppermute | solution.py:367
  70.8 15.9 %collective-permute-start.15 = (bf16[4,640,128]{2,1,0:T(8,128)(2,1)S(1)}, bf16[4,640,128]{2,1,0:T(8,128)(2,1)S(1)}, u32[]{:S(2)}, u32[]{:S(2)}) collective-permute-start(bf16[4,640,128]{2,1,0:T(8,128)(2,1)S(1)} %get-tuple-element.243), channel_id=1, source_target_pairs={{0,4},{1,5},{2,6},{3,7},{4,0},{5,1},{6,2},{7,3},{8,12},{9,13},{10,... | collective-permute-start | bytes 1966088 | tf_op jit(solution)/shard_map/ppermute | solution.py:367
  72.1 17.5 %collective-permute-start.18 = (bf16[512,1792]{1,0:T(8,128)(2,1)S(1)}, bf16[512,1792]{1,0:T(8,128)(2,1)S(1)}, u32[]{:S(2)}, u32[]{:S(2)}) collective-permute-start(bf16[512,1792]{1,0:T(8,128)(2,1)S(1)} %get-tuple-element.246.pack1_ref.refs_6_), channel_id=1, source_target_pairs={{0,1},{1,0},{2,3},{3,2},{4,5},{5,4},{6,7},{7,6},{8,9},{9,8},{10,11... | collective-permute-start | bytes 5505032 | tf_op jit(solution)/shard_map/ppermute | solution.py:367
  86.8 16.8 %collective-permute-start.16 = (bf16[4,640,128]{2,1,0:T(8,128)(2,1)S(1)}, bf16[4,640,128]{2,1,0:T(8,128)(2,1)S(1)}, u32[]{:S(2)}, u32[]{:S(2)}) collective-permute-start(bf16[4,640,128]{2,1,0:T(8,128)(2,1)S(1)} %get-tuple-element.251), channel_id=1, source_target_pairs={{0,2},{1,3},{2,0},{3,1},{4,6},{5,7},{6,4},{7,5},{8,10},{9,11},{10,... | collective-permute-start | bytes 1966088 | tf_op jit(solution)/shard_map/ppermute | solution.py:367
  88.3 15.7 %collective-permute-start.17 = (bf16[4,640,128]{2,1,0:T(8,128)(2,1)S(1)}, bf16[4,640,128]{2,1,0:T(8,128)(2,1)S(1)}, u32[]{:S(2)}, u32[]{:S(2)}) collective-permute-start(bf16[4,640,128]{2,1,0:T(8,128)(2,1)S(1)} %get-tuple-element.252), channel_id=1, source_target_pairs={{0,4},{1,5},{2,6},{3,7},{4,0},{5,1},{6,2},{7,3},{8,12},{9,13},{10,... | collective-permute-start | bytes 1966088 | tf_op jit(solution)/shard_map/ppermute | solution.py:367
  90.8 16.9 %collective-permute-start.21 = (bf16[512,3840]{1,0:T(8,128)(2,1)S(1)}, bf16[512,3840]{1,0:T(8,128)(2,1)S(1)}, u32[]{:S(2)}, u32[]{:S(2)}) collective-permute-start(bf16[512,3840]{1,0:T(8,128)(2,1)S(1)} %get-tuple-element.269.refs_12_), channel_id=1, source_target_pairs={{0,1},{1,0},{2,3},{3,2},{4,5},{5,4},{6,7},{7,6},{8,9},{9,8},{10,11... | collective-permute-start | bytes 11796488 | tf_op jit(solution)/shard_map/ppermute | solution.py:367
  106.1 22.7 %collective-permute-start.19 = (bf16[4,640,128]{2,1,0:T(8,128)(2,1)}, bf16[4,640,128]{2,1,0:T(8,128)(2,1)}, u32[]{:S(2)}, u32[]{:S(2)}) collective-permute-start(bf16[4,640,128]{2,1,0:T(8,128)(2,1)} %get-tuple-element.265), channel_id=1, source_target_pairs={{0,4},{1,5},{2,6},{3,7},{4,0},{5,1},{6,2},{7,3},{8,12},{9,13},{10,... | collective-permute-start | bytes 1966088 | tf_op jit(solution)/shard_map/ppermute | solution.py:367
  107.4 21.4 %collective-permute-start.20 = (bf16[4,640,128]{2,1,0:T(8,128)(2,1)}, bf16[4,640,128]{2,1,0:T(8,128)(2,1)}, u32[]{:S(2)}, u32[]{:S(2)}) collective-permute-start(bf16[4,640,128]{2,1,0:T(8,128)(2,1)} %get-tuple-element.266), channel_id=1, source_target_pairs={{0,2},{1,3},{2,0},{3,1},{4,6},{5,7},{6,4},{7,5},{8,10},{9,11},{10,... | collective-permute-start | bytes 1966088 | tf_op jit(solution)/shard_map/ppermute | solution.py:367
  107.8 8.4 %collective-permute-start.22 = (bf16[512,3840]{1,0:T(8,128)(2,1)S(1)}, bf16[512,3840]{1,0:T(8,128)(2,1)S(1)}, u32[]{:S(2)}, u32[]{:S(2)}) collective-permute-start(bf16[512,3840]{1,0:T(8,128)(2,1)S(1)} %get-tuple-element.270.pack3_ref.refs_14_), channel_id=1, source_target_pairs={{0,1},{1,0},{2,3},{3,2},{4,5},{5,4},{6,7},{7,6},{8,9},{9,8},{10,11... | collective-permute-start | bytes 11796488 | tf_op jit(solution)/shard_map/ppermute | solution.py:367
  116.1 8.7 %collective-permute-start.23 = (bf16[512,3840]{1,0:T(8,128)(2,1)S(1)}, bf16[512,3840]{1,0:T(8,128)(2,1)S(1)}, u32[]{:S(2)}, u32[]{:S(2)}) collective-permute-start(bf16[512,3840]{1,0:T(8,128)(2,1)S(1)} %get-tuple-element.275.pack4_ref.refs_10_), channel_id=1, source_target_pairs={{0,1},{1,0},{2,3},{3,2},{4,5},{5,4},{6,7},{7,6},{8,9},{9,8},{10,11... | collective-permute-start | bytes 11796488 | tf_op jit(solution)/shard_map/ppermute | solution.py:367
  128.9 5.5 %collective-permute-start.24 = (bf16[192,2048]{1,0:T(8,128)(2,1)S(1)}, bf16[192,2048]{1,0:T(8,128)(2,1)S(1)}, u32[]{:S(2)}, u32[]{:S(2)}) collective-permute-start(bf16[192,2048]{1,0:T(8,128)(2,1)S(1)} %get-tuple-element.284.refs_2_.dkv_ref), channel_id=1, source_target_pairs={{0,1},{1,0},{2,3},{3,2},{4,5},{5,4},{6,7},{7,6},{8,9},{9,8},{10,11... | collective-permute-start | bytes 2359304 | tf_op jit(solution)/shard_map/ppermute | solution.py:367
  131.4 26.4 %collective-permute-start.28 = (bf16[2,640,128]{2,1,0:T(8,128)(2,1)}, bf16[2,640,128]{2,1,0:T(8,128)(2,1)}, u32[]{:S(2)}, u32[]{:S(2)}) collective-permute-start(bf16[2,640,128]{2,1,0:T(8,128)(2,1)} %get-tuple-element.298), channel_id=1, source_target_pairs={{0,8},{1,9},{2,10},{3,11},{4,12},{5,13},{6,14},{7,15},{8,0},{9,1},... | collective-permute-start | bytes 983048 | tf_op jit(solution)/shard_map/ppermute | solution.py:367
  133.7 4.4 %collective-permute-start.25 = (bf16[512,1024]{1,0:T(8,128)(2,1)S(1)}, bf16[512,1024]{1,0:T(8,128)(2,1)S(1)}, u32[]{:S(2)}, u32[]{:S(2)}) collective-permute-start(bf16[512,1024]{1,0:T(8,128)(2,1)S(1)} %get-tuple-element.316.refs_2_.dq_ref), channel_id=1, source_target_pairs={{0,1},{1,0},{2,3},{3,2},{4,5},{5,4},{6,7},{7,6},{8,9},{9,8},{10,11... | collective-permute-start | bytes 3145736 | tf_op jit(solution)/shard_map/ppermute | solution.py:367
  136.8 21.0 %collective-permute-start.27 = (bf16[2,1280,128]{2,1,0:T(8,128)(2,1)S(1)}, bf16[2,1280,128]{2,1,0:T(8,128)(2,1)S(1)}, u32[]{:S(2)}, u32[]{:S(2)}) collective-permute-start(bf16[2,1280,128]{2,1,0:T(8,128)(2,1)S(1)} %get-tuple-element.293), channel_id=1, source_target_pairs={{0,2},{1,3},{2,0},{3,1},{4,6},{5,7},{6,4},{7,5},{8,10},{9,11},{10,... | collective-permute-start | bytes 1966088 | tf_op jit(solution)/shard_map/ppermute | solution.py:367
  162.0 18.7 %collective-permute-start.29 = (bf16[4,768,128]{2,1,0:T(8,128)(2,1)S(1)}, bf16[4,768,128]{2,1,0:T(8,128)(2,1)S(1)}, u32[]{:S(2)}, u32[]{:S(2)}) collective-permute-start(bf16[4,768,128]{2,1,0:T(8,128)(2,1)S(1)} %get-tuple-element.311), channel_id=1, source_target_pairs={{0,2},{1,3},{2,0},{3,1},{4,6},{5,7},{6,4},{7,5},{8,10},{9,11},{10,... | collective-permute-start | bytes 2359304 | tf_op jit(solution)/shard_map/ppermute | solution.py:367
  163.6 7.8 %collective-permute-start.32 = (f32[3,1792]{1,0:T(4,128)S(1)}, f32[3,1792]{1,0:T(4,128)S(1)}, u32[]{:S(2)}, u32[]{:S(2)}) collective-permute-start(f32[3,1792]{1,0:T(4,128)S(1)} %copy-done.70), channel_id=1, source_target_pairs={{0,8},{1,9},{2,10},{3,11},{4,12},{5,13},{6,14},{7,15},{8,0},{9,1},... | collective-permute-start | bytes 64520 | tf_op jit(solution)/shard_map/ppermute | solution.py:367
  163.7 16.2 %collective-permute-start.30 = (bf16[1,1280,128]{2,1,0:T(8,128)(2,1)S(1)}, bf16[1,1280,128]{2,1,0:T(8,128)(2,1)S(1)}, u32[]{:S(2)}, u32[]{:S(2)}) collective-permute-start(bf16[1,1280,128]{2,1,0:T(8,128)(2,1)S(1)} %get-tuple-element.312), channel_id=1, source_target_pairs={{0,4},{1,5},{2,6},{3,7},{4,0},{5,1},{6,2},{7,3},{8,12},{9,13},{10,... | collective-permute-start | bytes 983048 | tf_op jit(solution)/shard_map/ppermute | solution.py:367
  163.9 16.0 %collective-permute-start.31 = (bf16[2,640,128]{2,1,0:T(8,128)(2,1)S(1)}, bf16[2,640,128]{2,1,0:T(8,128)(2,1)S(1)}, u32[]{:S(2)}, u32[]{:S(2)}) collective-permute-start(bf16[2,640,128]{2,1,0:T(8,128)(2,1)S(1)} %get-tuple-element.313), channel_id=1, source_target_pairs={{0,8},{1,9},{2,10},{3,11},{4,12},{5,13},{6,14},{7,15},{8,0},{9,1},... | collective-permute-start | bytes 983048 | tf_op jit(solution)/shard_map/ppermute | solution.py:367
  181.5 15.3 %collective-permute-start.33 = (bf16[2,768,128]{2,1,0:T(8,128)(2,1)S(1)}, bf16[2,768,128]{2,1,0:T(8,128)(2,1)S(1)}, u32[]{:S(2)}, u32[]{:S(2)}) collective-permute-start(bf16[2,768,128]{2,1,0:T(8,128)(2,1)S(1)} %get-tuple-element.337), channel_id=1, source_target_pairs={{0,4},{1,5},{2,6},{3,7},{4,0},{5,1},{6,2},{7,3},{8,12},{9,13},{10,... | collective-permute-start | bytes 1179656 | tf_op jit(solution)/shard_map/ppermute | solution.py:367
  182.5 16.3 %collective-permute-start.34 = (bf16[4,736,128]{2,1,0:T(8,128)(2,1)S(1)}, bf16[4,736,128]{2,1,0:T(8,128)(2,1)S(1)}, u32[]{:S(2)}, u32[]{:S(2)}) collective-permute-start(bf16[4,736,128]{2,1,0:T(8,128)(2,1)S(1)} %get-tuple-element.338), channel_id=1, source_target_pairs={{0,2},{1,3},{2,0},{3,1},{4,6},{5,7},{6,4},{7,5},{8,10},{9,11},{10,... | collective-permute-start | bytes 2261000 | tf_op jit(solution)/shard_map/ppermute | solution.py:367
  183.1 13.7 %collective-permute-start.35 = (bf16[1,1280,128]{2,1,0:T(8,128)(2,1)S(1)}, bf16[1,1280,128]{2,1,0:T(8,128)(2,1)S(1)}, u32[]{:S(2)}, u32[]{:S(2)}) collective-permute-start(bf16[1,1280,128]{2,1,0:T(8,128)(2,1)S(1)} %add_convert_fusion.1), channel_id=1, source_target_pairs={{0,8},{1,9},{10,2},{11,3},{12,4},{13,5},{14,6},{15,7},{16,24},{17,... | collective-permute-start | bytes 983048 | tf_op jit(solution)/shard_map/ppermute | solution.py:1376
  186.5 10.3 %collective-permute-start.36 = (f32[3,1792]{1,0:T(4,128)S(1)}, f32[3,1792]{1,0:T(4,128)S(1)}, u32[]{:S(2)}, u32[]{:S(2)}) collective-permute-start(f32[3,1792]{1,0:T(4,128)S(1)} %add.60), channel_id=1, source_target_pairs={{0,4},{1,5},{2,6},{3,7},{4,0},{5,1},{6,2},{7,3},{8,12},{9,13},{10,... | collective-permute-start | bytes 64520 | tf_op jit(solution)/shard_map/ppermute | solution.py:367
  198.9 16.7 %collective-permute-start.40 = (bf16[1,1280,128]{2,1,0:T(8,128)(2,1)S(1)}, bf16[1,1280,128]{2,1,0:T(8,128)(2,1)S(1)}, u32[]{:S(2)}, u32[]{:S(2)}) collective-permute-start(bf16[1,1280,128]{2,1,0:T(8,128)(2,1)S(1)} %add_convert_fusion), channel_id=1, source_target_pairs={{16,0},{17,1},{18,2},{19,3},{20,4},{21,5},{22,6},{23,7},{24,8},{25... | collective-permute-start | bytes 983048 | tf_op jit(solution)/shard_map/ppermute | solution.py:1378
  201.0 14.7 %collective-permute-start.38 = (bf16[2,736,128]{2,1,0:T(8,128)(2,1)S(1)}, bf16[2,736,128]{2,1,0:T(8,128)(2,1)S(1)}, u32[]{:S(2)}, u32[]{:S(2)}) collective-permute-start(bf16[2,736,128]{2,1,0:T(8,128)(2,1)S(1)} %get-tuple-element.348), channel_id=1, source_target_pairs={{0,4},{1,5},{2,6},{3,7},{4,0},{5,1},{6,2},{7,3},{8,12},{9,13},{10,... | collective-permute-start | bytes 1130504 | tf_op jit(solution)/shard_map/ppermute | solution.py:367
  202.0 13.6 %collective-permute-start.39 = (bf16[4,608,128]{2,1,0:T(8,128)(2,1)S(1)}, bf16[4,608,128]{2,1,0:T(8,128)(2,1)S(1)}, u32[]{:S(2)}, u32[]{:S(2)}) collective-permute-start(bf16[4,608,128]{2,1,0:T(8,128)(2,1)S(1)} %get-tuple-element.349), channel_id=1, source_target_pairs={{0,2},{1,3},{2,0},{3,1},{4,6},{5,7},{6,4},{7,5},{8,10},{9,11},{10,... | collective-permute-start | bytes 1867784 | tf_op jit(solution)/shard_map/ppermute | solution.py:367
  204.2 11.4 %collective-permute-start.37 = (bf16[1,768,128]{2,1,0:T(8,128)(2,1)S(1)}, bf16[1,768,128]{2,1,0:T(8,128)(2,1)S(1)}, u32[]{:S(2)}, u32[]{:S(2)}) collective-permute-start(bf16[1,768,128]{2,1,0:T(8,128)(2,1)S(1)} %get-tuple-element.345), channel_id=1, source_target_pairs={{0,8},{1,9},{2,10},{3,11},{4,12},{5,13},{6,14},{7,15},{8,0},{9,1},... | collective-permute-start | bytes 589832 | tf_op jit(solution)/shard_map/ppermute | solution.py:367
  204.3 11.3 %collective-permute-start.41 = (f32[3,1792]{1,0:T(4,128)S(1)}, f32[3,1792]{1,0:T(4,128)S(1)}, u32[]{:S(2)}, u32[]{:S(2)}) collective-permute-start(f32[3,1792]{1,0:T(4,128)S(1)} %add.62), channel_id=1, source_target_pairs={{0,2},{1,3},{2,0},{3,1},{4,6},{5,7},{6,4},{7,5},{8,10},{9,11},{10,... | collective-permute-start | bytes 64520 | tf_op jit(solution)/shard_map/ppermute | solution.py:367
  216.4 10.6 %collective-permute-start.43 = (bf16[2,608,128]{2,1,0:T(8,128)(2,1)S(1)}, bf16[2,608,128]{2,1,0:T(8,128)(2,1)S(1)}, u32[]{:S(2)}, u32[]{:S(2)}) collective-permute-start(bf16[2,608,128]{2,1,0:T(8,128)(2,1)S(1)} %get-tuple-element.360), channel_id=1, source_target_pairs={{0,4},{1,5},{2,6},{3,7},{4,0},{5,1},{6,2},{7,3},{8,12},{9,13},{10,... | collective-permute-start | bytes 933896 | tf_op jit(solution)/shard_map/ppermute | solution.py:367
  217.7 9.3 %collective-permute-start.44 = (bf16[4,384,128]{2,1,0:T(8,128)(2,1)S(1)}, bf16[4,384,128]{2,1,0:T(8,128)(2,1)S(1)}, u32[]{:S(2)}, u32[]{:S(2)}) collective-permute-start(bf16[4,384,128]{2,1,0:T(8,128)(2,1)S(1)} %get-tuple-element.361), channel_id=1, source_target_pairs={{0,2},{1,3},{2,0},{3,1},{4,6},{5,7},{6,4},{7,5},{8,10},{9,11},{10,... | collective-permute-start | bytes 1179656 | tf_op jit(solution)/shard_map/ppermute | solution.py:367
  219.6 7.4 %collective-permute-start.42 = (bf16[1,736,128]{2,1,0:T(8,128)(2,1)S(1)}, bf16[1,736,128]{2,1,0:T(8,128)(2,1)S(1)}, u32[]{:S(2)}, u32[]{:S(2)}) collective-permute-start(bf16[1,736,128]{2,1,0:T(8,128)(2,1)S(1)} %get-tuple-element.357), channel_id=1, source_target_pairs={{0,8},{1,9},{2,10},{3,11},{4,12},{5,13},{6,14},{7,15},{8,0},{9,1},... | collective-permute-start | bytes 565256 | tf_op jit(solution)/shard_map/ppermute | solution.py:367
  219.6 5.4 %collective-permute-start.45 = (f32[3,1792]{1,0:T(4,128)S(1)}, f32[3,1792]{1,0:T(4,128)S(1)}, u32[]{:S(2)}, u32[]{:S(2)}) collective-permute-start(f32[3,1792]{1,0:T(4,128)S(1)} %add.64), channel_id=1, source_target_pairs={{0,1},{1,0},{2,3},{3,2},{4,5},{5,4},{6,7},{7,6},{8,9},{9,8},{10,11... | collective-permute-start | bytes 64520 | tf_op jit(solution)/shard_map/ppermute | solution.py:367
  227.6 7.7 %collective-permute-start.47 = (bf16[2,384,128]{2,1,0:T(8,128)(2,1)S(1)}, bf16[2,384,128]{2,1,0:T(8,128)(2,1)S(1)}, u32[]{:S(2)}, u32[]{:S(2)}) collective-permute-start(bf16[2,384,128]{2,1,0:T(8,128)(2,1)S(1)} %get-tuple-element.370), channel_id=1, source_target_pairs={{0,4},{1,5},{2,6},{3,7},{4,0},{5,1},{6,2},{7,3},{8,12},{9,13},{10,... | collective-permute-start | bytes 589832 | tf_op jit(solution)/shard_map/ppermute | solution.py:367
  228.5 6.9 %collective-permute-start.46 = (bf16[1,608,128]{2,1,0:T(8,128)(2,1)S(1)}, bf16[1,608,128]{2,1,0:T(8,128)(2,1)S(1)}, u32[]{:S(2)}, u32[]{:S(2)}) collective-permute-start(bf16[1,608,128]{2,1,0:T(8,128)(2,1)S(1)} %get-tuple-element.367), channel_id=1, source_target_pairs={{0,8},{1,9},{2,10},{3,11},{4,12},{5,13},{6,14},{7,15},{8,0},{9,1},... | collective-permute-start | bytes 466952 | tf_op jit(solution)/shard_map/ppermute | solution.py:367
  236.0 7.6 %collective-permute-start.48 = (bf16[1,384,128]{2,1,0:T(8,128)(2,1)S(1)}, bf16[1,384,128]{2,1,0:T(8,128)(2,1)S(1)}, u32[]{:S(2)}, u32[]{:S(2)}) collective-permute-start(bf16[1,384,128]{2,1,0:T(8,128)(2,1)S(1)} %get-tuple-element.375), channel_id=1, source_target_pairs={{0,8},{1,9},{2,10},{3,11},{4,12},{5,13},{6,14},{7,15},{8,0},{9,1},... | collective-permute-start | bytes 294920 | tf_op jit(solution)/shard_map/ppermute | solution.py:367
  245.8 9.5 %collective-permute-start.49 = (f32[2528,128]{1,0:T(8,128)S(1)}, f32[2528,128]{1,0:T(8,128)S(1)}, u32[]{:S(2)}, u32[]{:S(2)}) collective-permute-start(f32[2528,128]{1,0:T(8,128)S(1)} %get-tuple-element.378), channel_id=1, source_target_pairs={{0,1},{1,0},{2,3},{3,2},{4,5},{5,4},{6,7},{7,6},{8,9},{9,8},{10,11... | collective-permute-start | bytes 3883016 | tf_op jit(solution)/shard_map/ppermute | solution.py:367
  (94 other events, 893.2 us)

commit v4 on v3

--- a/solution.py
+++ b/solution.py
@@ -582,7 +582,8 @@
     for total_ref in totals:
         half = total_ref.shape[0] // 2
         for ref, index in ((out_ref, core), (send_ref, 1 - core)):
-            ref[row : row + half, :] = total_ref[pl.ds(pl.multiple_of(index * half, 8), half), :]
+            part = total_ref[pl.ds(pl.multiple_of(index * half, 8), half), :]
+            ref[row : row + half, :] = part.astype(ref.dtype)
         row += half
 
 
@@ -592,7 +593,7 @@
     for out_ref in outs:
         half = out_ref.shape[0] // 2
         out_ref[pl.ds(core, half, stride=2), :] = near_ref[row : row + half, :]
-        out_ref[pl.ds(1 - core, half, stride=2), :] = far_ref[row : row + half, :]
+        out_ref[pl.ds(1 - core, half, stride=2), :] = far_ref[row : row + half, :].astype(F32)
         row += half
 
 
@@ -609,7 +610,7 @@
         functools.partial(finish_kernel, rows=rows),
         in_specs=[smem] + [vmem] * len(operands),
         out_specs=[vmem] * 2,
-        out_shape=[half] * 2,
+        out_shape=[half, jax.ShapeDtypeStruct(half.shape, BF16)],
         scratch_shapes=[pltpu.VMEM((rows, LANES), F32) for rows in (*sizes, sizes[0])],
         compiler_params=pltpu.CompilerParams(vmem_limit_bytes=12 * 1024 * 1024),
         cost_estimate=cost(3),

time: 261 us -> 260 us (level)
  transfers between devices with their start and end apart: 50 -> 50, of which waited for: 14 -> 14; matrix products, arithmetic and copies ran while one was open for 4% -> 4% of each run, Pallas kernels for 45% -> 46%
where the time goes in v4:
time: 260 us; the launch traced here: 257 us
  Pallas kernels  126 us (48%)
  starting transfers between devices  56.6 us (22%)
  waiting for transfers between devices  53.2 us (20%)
  local copies, waits for them, and re-layouts  11.1 us (4%)
  matrix products  5.8 us (2%)
    pallas_call x10, Pallas kernels, fused(): pl.pallas_call(kernel, in_specs=in_specs, out_specs=[vmem] * len(outs), o...  69.8 us
    ppermute x43, waiting for transfers between devices, dp_swap(): return lax.ppermute(block, 'dp', [(i, i ^ bit) for i in range(count)])  49.6 us
    ppermute x43, starting transfers between devices, dp_swap(): return lax.ppermute(block, 'dp', [(i, i ^ bit) for i in range(count)])  48.8 us
    pallas_call x3, Pallas kernels, flat_grads(): pl.pallas_call(functools.partial(flat_kernel, plans=plans, found=found, q...  24.8 us
    pallas_call x11, Pallas kernels, add_split(): pl.pallas_call(functools.partial(add_split_kernel, plan=tuple(plan), inpu...  10.6 us
    unnamed x184, local copies, waits for them, and re-layouts  9.75 us
    pallas_call x2, Pallas kernels, attend_back(): pl.pallas_call(functools.partial(body, pairs=pairs, blocks=blocks, cols=c...  8.42 us
    dot_general x6, matrix products, mm(): return jnp.dot(a, b, preferred_element_type=F32)  5.8 us
  transfers between devices with their start and end apart: 50, of which 14 were waited for; matrix products, arithmetic and copies ran while one was open for 4% of the time, Pallas kernels for 46%

profile of v4, /device:TPU:3, one launch (start us, length us, event | category | flops | bytes accessed | tf_op | source)
XLA Modules:
  0.0 256.8 jit_solution(145074312750688693)
XLA Ops:
  0.7 1.5 collective-permute-start
  2.4 1.3 fusion.9
  3.9 1.8 collective-permute-done.2
  6.1 2.8 %collective-permute-start.3 = (bf16[192,1024]{1,0:T(8,128)(2,1)S(1)}, bf16[192,1024]{1,0:T(8,128)(2,1)S(1)}, u32[]{:S(2)}, u32[]{:S(2)}) collective-permute-start(bf16[192,1024]{1,0:T(8,128)(2,1)S(1)} %fusion.x_ref.refs_0_), channel_id=1, source_target_pairs={{0,1},{1,0},{2,3},{3,2},{4,5},{5,4},{6,7},{7,6},{8,9},{9,8},{10,11... | collective-permute-start | bytes 1179656 | tf_op jit(solution)/shard_map/ppermute | solution.py:367
  8.8 2.2 convolution_convert_fusion.1.given_ref.refs_0_
  12.2 1.9 collective-permute-done.1
  16.6 2.2 collective-permute-start.12
  18.8 7.8 %co_forward.3 = (bf16[512,2048]{1,0:T(8,128)(2,1)S(1)}, bf16[192,2048]{1,0:T(8,128)(2,1)S(1)}, f32[192,1024]{1,0:T(8,128)S(1)}, f32[192,128]{1,0:T(8,128)S(1)}) custom-call(s32[4]{0:T(128)S(1)} %pad_add_fusion.1.lens_ref, bf16[192,1024]{1,0:T(8,128)(2,1)S(1)} %fusion.x_ref.refs_0_, bf16[192,1024]{1,0:T(8,128)(2,1)S(1)} %convolution_convert_fusion.1.given_ref.refs_0_, ...), custom_call_target="tpu_custom_call" | custom-call | flops 70000001024 | bytes 1000 | tf_op jit(solution)/shard_map/co_forward/pallas_call | solution.py:846
  28.7 3.7 %mlp_forward.2 = (bf16[192,2048]{1,0:T(8,128)(2,1)S(1)}, bf16[192,1024]{1,0:T(8,128)(2,1)S(1)}, f32[192,1024]{1,0:T(8,128)S(1)}, f32[192,128]{1,0:T(8,128)S(1)}, bf16[192,3072]{1,0:T(8,128)(2,1)S(1)}) custom-call(bf16[192,2048]{1,0:T(8,128)(2,1)S(1)} %get-tuple-element.204.pack1_ref.refs_4_, f32[192,1024]{1,0:T(8,128)S(1)} %get-tuple-element.205.n1_ref, ...), custom_call_target="tpu_custom_call" | custom-call | flops 48000000000 | bytes 1000 | tf_op jit(solution)/shard_map/mlp_forward/pallas_call | solution.py:846
  33.0 8.9 %self_turn.2 = (bf16[192,5120]{1,0:T(8,128)(2,1)S(1)}, bf16[192,1024]{1,0:T(8,128)(2,1)S(1)}, f32[192,1024]{1,0:T(8,128)S(1)}, f32[1,1024]{1,0:T(1,128)S(1)}) custom-call(s32[4]{0:T(128)S(1)} %pad_add_fusion.1.lens_ref, bf16[192,3072]{1,0:T(8,128)(2,1)S(1)} %get-tuple-element.209.r_ref, f32[192,1024]{1,0:T(8,128)S(1)} %get-tuple-element.210.n2_ref, ...), custom_call_target="tpu_custom_call" | custom-call | flops 105000001536 | bytes 1000 | tf_op jit(solution)/shard_map/self_turn/pallas_call | solution.py:846
  42.5 3.6 %mlp_back.2 = (bf16[192,2048]{1,0:T(8,128)(2,1)S(1)}, f32[192,1024]{1,0:T(8,128)S(1)}, f32[1,1024]{1,0:T(1,128)S(1)}) custom-call(bf16[192,5120]{1,0:T(8,128)(2,1)S(1)} %get-tuple-element.216.pack3_ref.refs_12_, f32[192,1024]{1,0:T(8,128)S(1)} %get-tuple-element.217.de_ref, f32[192,1024]{1,0:T(8,128)S(1)} %get-tuple-element.210.n2_ref, ...), custom_call_target="tpu_custom_call" | custom-call | flops 27428571136 | bytes 1000 | tf_op jit(solution)/shard_map/mlp_back/pallas_call | solution.py:846
  46.5 2.2 context_back.2
  49.0 4.4 %attend_back.2 = (bf16[192,1024]{1,0:T(8,128)(2,1)S(1)}, bf16[512,2048]{1,0:T(8,128)(2,1)S(1)}) custom-call(s32[4]{0:T(128)S(1)} %pad_add_fusion.1.lens_ref, bf16[192,1024]{1,0:T(8,128)(2,1)S(1)} %copy-done.19, bf16[512,2048]{1,0:T(8,128)(2,1)S(1)} %get-tuple-element.203.refs_1_, bf16[192,1024]{1,0:T(8,128)(2,1)S(1)} %get-tuple-element.225.refs_2_), custom_call_target="tpu_custom_call" | custom-call | flops 60000002048 | bytes 1000 | tf_op jit(solution)/shard_map/attend_back/pallas_call | solution.py:213
  53.9 8.5 %co_forward.2 = (bf16[512,1024]{1,0:T(8,128)(2,1)S(1)}, bf16[512,1792]{1,0:T(8,128)(2,1)S(1)}, f32[512,768]{1,0:T(8,128)S(1)}, f32[512,128]{1,0:T(8,128)S(1)}) custom-call(s32[4]{0:T(128)S(1)} %pad_add_fusion.1.lens_ref, bf16[512,768]{1,0:T(8,128)(2,1)} %pad_maximum_fusion.x_ref.source_ref.refs_0_, ...), custom_call_target="tpu_custom_call" | custom-call | flops 70000001024 | bytes 1000 | tf_op jit(solution)/shard_map/co_forward/pallas_call | solution.py:846
  62.8 5.8 %flat_grads.3.flat_ref = bf16[20480,128]{1,0:T(8,128)(2,1)S(1)} custom-call(s32[2]{0:T(128)S(1)} %pad_add_fusion.side_ref, bf16[192,1024]{1,0:T(8,128)(2,1)S(1)} %copy-done.4, bf16[192,1024]{1,0:T(8,128)(2,1)S(1)} %copy-done.54, bf16[192,1024]{1,0:T(8,128)(2,1)S(1)} %get-tuple-element.321.refs_2_.dq_ref, ...), custom_call_target="tpu_custom_call" | custom-call | flops 60000002048 | bytes 1000 | tf_op jit(solution)/shard_map/flat_grads/pallas_call | solution.py:350
  73.9 11.1 %mlp_forward.3 = (bf16[512,3840]{1,0:T(8,128)(2,1)S(1)}, bf16[512,3072]{1,0:T(8,128)(2,1)S(1)}, f32[512,768]{1,0:T(8,128)S(1)}, f32[512,128]{1,0:T(8,128)S(1)}, bf16[512,2304]{1,0:T(8,128)(2,1)S(1)}) custom-call(bf16[512,1792]{1,0:T(8,128)(2,1)S(1)} %get-tuple-element.246.pack1_ref.refs_6_, f32[512,768]{1,0:T(8,128)S(1)} %get-tuple-element.247.n1_ref, ...), custom_call_target="tpu_custom_call" | custom-call | flops 128000000000 | bytes 1000 | tf_op jit(solution)/shard_map/mlp_forward/pallas_call | solution.py:846
  85.0 1.7 copy-done.64
  86.8 1.6 collective-permute-start.16
  91.8 11.8 %self_turn.3 = (bf16[512,3840]{1,0:T(8,128)(2,1)S(1)}, bf16[512,768]{1,0:T(8,128)(2,1)S(1)}, f32[512,768]{1,0:T(8,128)S(1)}, f32[1,768]{1,0:T(1,128)S(1)}) custom-call(s32[4]{0:T(128)S(1)} %copy-done.61, bf16[512,2304]{1,0:T(8,128)(2,1)S(1)} %get-tuple-element.256.r_ref, f32[512,768]{1,0:T(8,128)S(1)} %get-tuple-element.257.n2_ref, f32[3,768]{1,0:T(4,128)S(1)} %copy-done.57, ...), custom_call_target="tpu_custom_call" | custom-call | flops 130000003072 | bytes 1000 | tf_op jit(solution)/shard_map/self_turn/pallas_call | solution.py:846
  104.0 2.2 add_split.11
  107.8 2.0 collective-permute-start.22
  109.8 6.2 %mlp_back.3 = (bf16[512,3840]{1,0:T(8,128)(2,1)S(1)}, f32[512,768]{1,0:T(8,128)S(1)}, f32[1,768]{1,0:T(1,128)S(1)}) custom-call(bf16[512,3840]{1,0:T(8,128)(2,1)S(1)} %get-tuple-element.270.pack3_ref.refs_14_, f32[512,768]{1,0:T(8,128)S(1)} %get-tuple-element.271.de_ref, f32[512,768]{1,0:T(8,128)S(1)} %get-tuple-element.257.n2_ref, ...), custom_call_target="tpu_custom_call" | custom-call | flops 73142853632 | bytes 1000 | tf_op jit(solution)/shard_map/mlp_back/pallas_call | solution.py:846
  116.1 1.8 collective-permute-start.23
  118.0 6.2 %context_back.3 = (bf16[512,768]{1,0:T(8,128)(2,1)S(1)}, f32[512,768]{1,0:T(8,128)S(1)}, bf16[512,1024]{1,0:T(8,128)(2,1)S(1)}, f32[1,768]{1,0:T(1,128)S(1)}) custom-call(bf16[512,3840]{1,0:T(8,128)(2,1)S(1)} %get-tuple-element.275.pack4_ref.refs_10_, f32[512,768]{1,0:T(8,128)S(1)} %get-tuple-element.276.db_ref, f32[512,768]{1,0:T(8,128)S(1)} %copy-done.67, ...), custom_call_target="tpu_custom_call" | custom-call | flops 64000000000 | bytes 1000 | tf_op jit(solution)/shard_map/context_back/pallas_call | solution.py:846
  124.9 4.0 %attend_back.3 = (bf16[512,1024]{1,0:T(8,128)(2,1)S(1)}, bf16[192,2048]{1,0:T(8,128)(2,1)S(1)}) custom-call(s32[4]{0:T(128)S(1)} %copy-done.62, bf16[512,1024]{1,0:T(8,128)(2,1)S(1)} %get-tuple-element.267.refs_0_, bf16[192,2048]{1,0:T(8,128)(2,1)S(1)} %copy-done.15, bf16[512,1024]{1,0:T(8,128)(2,1)S(1)} %get-tuple-element.279.refs_2_), custom_call_target="tpu_custom_call" | custom-call | flops 60000002048 | bytes 1000 | tf_op jit(solution)/shard_map/attend_back/pallas_call | solution.py:213
  129.0 2.4 add_split.12
  131.4 2.3 collective-permute-start.28
  134.4 1.7 flat_grads.4.flat_ref
  140.6 17.3 %flat_grads.5.flat_ref = bf16[19968,128]{1,0:T(8,128)(2,1)} custom-call(s32[2]{0:T(128)S(1)} %copy-done.59, bf16[512,768]{1,0:T(8,128)(2,1)} %pad_maximum_fusion.x_ref.source_ref.refs_0_, bf16[512,768]{1,0:T(8,128)(2,1)} %collective-permute-done.12.refs_1_, bf16[512,1024]{1,0:T(8,128)(2,1)S(1)} %get-tuple-element.316.refs_2_.dq_ref, ...), custom_call_target="tpu_custom_call" | custom-call | flops 140000002048 | bytes 1000 | tf_op jit(solution)/shard_map/flat_grads/pallas_call | solution.py:350
  157.9 2.4 copy-done.63
  162.0 1.3 collective-permute-start.29
  163.9 2.3 collective-permute-start.31
  166.3 2.9 %input_grads.3 = (bf16[72,1024]{1,0:T(8,128)(2,1)}, bf16[72,1024]{1,0:T(8,128)(2,1)}) custom-call(f32[192,1024]{1,0:T(8,128)S(1)} %get-tuple-element.320.da_ref, bf16[192,1024]{1,0:T(8,128)(2,1)S(1)} %copy-done.17, bf16[192,2048]{1,0:T(8,128)(2,1)S(1)} %copy-done.13, bf16[192,1024]{1,0:T(8,128)(2,1)S(1)} %get-tuple-element.322.y_ref, ...), custom_call_target="tpu_custom_call" | custom-call | flops 2000000000 | bytes 1000 | tf_op jit(solution)/shard_map/input_grads/pallas_call | solution.py:938
  169.2 2.3 input_grads.2
  171.5 8.5 %collective-permute-done.30 = bf16[1,1280,128]{2,1,0:T(8,128)(2,1)S(1)} collective-permute-done((bf16[1,1280,128]{2,1,0:T(8,128)(2,1)S(1)}, bf16[1,1280,128]{2,1,0:T(8,128)(2,1)S(1)}, u32[]{:S(2)}, u32[]{:S(2)}) %collective-permute-start.30) | collective-permute-done | bytes 327712 | tf_op jit(solution)/shard_map/ppermute | solution.py:367
  183.1 3.4 %collective-permute-start.35 = (bf16[1,1280,128]{2,1,0:T(8,128)(2,1)S(1)}, bf16[1,1280,128]{2,1,0:T(8,128)(2,1)S(1)}, u32[]{:S(2)}, u32[]{:S(2)}) collective-permute-start(bf16[1,1280,128]{2,1,0:T(8,128)(2,1)S(1)} %add_convert_fusion.1), channel_id=1, source_target_pairs={{0,8},{1,9},{10,2},{11,3},{12,4},{13,5},{14,6},{15,7},{16,24},{17,... | collective-permute-start | bytes 983048 | tf_op jit(solution)/shard_map/ppermute | solution.py:1377
  186.6 10.2 %collective-permute-done.36 = f32[3,1792]{1,0:T(4,128)S(1)} collective-permute-done((f32[3,1792]{1,0:T(4,128)S(1)}, f32[3,1792]{1,0:T(4,128)S(1)}, u32[]{:S(2)}, u32[]{:S(2)}) %collective-permute-start.36) | collective-permute-done | bytes 21536 | tf_op jit(solution)/shard_map/ppermute | solution.py:367
  196.9 2.0 collective-permute-done.34.refs_1_
  202.0 1.6 collective-permute-start.39
  204.9 10.7 %collective-permute-done.41 = f32[3,1792]{1,0:T(4,128)S(1)} collective-permute-done((f32[3,1792]{1,0:T(4,128)S(1)}, f32[3,1792]{1,0:T(4,128)S(1)}, u32[]{:S(2)}, u32[]{:S(2)}) %collective-permute-start.41) | collective-permute-done | bytes 21536 | tf_op jit(solution)/shard_map/ppermute | solution.py:367
  216.4 1.4 collective-permute-start.43
  219.6 4.6 %collective-permute-start.45 = (f32[3,1792]{1,0:T(4,128)S(1)}, f32[3,1792]{1,0:T(4,128)S(1)}, u32[]{:S(2)}, u32[]{:S(2)}) collective-permute-start(f32[3,1792]{1,0:T(4,128)S(1)} %add.64), channel_id=1, source_target_pairs={{0,1},{1,0},{2,3},{3,2},{4,5},{5,4},{6,7},{7,6},{8,9},{9,8},{10,11... | collective-permute-start | bytes 64520 | tf_op jit(solution)/shard_map/ppermute | solution.py:367
  225.1 1.9 collective-permute-done.42.refs_7_
  229.2 6.2 %collective-permute-done.46.refs_9_ = bf16[1,608,128]{2,1,0:T(8,128)(2,1)S(1)} collective-permute-done((bf16[1,608,128]{2,1,0:T(8,128)(2,1)S(1)}, bf16[1,608,128]{2,1,0:T(8,128)(2,1)S(1)}, u32[]{:S(2)}, u32[]{:S(2)}) %collective-permute-start.46) | collective-permute-done | bytes 155680 | tf_op jit(solution)/shard_map/ppermute | solution.py:367
  236.3 7.2 %collective-permute-done.48.refs_11_ = bf16[1,384,128]{2,1,0:T(8,128)(2,1)S(1)} collective-permute-done((bf16[1,384,128]{2,1,0:T(8,128)(2,1)S(1)}, bf16[1,384,128]{2,1,0:T(8,128)(2,1)S(1)}, u32[]{:S(2)}, u32[]{:S(2)}) %collective-permute-start.48) | collective-permute-done | bytes 98336 | tf_op jit(solution)/shard_map/ppermute | solution.py:367
  243.5 2.2 finish.1
  245.8 6.9 %collective-permute-start.49 = (bf16[2528,128]{1,0:T(8,128)(2,1)S(1)}, bf16[2528,128]{1,0:T(8,128)(2,1)S(1)}, u32[]{:S(2)}, u32[]{:S(2)}) collective-permute-start(bf16[2528,128]{1,0:T(8,128)(2,1)S(1)} %get-tuple-element.378), channel_id=1, source_target_pairs={{0,1},{1,0},{2,3},{3,2},{4,5},{5,4},{6,7},{7,6},{8,9},{9,8},{10,11... | collective-permute-start | bytes 1941512 | tf_op jit(solution)/shard_map/ppermute | solution.py:367
  254.4 2.2 join.1
  (297 shorter events, 43.7 us)
Async XLA Ops:
  0.6 5.0 %collective-permute-start.2 = (bf16[72,1024]{1,0:T(8,128)(2,1)}, bf16[72,1024]{1,0:T(8,128)(2,1)S(1)}, u32[]{:S(2)}, u32[]{:S(2)}) collective-permute-start(bf16[72,1024]{1,0:T(8,128)(2,1)} %param.22), channel_id=1, source_target_pairs={{0,16},{16,0},{1,17},{17,1},{2,18},{18,2},{3,19},{19,3},{4,20},{20... | collective-permute-start | bytes 442376 | tf_op jit(solution)/shard_map/ppermute | solution.py:371
  0.7 13.3 %collective-permute-start = (bf16[256,768]{1,0:T(8,128)(2,1)}, bf16[256,768]{1,0:T(8,128)(2,1)S(1)}, u32[]{:S(2)}, u32[]{:S(2)}) collective-permute-start(bf16[256,768]{1,0:T(8,128)(2,1)} %param.21), channel_id=1, source_target_pairs={{0,16},{16,0},{1,17},{17,1},{2,18},{18,2},{3,19},{19,3},{4,20},{20... | collective-permute-start | bytes 1179656 | tf_op jit(solution)/shard_map/ppermute | solution.py:371
  2.2 11.9 %collective-permute-start.1 = (s32[2]{0:T(128)}, s32[2]{0:T(128)S(1)}, u32[]{:S(2)}, u32[]{:S(2)}) collective-permute-start(s32[2]{0:T(128)} %param.23), channel_id=1, source_target_pairs={{0,16},{16,0},{1,17},{17,1},{2,18},{18,2},{3,19},{19,3},{4,20},{20... | collective-permute-start | bytes 32 | tf_op jit(solution)/shard_map/ppermute | solution.py:371
  6.1 21.0 %collective-permute-start.3 = (bf16[192,1024]{1,0:T(8,128)(2,1)S(1)}, bf16[192,1024]{1,0:T(8,128)(2,1)S(1)}, u32[]{:S(2)}, u32[]{:S(2)}) collective-permute-start(bf16[192,1024]{1,0:T(8,128)(2,1)S(1)} %fusion.x_ref.refs_0_), channel_id=1, source_target_pairs={{0,1},{1,0},{2,3},{3,2},{4,5},{5,4},{6,7},{7,6},{8,9},{9,8},{10,11... | collective-permute-start | bytes 1179656 | tf_op jit(solution)/shard_map/ppermute | solution.py:367
  15.1 17.3 %collective-permute-start.5 = (bf16[72,1024]{1,0:T(8,128)(2,1)S(1)}, bf16[72,1024]{1,0:T(8,128)(2,1)S(1)}, u32[]{:S(2)}, u32[]{:S(2)}) collective-permute-start(bf16[72,1024]{1,0:T(8,128)(2,1)S(1)} %copy-done.69), channel_id=1, source_target_pairs={{0,16},{16,0},{1,17},{17,1},{2,18},{18,2},{3,19},{19,3},{4,20},{20... | collective-permute-start | bytes 442376 | tf_op jit(solution)/shard_map/ppermute | solution.py:371
  15.5 26.4 %collective-permute-start.6 = (bf16[256,768]{1,0:T(8,128)(2,1)}, bf16[256,768]{1,0:T(8,128)(2,1)}, u32[]{:S(2)}, u32[]{:S(2)}) collective-permute-start(bf16[256,768]{1,0:T(8,128)(2,1)} %cot_ref), channel_id=1, source_target_pairs={{0,16},{16,0},{1,17},{17,1},{2,18},{18,2},{3,19},{19,3},{4,20},{20... | collective-permute-start | bytes 1179656 | tf_op jit(solution)/shard_map/ppermute | solution.py:371
  16.6 55.5 %collective-permute-start.12 = (bf16[512,768]{1,0:T(8,128)(2,1)}, bf16[512,768]{1,0:T(8,128)(2,1)}, u32[]{:S(2)}, u32[]{:S(2)}) collective-permute-start(bf16[512,768]{1,0:T(8,128)(2,1)} %pad_maximum_fusion.x_ref.source_ref.refs_0_), channel_id=1, source_target_pairs={{0,1},{1,0},{2,3},{3,2},{4,5},{5,4},{6,7},{7,6},{8,9},{9,8},{10,11... | collective-permute-start | bytes 2359304 | tf_op jit(solution)/shard_map/ppermute | solution.py:367
  27.8 5.0 %collective-permute-start.4 = (bf16[192,2048]{1,0:T(8,128)(2,1)S(1)}, bf16[192,2048]{1,0:T(8,128)(2,1)S(1)}, u32[]{:S(2)}, u32[]{:S(2)}) collective-permute-start(bf16[192,2048]{1,0:T(8,128)(2,1)S(1)} %get-tuple-element.204.pack1_ref.refs_4_), channel_id=1, source_target_pairs={{0,1},{1,0},{2,3},{3,2},{4,5},{5,4},{6,7},{7,6},{8,9},{9,8},{10,11... | collective-permute-start | bytes 2359304 | tf_op jit(solution)/shard_map/ppermute | solution.py:367
  32.9 9.0 %collective-permute-start.7 = (bf16[192,2048]{1,0:T(8,128)(2,1)S(1)}, bf16[192,2048]{1,0:T(8,128)(2,1)S(1)}, u32[]{:S(2)}, u32[]{:S(2)}) collective-permute-start(bf16[192,2048]{1,0:T(8,128)(2,1)S(1)} %get-tuple-element.215.refs_10_), channel_id=1, source_target_pairs={{0,1},{1,0},{2,3},{3,2},{4,5},{5,4},{6,7},{7,6},{8,9},{9,8},{10,11... | collective-permute-start | bytes 2359304 | tf_op jit(solution)/shard_map/ppermute | solution.py:367
  41.9 4.2 %collective-permute-start.8 = (bf16[192,5120]{1,0:T(8,128)(2,1)S(1)}, bf16[192,5120]{1,0:T(8,128)(2,1)S(1)}, u32[]{:S(2)}, u32[]{:S(2)}) collective-permute-start(bf16[192,5120]{1,0:T(8,128)(2,1)S(1)} %get-tuple-element.216.pack3_ref.refs_12_), channel_id=1, source_target_pairs={{0,1},{1,0},{2,3},{3,2},{4,5},{5,4},{6,7},{7,6},{8,9},{9,8},{10,11... | collective-permute-start | bytes 5898248 | tf_op jit(solution)/shard_map/ppermute | solution.py:367
  48.7 14.0 %collective-permute-start.11 = (bf16[192,1024]{1,0:T(8,128)(2,1)S(1)}, bf16[192,1024]{1,0:T(8,128)(2,1)S(1)}, u32[]{:S(2)}, u32[]{:S(2)}) collective-permute-start(bf16[192,1024]{1,0:T(8,128)(2,1)S(1)} %get-tuple-element.228.refs_6_), channel_id=1, source_target_pairs={{0,1},{1,0},{2,3},{3,2},{4,5},{5,4},{6,7},{7,6},{8,9},{9,8},{10,11... | collective-permute-start | bytes 1179656 | tf_op jit(solution)/shard_map/ppermute | solution.py:367
  53.5 9.2 %collective-permute-start.10 = (bf16[192,1024]{1,0:T(8,128)(2,1)S(1)}, bf16[192,1024]{1,0:T(8,128)(2,1)S(1)}, u32[]{:S(2)}, u32[]{:S(2)}) collective-permute-start(bf16[192,1024]{1,0:T(8,128)(2,1)S(1)} %get-tuple-element.321.refs_2_.dq_ref), channel_id=1, source_target_pairs={{0,1},{1,0},{2,3},{3,2},{4,5},{5,4},{6,7},{7,6},{8,9},{9,8},{10,11... | collective-permute-start | bytes 1179656 | tf_op jit(solution)/shard_map/ppermute | solution.py:367
  62.4 9.7 %collective-permute-start.13 = (bf16[512,2048]{1,0:T(8,128)(2,1)S(1)}, bf16[512,2048]{1,0:T(8,128)(2,1)S(1)}, u32[]{:S(2)}, u32[]{:S(2)}) collective-permute-start(bf16[512,2048]{1,0:T(8,128)(2,1)S(1)} %get-tuple-element.239.refs_4_.dkv_ref), channel_id=1, source_target_pairs={{0,1},{1,0},{2,3},{3,2},{4,5},{5,4},{6,7},{7,6},{8,9},{9,8},{10,11... | collective-permute-start | bytes 6291464 | tf_op jit(solution)/shard_map/ppermute | solution.py:367
  69.5 17.2 %collective-permute-start.14 = (bf16[4,640,128]{2,1,0:T(8,128)(2,1)S(1)}, bf16[4,640,128]{2,1,0:T(8,128)(2,1)S(1)}, u32[]{:S(2)}, u32[]{:S(2)}) collective-permute-start(bf16[4,640,128]{2,1,0:T(8,128)(2,1)S(1)} %get-tuple-element.242), channel_id=1, source_target_pairs={{0,2},{1,3},{2,0},{3,1},{4,6},{5,7},{6,4},{7,5},{8,10},{9,11},{10,... | collective-permute-start | bytes 1966088 | tf_op jit(solution)/shard_map/ppermute | solution.py:367
  70.8 15.9 %collective-permute-start.15 = (bf16[4,640,128]{2,1,0:T(8,128)(2,1)S(1)}, bf16[4,640,128]{2,1,0:T(8,128)(2,1)S(1)}, u32[]{:S(2)}, u32[]{:S(2)}) collective-permute-start(bf16[4,640,128]{2,1,0:T(8,128)(2,1)S(1)} %get-tuple-element.243), channel_id=1, source_target_pairs={{0,4},{1,5},{2,6},{3,7},{4,0},{5,1},{6,2},{7,3},{8,12},{9,13},{10,... | collective-permute-start | bytes 1966088 | tf_op jit(solution)/shard_map/ppermute | solution.py:367
  72.1 17.5 %collective-permute-start.18 = (bf16[512,1792]{1,0:T(8,128)(2,1)S(1)}, bf16[512,1792]{1,0:T(8,128)(2,1)S(1)}, u32[]{:S(2)}, u32[]{:S(2)}) collective-permute-start(bf16[512,1792]{1,0:T(8,128)(2,1)S(1)} %get-tuple-element.246.pack1_ref.refs_6_), channel_id=1, source_target_pairs={{0,1},{1,0},{2,3},{3,2},{4,5},{5,4},{6,7},{7,6},{8,9},{9,8},{10,11... | collective-permute-start | bytes 5505032 | tf_op jit(solution)/shard_map/ppermute | solution.py:367
  86.8 16.8 %collective-permute-start.16 = (bf16[4,640,128]{2,1,0:T(8,128)(2,1)S(1)}, bf16[4,640,128]{2,1,0:T(8,128)(2,1)S(1)}, u32[]{:S(2)}, u32[]{:S(2)}) collective-permute-start(bf16[4,640,128]{2,1,0:T(8,128)(2,1)S(1)} %get-tuple-element.251), channel_id=1, source_target_pairs={{0,2},{1,3},{2,0},{3,1},{4,6},{5,7},{6,4},{7,5},{8,10},{9,11},{10,... | collective-permute-start | bytes 1966088 | tf_op jit(solution)/shard_map/ppermute | solution.py:367
  88.3 15.7 %collective-permute-start.17 = (bf16[4,640,128]{2,1,0:T(8,128)(2,1)S(1)}, bf16[4,640,128]{2,1,0:T(8,128)(2,1)S(1)}, u32[]{:S(2)}, u32[]{:S(2)}) collective-permute-start(bf16[4,640,128]{2,1,0:T(8,128)(2,1)S(1)} %get-tuple-element.252), channel_id=1, source_target_pairs={{0,4},{1,5},{2,6},{3,7},{4,0},{5,1},{6,2},{7,3},{8,12},{9,13},{10,... | collective-permute-start | bytes 1966088 | tf_op jit(solution)/shard_map/ppermute | solution.py:367
  90.8 16.9 %collective-permute-start.21 = (bf16[512,3840]{1,0:T(8,128)(2,1)S(1)}, bf16[512,3840]{1,0:T(8,128)(2,1)S(1)}, u32[]{:S(2)}, u32[]{:S(2)}) collective-permute-start(bf16[512,3840]{1,0:T(8,128)(2,1)S(1)} %get-tuple-element.269.refs_12_), channel_id=1, source_target_pairs={{0,1},{1,0},{2,3},{3,2},{4,5},{5,4},{6,7},{7,6},{8,9},{9,8},{10,11... | collective-permute-start | bytes 11796488 | tf_op jit(solution)/shard_map/ppermute | solution.py:367
  106.1 22.7 %collective-permute-start.19 = (bf16[4,640,128]{2,1,0:T(8,128)(2,1)}, bf16[4,640,128]{2,1,0:T(8,128)(2,1)}, u32[]{:S(2)}, u32[]{:S(2)}) collective-permute-start(bf16[4,640,128]{2,1,0:T(8,128)(2,1)} %get-tuple-element.265), channel_id=1, source_target_pairs={{0,4},{1,5},{2,6},{3,7},{4,0},{5,1},{6,2},{7,3},{8,12},{9,13},{10,... | collective-permute-start | bytes 1966088 | tf_op jit(solution)/shard_map/ppermute | solution.py:367
  107.4 21.4 %collective-permute-start.20 = (bf16[4,640,128]{2,1,0:T(8,128)(2,1)}, bf16[4,640,128]{2,1,0:T(8,128)(2,1)}, u32[]{:S(2)}, u32[]{:S(2)}) collective-permute-start(bf16[4,640,128]{2,1,0:T(8,128)(2,1)} %get-tuple-element.266), channel_id=1, source_target_pairs={{0,2},{1,3},{2,0},{3,1},{4,6},{5,7},{6,4},{7,5},{8,10},{9,11},{10,... | collective-permute-start | bytes 1966088 | tf_op jit(solution)/shard_map/ppermute | solution.py:367
  107.8 8.4 %collective-permute-start.22 = (bf16[512,3840]{1,0:T(8,128)(2,1)S(1)}, bf16[512,3840]{1,0:T(8,128)(2,1)S(1)}, u32[]{:S(2)}, u32[]{:S(2)}) collective-permute-start(bf16[512,3840]{1,0:T(8,128)(2,1)S(1)} %get-tuple-element.270.pack3_ref.refs_14_), channel_id=1, source_target_pairs={{0,1},{1,0},{2,3},{3,2},{4,5},{5,4},{6,7},{7,6},{8,9},{9,8},{10,11... | collective-permute-start | bytes 11796488 | tf_op jit(solution)/shard_map/ppermute | solution.py:367
  116.1 8.7 %collective-permute-start.23 = (bf16[512,3840]{1,0:T(8,128)(2,1)S(1)}, bf16[512,3840]{1,0:T(8,128)(2,1)S(1)}, u32[]{:S(2)}, u32[]{:S(2)}) collective-permute-start(bf16[512,3840]{1,0:T(8,128)(2,1)S(1)} %get-tuple-element.275.pack4_ref.refs_10_), channel_id=1, source_target_pairs={{0,1},{1,0},{2,3},{3,2},{4,5},{5,4},{6,7},{7,6},{8,9},{9,8},{10,11... | collective-permute-start | bytes 11796488 | tf_op jit(solution)/shard_map/ppermute | solution.py:367
  128.9 5.5 %collective-permute-start.24 = (bf16[192,2048]{1,0:T(8,128)(2,1)S(1)}, bf16[192,2048]{1,0:T(8,128)(2,1)S(1)}, u32[]{:S(2)}, u32[]{:S(2)}) collective-permute-start(bf16[192,2048]{1,0:T(8,128)(2,1)S(1)} %get-tuple-element.284.refs_2_.dkv_ref), channel_id=1, source_target_pairs={{0,1},{1,0},{2,3},{3,2},{4,5},{5,4},{6,7},{7,6},{8,9},{9,8},{10,11... | collective-permute-start | bytes 2359304 | tf_op jit(solution)/shard_map/ppermute | solution.py:367
  131.4 26.4 %collective-permute-start.28 = (bf16[2,640,128]{2,1,0:T(8,128)(2,1)}, bf16[2,640,128]{2,1,0:T(8,128)(2,1)}, u32[]{:S(2)}, u32[]{:S(2)}) collective-permute-start(bf16[2,640,128]{2,1,0:T(8,128)(2,1)} %get-tuple-element.298), channel_id=1, source_target_pairs={{0,8},{1,9},{2,10},{3,11},{4,12},{5,13},{6,14},{7,15},{8,0},{9,1},... | collective-permute-start | bytes 983048 | tf_op jit(solution)/shard_map/ppermute | solution.py:367
  133.7 4.4 %collective-permute-start.25 = (bf16[512,1024]{1,0:T(8,128)(2,1)S(1)}, bf16[512,1024]{1,0:T(8,128)(2,1)S(1)}, u32[]{:S(2)}, u32[]{:S(2)}) collective-permute-start(bf16[512,1024]{1,0:T(8,128)(2,1)S(1)} %get-tuple-element.316.refs_2_.dq_ref), channel_id=1, source_target_pairs={{0,1},{1,0},{2,3},{3,2},{4,5},{5,4},{6,7},{7,6},{8,9},{9,8},{10,11... | collective-permute-start | bytes 3145736 | tf_op jit(solution)/shard_map/ppermute | solution.py:367
  136.8 21.0 %collective-permute-start.27 = (bf16[2,1280,128]{2,1,0:T(8,128)(2,1)S(1)}, bf16[2,1280,128]{2,1,0:T(8,128)(2,1)S(1)}, u32[]{:S(2)}, u32[]{:S(2)}) collective-permute-start(bf16[2,1280,128]{2,1,0:T(8,128)(2,1)S(1)} %get-tuple-element.293), channel_id=1, source_target_pairs={{0,2},{1,3},{2,0},{3,1},{4,6},{5,7},{6,4},{7,5},{8,10},{9,11},{10,... | collective-permute-start | bytes 1966088 | tf_op jit(solution)/shard_map/ppermute | solution.py:367
  162.0 18.7 %collective-permute-start.29 = (bf16[4,768,128]{2,1,0:T(8,128)(2,1)S(1)}, bf16[4,768,128]{2,1,0:T(8,128)(2,1)S(1)}, u32[]{:S(2)}, u32[]{:S(2)}) collective-permute-start(bf16[4,768,128]{2,1,0:T(8,128)(2,1)S(1)} %get-tuple-element.311), channel_id=1, source_target_pairs={{0,2},{1,3},{2,0},{3,1},{4,6},{5,7},{6,4},{7,5},{8,10},{9,11},{10,... | collective-permute-start | bytes 2359304 | tf_op jit(solution)/shard_map/ppermute | solution.py:367
  163.6 7.8 %collective-permute-start.32 = (f32[3,1792]{1,0:T(4,128)S(1)}, f32[3,1792]{1,0:T(4,128)S(1)}, u32[]{:S(2)}, u32[]{:S(2)}) collective-permute-start(f32[3,1792]{1,0:T(4,128)S(1)} %copy-done.70), channel_id=1, source_target_pairs={{0,8},{1,9},{2,10},{3,11},{4,12},{5,13},{6,14},{7,15},{8,0},{9,1},... | collective-permute-start | bytes 64520 | tf_op jit(solution)/shard_map/ppermute | solution.py:367
  163.7 16.2 %collective-permute-start.30 = (bf16[1,1280,128]{2,1,0:T(8,128)(2,1)S(1)}, bf16[1,1280,128]{2,1,0:T(8,128)(2,1)S(1)}, u32[]{:S(2)}, u32[]{:S(2)}) collective-permute-start(bf16[1,1280,128]{2,1,0:T(8,128)(2,1)S(1)} %get-tuple-element.312), channel_id=1, source_target_pairs={{0,4},{1,5},{2,6},{3,7},{4,0},{5,1},{6,2},{7,3},{8,12},{9,13},{10,... | collective-permute-start | bytes 983048 | tf_op jit(solution)/shard_map/ppermute | solution.py:367
  163.9 16.0 %collective-permute-start.31 = (bf16[2,640,128]{2,1,0:T(8,128)(2,1)S(1)}, bf16[2,640,128]{2,1,0:T(8,128)(2,1)S(1)}, u32[]{:S(2)}, u32[]{:S(2)}) collective-permute-start(bf16[2,640,128]{2,1,0:T(8,128)(2,1)S(1)} %get-tuple-element.313), channel_id=1, source_target_pairs={{0,8},{1,9},{2,10},{3,11},{4,12},{5,13},{6,14},{7,15},{8,0},{9,1},... | collective-permute-start | bytes 983048 | tf_op jit(solution)/shard_map/ppermute | solution.py:367
  181.5 15.3 %collective-permute-start.33 = (bf16[2,768,128]{2,1,0:T(8,128)(2,1)S(1)}, bf16[2,768,128]{2,1,0:T(8,128)(2,1)S(1)}, u32[]{:S(2)}, u32[]{:S(2)}) collective-permute-start(bf16[2,768,128]{2,1,0:T(8,128)(2,1)S(1)} %get-tuple-element.337), channel_id=1, source_target_pairs={{0,4},{1,5},{2,6},{3,7},{4,0},{5,1},{6,2},{7,3},{8,12},{9,13},{10,... | collective-permute-start | bytes 1179656 | tf_op jit(solution)/shard_map/ppermute | solution.py:367
  182.5 16.3 %collective-permute-start.34 = (bf16[4,736,128]{2,1,0:T(8,128)(2,1)S(1)}, bf16[4,736,128]{2,1,0:T(8,128)(2,1)S(1)}, u32[]{:S(2)}, u32[]{:S(2)}) collective-permute-start(bf16[4,736,128]{2,1,0:T(8,128)(2,1)S(1)} %get-tuple-element.338), channel_id=1, source_target_pairs={{0,2},{1,3},{2,0},{3,1},{4,6},{5,7},{6,4},{7,5},{8,10},{9,11},{10,... | collective-permute-start | bytes 2261000 | tf_op jit(solution)/shard_map/ppermute | solution.py:367
  183.1 13.7 %collective-permute-start.35 = (bf16[1,1280,128]{2,1,0:T(8,128)(2,1)S(1)}, bf16[1,1280,128]{2,1,0:T(8,128)(2,1)S(1)}, u32[]{:S(2)}, u32[]{:S(2)}) collective-permute-start(bf16[1,1280,128]{2,1,0:T(8,128)(2,1)S(1)} %add_convert_fusion.1), channel_id=1, source_target_pairs={{0,8},{1,9},{10,2},{11,3},{12,4},{13,5},{14,6},{15,7},{16,24},{17,... | collective-permute-start | bytes 983048 | tf_op jit(solution)/shard_map/ppermute | solution.py:1377
  186.5 10.3 %collective-permute-start.36 = (f32[3,1792]{1,0:T(4,128)S(1)}, f32[3,1792]{1,0:T(4,128)S(1)}, u32[]{:S(2)}, u32[]{:S(2)}) collective-permute-start(f32[3,1792]{1,0:T(4,128)S(1)} %add.60), channel_id=1, source_target_pairs={{0,4},{1,5},{2,6},{3,7},{4,0},{5,1},{6,2},{7,3},{8,12},{9,13},{10,... | collective-permute-start | bytes 64520 | tf_op jit(solution)/shard_map/ppermute | solution.py:367
  198.9 16.7 %collective-permute-start.40 = (bf16[1,1280,128]{2,1,0:T(8,128)(2,1)S(1)}, bf16[1,1280,128]{2,1,0:T(8,128)(2,1)S(1)}, u32[]{:S(2)}, u32[]{:S(2)}) collective-permute-start(bf16[1,1280,128]{2,1,0:T(8,128)(2,1)S(1)} %add_convert_fusion), channel_id=1, source_target_pairs={{16,0},{17,1},{18,2},{19,3},{20,4},{21,5},{22,6},{23,7},{24,8},{25... | collective-permute-start | bytes 983048 | tf_op jit(solution)/shard_map/ppermute | solution.py:1379
  201.0 14.7 %collective-permute-start.38 = (bf16[2,736,128]{2,1,0:T(8,128)(2,1)S(1)}, bf16[2,736,128]{2,1,0:T(8,128)(2,1)S(1)}, u32[]{:S(2)}, u32[]{:S(2)}) collective-permute-start(bf16[2,736,128]{2,1,0:T(8,128)(2,1)S(1)} %get-tuple-element.348), channel_id=1, source_target_pairs={{0,4},{1,5},{2,6},{3,7},{4,0},{5,1},{6,2},{7,3},{8,12},{9,13},{10,... | collective-permute-start | bytes 1130504 | tf_op jit(solution)/shard_map/ppermute | solution.py:367
  202.0 13.6 %collective-permute-start.39 = (bf16[4,608,128]{2,1,0:T(8,128)(2,1)S(1)}, bf16[4,608,128]{2,1,0:T(8,128)(2,1)S(1)}, u32[]{:S(2)}, u32[]{:S(2)}) collective-permute-start(bf16[4,608,128]{2,1,0:T(8,128)(2,1)S(1)} %get-tuple-element.349), channel_id=1, source_target_pairs={{0,2},{1,3},{2,0},{3,1},{4,6},{5,7},{6,4},{7,5},{8,10},{9,11},{10,... | collective-permute-start | bytes 1867784 | tf_op jit(solution)/shard_map/ppermute | solution.py:367
  204.2 11.4 %collective-permute-start.37 = (bf16[1,768,128]{2,1,0:T(8,128)(2,1)S(1)}, bf16[1,768,128]{2,1,0:T(8,128)(2,1)S(1)}, u32[]{:S(2)}, u32[]{:S(2)}) collective-permute-start(bf16[1,768,128]{2,1,0:T(8,128)(2,1)S(1)} %get-tuple-element.345), channel_id=1, source_target_pairs={{0,8},{1,9},{2,10},{3,11},{4,12},{5,13},{6,14},{7,15},{8,0},{9,1},... | collective-permute-start | bytes 589832 | tf_op jit(solution)/shard_map/ppermute | solution.py:367
  204.3 11.3 %collective-permute-start.41 = (f32[3,1792]{1,0:T(4,128)S(1)}, f32[3,1792]{1,0:T(4,128)S(1)}, u32[]{:S(2)}, u32[]{:S(2)}) collective-permute-start(f32[3,1792]{1,0:T(4,128)S(1)} %add.62), channel_id=1, source_target_pairs={{0,2},{1,3},{2,0},{3,1},{4,6},{5,7},{6,4},{7,5},{8,10},{9,11},{10,... | collective-permute-start | bytes 64520 | tf_op jit(solution)/shard_map/ppermute | solution.py:367
  216.4 10.6 %collective-permute-start.43 = (bf16[2,608,128]{2,1,0:T(8,128)(2,1)S(1)}, bf16[2,608,128]{2,1,0:T(8,128)(2,1)S(1)}, u32[]{:S(2)}, u32[]{:S(2)}) collective-permute-start(bf16[2,608,128]{2,1,0:T(8,128)(2,1)S(1)} %get-tuple-element.360), channel_id=1, source_target_pairs={{0,4},{1,5},{2,6},{3,7},{4,0},{5,1},{6,2},{7,3},{8,12},{9,13},{10,... | collective-permute-start | bytes 933896 | tf_op jit(solution)/shard_map/ppermute | solution.py:367
  217.7 9.3 %collective-permute-start.44 = (bf16[4,384,128]{2,1,0:T(8,128)(2,1)S(1)}, bf16[4,384,128]{2,1,0:T(8,128)(2,1)S(1)}, u32[]{:S(2)}, u32[]{:S(2)}) collective-permute-start(bf16[4,384,128]{2,1,0:T(8,128)(2,1)S(1)} %get-tuple-element.361), channel_id=1, source_target_pairs={{0,2},{1,3},{2,0},{3,1},{4,6},{5,7},{6,4},{7,5},{8,10},{9,11},{10,... | collective-permute-start | bytes 1179656 | tf_op jit(solution)/shard_map/ppermute | solution.py:367
  219.6 7.4 %collective-permute-start.42 = (bf16[1,736,128]{2,1,0:T(8,128)(2,1)S(1)}, bf16[1,736,128]{2,1,0:T(8,128)(2,1)S(1)}, u32[]{:S(2)}, u32[]{:S(2)}) collective-permute-start(bf16[1,736,128]{2,1,0:T(8,128)(2,1)S(1)} %get-tuple-element.357), channel_id=1, source_target_pairs={{0,8},{1,9},{2,10},{3,11},{4,12},{5,13},{6,14},{7,15},{8,0},{9,1},... | collective-permute-start | bytes 565256 | tf_op jit(solution)/shard_map/ppermute | solution.py:367
  219.6 5.4 %collective-permute-start.45 = (f32[3,1792]{1,0:T(4,128)S(1)}, f32[3,1792]{1,0:T(4,128)S(1)}, u32[]{:S(2)}, u32[]{:S(2)}) collective-permute-start(f32[3,1792]{1,0:T(4,128)S(1)} %add.64), channel_id=1, source_target_pairs={{0,1},{1,0},{2,3},{3,2},{4,5},{5,4},{6,7},{7,6},{8,9},{9,8},{10,11... | collective-permute-start | bytes 64520 | tf_op jit(solution)/shard_map/ppermute | solution.py:367
  227.6 7.7 %collective-permute-start.47 = (bf16[2,384,128]{2,1,0:T(8,128)(2,1)S(1)}, bf16[2,384,128]{2,1,0:T(8,128)(2,1)S(1)}, u32[]{:S(2)}, u32[]{:S(2)}) collective-permute-start(bf16[2,384,128]{2,1,0:T(8,128)(2,1)S(1)} %get-tuple-element.370), channel_id=1, source_target_pairs={{0,4},{1,5},{2,6},{3,7},{4,0},{5,1},{6,2},{7,3},{8,12},{9,13},{10,... | collective-permute-start | bytes 589832 | tf_op jit(solution)/shard_map/ppermute | solution.py:367
  228.5 6.9 %collective-permute-start.46 = (bf16[1,608,128]{2,1,0:T(8,128)(2,1)S(1)}, bf16[1,608,128]{2,1,0:T(8,128)(2,1)S(1)}, u32[]{:S(2)}, u32[]{:S(2)}) collective-permute-start(bf16[1,608,128]{2,1,0:T(8,128)(2,1)S(1)} %get-tuple-element.367), channel_id=1, source_target_pairs={{0,8},{1,9},{2,10},{3,11},{4,12},{5,13},{6,14},{7,15},{8,0},{9,1},... | collective-permute-start | bytes 466952 | tf_op jit(solution)/shard_map/ppermute | solution.py:367
  236.0 7.6 %collective-permute-start.48 = (bf16[1,384,128]{2,1,0:T(8,128)(2,1)S(1)}, bf16[1,384,128]{2,1,0:T(8,128)(2,1)S(1)}, u32[]{:S(2)}, u32[]{:S(2)}) collective-permute-start(bf16[1,384,128]{2,1,0:T(8,128)(2,1)S(1)} %get-tuple-element.375), channel_id=1, source_target_pairs={{0,8},{1,9},{2,10},{3,11},{4,12},{5,13},{6,14},{7,15},{8,0},{9,1},... | collective-permute-start | bytes 294920 | tf_op jit(solution)/shard_map/ppermute | solution.py:367
  245.8 8.6 %collective-permute-start.49 = (bf16[2528,128]{1,0:T(8,128)(2,1)S(1)}, bf16[2528,128]{1,0:T(8,128)(2,1)S(1)}, u32[]{:S(2)}, u32[]{:S(2)}) collective-permute-start(bf16[2528,128]{1,0:T(8,128)(2,1)S(1)} %get-tuple-element.378), channel_id=1, source_target_pairs={{0,1},{1,0},{2,3},{3,2},{4,5},{5,4},{6,7},{7,6},{8,9},{9,8},{10,11... | collective-permute-start | bytes 1941512 | tf_op jit(solution)/shard_map/ppermute | solution.py:367
  (94 other events, 893.2 us)

commit v5 on v4

--- a/solution.py
+++ b/solution.py
@@ -70,7 +70,7 @@
     else:
         masks = [keys < fixed] * pairs
 
-    @pl.loop(0, blocks, unroll=4 if blocks % 4 == 0 else 3)
+    @pl.loop(0, blocks, unroll=blocks)
     def _(j):
         scores = []
         for p in range(pairs):
@@ -149,7 +149,7 @@
     else:
         masks = [keys < fixed] * pairs
 
-    @pl.loop(0, blocks, unroll=4 if blocks % 4 == 0 else 3)
+    @pl.loop(0, blocks, unroll=blocks)
     def _(j):
         scores, slopes = [], []
         for p in range(pairs):

time: 260 us -> 257 us (0.988)
  Pallas kernels: 126 us -> 123 us
  transfers between devices with their start and end apart: 50 -> 50, of which waited for: 14 -> 15; matrix products, arithmetic and copies ran while one was open for 4% -> 4% of each run, Pallas kernels for 46% -> 45%
where the time goes in v5:
time: 257 us; the launch traced here: 254 us
  Pallas kernels  123 us (48%)
  starting transfers between devices  56.5 us (22%)
  waiting for transfers between devices  52.4 us (20%)
  local copies, waits for them, and re-layouts  11.6 us (5%)
  matrix products  5.8 us (2%)
    pallas_call x10, Pallas kernels, fused(): pl.pallas_call(kernel, in_specs=in_specs, out_specs=[vmem] * len(outs), o...  67.8 us
    ppermute x43, waiting for transfers between devices, dp_swap(): return lax.ppermute(block, 'dp', [(i, i ^ bit) for i in range(count)])  48.8 us
    ppermute x43, starting transfers between devices, dp_swap(): return lax.ppermute(block, 'dp', [(i, i ^ bit) for i in range(count)])  48.4 us
    pallas_call x3, Pallas kernels, flat_grads(): pl.pallas_call(functools.partial(flat_kernel, plans=plans, found=found, q...  25.2 us
    pallas_call x11, Pallas kernels, add_split(): pl.pallas_call(functools.partial(add_split_kernel, plan=tuple(plan), inpu...  10.6 us
    unnamed x184, local copies, waits for them, and re-layouts  10.3 us
    pallas_call x2, Pallas kernels, attend_back(): pl.pallas_call(functools.partial(body, pairs=pairs, blocks=blocks, cols=c...  7.72 us
    dot_general x6, matrix products, mm(): return jnp.dot(a, b, preferred_element_type=F32)  5.8 us
  transfers between devices with their start and end apart: 50, of which 15 were waited for; matrix products, arithmetic and copies ran while one was open for 4% of the time, Pallas kernels for 45%

profile of v5, /device:TPU:3, one launch (start us, length us, event | category | flops | bytes accessed | tf_op | source)
XLA Modules:
  0.0 254.2 jit_solution(13470366232374160379)
XLA Ops:
  0.7 1.5 collective-permute-start
  2.4 1.3 fusion.9
  3.9 1.8 collective-permute-done.2
  6.1 2.8 %collective-permute-start.3 = (bf16[192,1024]{1,0:T(8,128)(2,1)S(1)}, bf16[192,1024]{1,0:T(8,128)(2,1)S(1)}, u32[]{:S(2)}, u32[]{:S(2)}) collective-permute-start(bf16[192,1024]{1,0:T(8,128)(2,1)S(1)} %fusion.x_ref.refs_0_), channel_id=1, source_target_pairs={{0,1},{1,0},{2,3},{3,2},{4,5},{5,4},{6,7},{7,6},{8,9},{9,8},{10,11... | collective-permute-start | bytes 1179656 | tf_op jit(solution)/shard_map/ppermute | solution.py:367
  8.8 2.2 convolution_convert_fusion.1.given_ref.refs_0_
  12.2 1.9 collective-permute-done.1
  16.6 2.2 collective-permute-start.12
  18.8 7.6 %co_forward.3 = (bf16[512,2048]{1,0:T(8,128)(2,1)S(1)}, bf16[192,2048]{1,0:T(8,128)(2,1)S(1)}, f32[192,1024]{1,0:T(8,128)S(1)}, f32[192,128]{1,0:T(8,128)S(1)}) custom-call(s32[4]{0:T(128)S(1)} %pad_add_fusion.1.lens_ref, bf16[192,1024]{1,0:T(8,128)(2,1)S(1)} %fusion.x_ref.refs_0_, bf16[192,1024]{1,0:T(8,128)(2,1)S(1)} %convolution_convert_fusion.1.given_ref.refs_0_, ...), custom_call_target="tpu_custom_call" | custom-call | flops 70000001024 | bytes 1000 | tf_op jit(solution)/shard_map/co_forward/pallas_call | solution.py:846
  28.4 3.7 %mlp_forward.2 = (bf16[192,2048]{1,0:T(8,128)(2,1)S(1)}, bf16[192,1024]{1,0:T(8,128)(2,1)S(1)}, f32[192,1024]{1,0:T(8,128)S(1)}, f32[192,128]{1,0:T(8,128)S(1)}, bf16[192,3072]{1,0:T(8,128)(2,1)S(1)}) custom-call(bf16[192,2048]{1,0:T(8,128)(2,1)S(1)} %get-tuple-element.204.pack1_ref.refs_4_, f32[192,1024]{1,0:T(8,128)S(1)} %get-tuple-element.205.n1_ref, ...), custom_call_target="tpu_custom_call" | custom-call | flops 48000000000 | bytes 1000 | tf_op jit(solution)/shard_map/mlp_forward/pallas_call | solution.py:846
  32.8 8.3 %self_turn.2 = (bf16[192,5120]{1,0:T(8,128)(2,1)S(1)}, bf16[192,1024]{1,0:T(8,128)(2,1)S(1)}, f32[192,1024]{1,0:T(8,128)S(1)}, f32[1,1024]{1,0:T(1,128)S(1)}) custom-call(s32[4]{0:T(128)S(1)} %pad_add_fusion.1.lens_ref, bf16[192,3072]{1,0:T(8,128)(2,1)S(1)} %get-tuple-element.209.r_ref, f32[192,1024]{1,0:T(8,128)S(1)} %get-tuple-element.210.n2_ref, ...), custom_call_target="tpu_custom_call" | custom-call | flops 105000001536 | bytes 1000 | tf_op jit(solution)/shard_map/self_turn/pallas_call | solution.py:846
  41.6 3.8 %mlp_back.2 = (bf16[192,2048]{1,0:T(8,128)(2,1)S(1)}, f32[192,1024]{1,0:T(8,128)S(1)}, f32[1,1024]{1,0:T(1,128)S(1)}) custom-call(bf16[192,5120]{1,0:T(8,128)(2,1)S(1)} %get-tuple-element.216.pack3_ref.refs_12_, f32[192,1024]{1,0:T(8,128)S(1)} %get-tuple-element.217.de_ref, f32[192,1024]{1,0:T(8,128)S(1)} %get-tuple-element.210.n2_ref, ...), custom_call_target="tpu_custom_call" | custom-call | flops 27428571136 | bytes 1000 | tf_op jit(solution)/shard_map/mlp_back/pallas_call | solution.py:846
  45.6 2.2 context_back.2
  48.4 3.9 %attend_back.2 = (bf16[192,1024]{1,0:T(8,128)(2,1)S(1)}, bf16[512,2048]{1,0:T(8,128)(2,1)S(1)}) custom-call(s32[4]{0:T(128)S(1)} %pad_add_fusion.1.lens_ref, bf16[192,1024]{1,0:T(8,128)(2,1)S(1)} %copy-done.19, bf16[512,2048]{1,0:T(8,128)(2,1)S(1)} %get-tuple-element.203.refs_1_, bf16[192,1024]{1,0:T(8,128)(2,1)S(1)} %get-tuple-element.225.refs_2_), custom_call_target="tpu_custom_call" | custom-call | flops 60000002048 | bytes 1000 | tf_op jit(solution)/shard_map/attend_back/pallas_call | solution.py:213
  52.6 7.9 %co_forward.2 = (bf16[512,1024]{1,0:T(8,128)(2,1)S(1)}, bf16[512,1792]{1,0:T(8,128)(2,1)S(1)}, f32[512,768]{1,0:T(8,128)S(1)}, f32[512,128]{1,0:T(8,128)S(1)}) custom-call(s32[4]{0:T(128)S(1)} %pad_add_fusion.1.lens_ref, bf16[512,768]{1,0:T(8,128)(2,1)} %pad_maximum_fusion.x_ref.source_ref.refs_0_, ...), custom_call_target="tpu_custom_call" | custom-call | flops 70000001024 | bytes 1000 | tf_op jit(solution)/shard_map/co_forward/pallas_call | solution.py:846
  61.3 6.2 %flat_grads.3.flat_ref = bf16[20480,128]{1,0:T(8,128)(2,1)S(1)} custom-call(s32[2]{0:T(128)S(1)} %pad_add_fusion.side_ref, bf16[192,1024]{1,0:T(8,128)(2,1)S(1)} %copy-done.4, bf16[192,1024]{1,0:T(8,128)(2,1)S(1)} %copy-done.54, bf16[192,1024]{1,0:T(8,128)(2,1)S(1)} %get-tuple-element.321.refs_2_.dq_ref, ...), custom_call_target="tpu_custom_call" | custom-call | flops 60000002048 | bytes 1000 | tf_op jit(solution)/shard_map/flat_grads/pallas_call | solution.py:350
  68.4 1.3 collective-permute-start.14
  69.7 1.3 collective-permute-start.15
  72.8 10.7 %mlp_forward.3 = (bf16[512,3840]{1,0:T(8,128)(2,1)S(1)}, bf16[512,3072]{1,0:T(8,128)(2,1)S(1)}, f32[512,768]{1,0:T(8,128)S(1)}, f32[512,128]{1,0:T(8,128)S(1)}, bf16[512,2304]{1,0:T(8,128)(2,1)S(1)}) custom-call(bf16[512,1792]{1,0:T(8,128)(2,1)S(1)} %get-tuple-element.246.pack1_ref.refs_6_, f32[512,768]{1,0:T(8,128)S(1)} %get-tuple-element.247.n1_ref, ...), custom_call_target="tpu_custom_call" | custom-call | flops 128000000000 | bytes 1000 | tf_op jit(solution)/shard_map/mlp_forward/pallas_call | solution.py:846
  83.5 1.7 copy-done.64
  86.8 1.3 collective-permute-start.17
  90.2 11.4 %self_turn.3 = (bf16[512,3840]{1,0:T(8,128)(2,1)S(1)}, bf16[512,768]{1,0:T(8,128)(2,1)S(1)}, f32[512,768]{1,0:T(8,128)S(1)}, f32[1,768]{1,0:T(1,128)S(1)}) custom-call(s32[4]{0:T(128)S(1)} %copy-done.61, bf16[512,2304]{1,0:T(8,128)(2,1)S(1)} %get-tuple-element.256.r_ref, f32[512,768]{1,0:T(8,128)S(1)} %get-tuple-element.257.n2_ref, f32[3,768]{1,0:T(4,128)S(1)} %copy-done.57, ...), custom_call_target="tpu_custom_call" | custom-call | flops 130000003072 | bytes 1000 | tf_op jit(solution)/shard_map/self_turn/pallas_call | solution.py:846
  102.4 2.2 add_split.11
  106.3 2.2 collective-permute-start.22
  108.5 6.0 %mlp_back.3 = (bf16[512,3840]{1,0:T(8,128)(2,1)S(1)}, f32[512,768]{1,0:T(8,128)S(1)}, f32[1,768]{1,0:T(1,128)S(1)}) custom-call(bf16[512,3840]{1,0:T(8,128)(2,1)S(1)} %get-tuple-element.270.pack3_ref.refs_14_, f32[512,768]{1,0:T(8,128)S(1)} %get-tuple-element.271.de_ref, f32[512,768]{1,0:T(8,128)S(1)} %get-tuple-element.257.n2_ref, ...), custom_call_target="tpu_custom_call" | custom-call | flops 73142853632 | bytes 1000 | tf_op jit(solution)/shard_map/mlp_back/pallas_call | solution.py:846
  114.8 1.7 collective-permute-start.23
  116.5 6.4 %context_back.3 = (bf16[512,768]{1,0:T(8,128)(2,1)S(1)}, f32[512,768]{1,0:T(8,128)S(1)}, bf16[512,1024]{1,0:T(8,128)(2,1)S(1)}, f32[1,768]{1,0:T(1,128)S(1)}) custom-call(bf16[512,3840]{1,0:T(8,128)(2,1)S(1)} %get-tuple-element.275.pack4_ref.refs_10_, f32[512,768]{1,0:T(8,128)S(1)} %get-tuple-element.276.db_ref, f32[512,768]{1,0:T(8,128)S(1)} %copy-done.67, ...), custom_call_target="tpu_custom_call" | custom-call | flops 64000000000 | bytes 1000 | tf_op jit(solution)/shard_map/context_back/pallas_call | solution.py:846
  123.6 3.8 %attend_back.3 = (bf16[512,1024]{1,0:T(8,128)(2,1)S(1)}, bf16[192,2048]{1,0:T(8,128)(2,1)S(1)}) custom-call(s32[4]{0:T(128)S(1)} %copy-done.62, bf16[512,1024]{1,0:T(8,128)(2,1)S(1)} %get-tuple-element.267.refs_0_, bf16[192,2048]{1,0:T(8,128)(2,1)S(1)} %copy-done.15, bf16[512,1024]{1,0:T(8,128)(2,1)S(1)} %get-tuple-element.279.refs_2_), custom_call_target="tpu_custom_call" | custom-call | flops 60000002048 | bytes 1000 | tf_op jit(solution)/shard_map/attend_back/pallas_call | solution.py:213
  127.5 2.4 add_split.12
  130.0 2.3 collective-permute-start.28
  133.0 1.7 flat_grads.4.flat_ref
  139.1 17.3 %flat_grads.5.flat_ref = bf16[19968,128]{1,0:T(8,128)(2,1)} custom-call(s32[2]{0:T(128)S(1)} %copy-done.59, bf16[512,768]{1,0:T(8,128)(2,1)} %pad_maximum_fusion.x_ref.source_ref.refs_0_, bf16[512,768]{1,0:T(8,128)(2,1)} %collective-permute-done.12.refs_1_, bf16[512,1024]{1,0:T(8,128)(2,1)S(1)} %get-tuple-element.316.refs_2_.dq_ref, ...), custom_call_target="tpu_custom_call" | custom-call | flops 140000002048 | bytes 1000 | tf_op jit(solution)/shard_map/flat_grads/pallas_call | solution.py:350
  156.4 2.4 copy-done.63
  162.3 2.3 collective-permute-start.31
  164.6 2.9 %input_grads.3 = (bf16[72,1024]{1,0:T(8,128)(2,1)}, bf16[72,1024]{1,0:T(8,128)(2,1)}) custom-call(f32[192,1024]{1,0:T(8,128)S(1)} %get-tuple-element.320.da_ref, bf16[192,1024]{1,0:T(8,128)(2,1)S(1)} %copy-done.17, bf16[192,2048]{1,0:T(8,128)(2,1)S(1)} %copy-done.13, bf16[192,1024]{1,0:T(8,128)(2,1)S(1)} %get-tuple-element.322.y_ref, ...), custom_call_target="tpu_custom_call" | custom-call | flops 2000000000 | bytes 1000 | tf_op jit(solution)/shard_map/input_grads/pallas_call | solution.py:938
  167.5 2.3 input_grads.2
  169.8 8.5 %collective-permute-done.30 = bf16[1,1280,128]{2,1,0:T(8,128)(2,1)S(1)} collective-permute-done((bf16[1,1280,128]{2,1,0:T(8,128)(2,1)S(1)}, bf16[1,1280,128]{2,1,0:T(8,128)(2,1)S(1)}, u32[]{:S(2)}, u32[]{:S(2)}) %collective-permute-start.30) | collective-permute-done | bytes 327712 | tf_op jit(solution)/shard_map/ppermute | solution.py:367
  181.4 3.6 %collective-permute-start.35 = (bf16[1,1280,128]{2,1,0:T(8,128)(2,1)S(1)}, bf16[1,1280,128]{2,1,0:T(8,128)(2,1)S(1)}, u32[]{:S(2)}, u32[]{:S(2)}) collective-permute-start(bf16[1,1280,128]{2,1,0:T(8,128)(2,1)S(1)} %add_convert_fusion.1), channel_id=1, source_target_pairs={{0,8},{1,9},{10,2},{11,3},{12,4},{13,5},{14,6},{15,7},{16,24},{17,... | collective-permute-start | bytes 983048 | tf_op jit(solution)/shard_map/ppermute | solution.py:1377
  185.1 10.0 %collective-permute-done.36 = f32[3,1792]{1,0:T(4,128)S(1)} collective-permute-done((f32[3,1792]{1,0:T(4,128)S(1)}, f32[3,1792]{1,0:T(4,128)S(1)}, u32[]{:S(2)}, u32[]{:S(2)}) %collective-permute-start.36) | collective-permute-done | bytes 21536 | tf_op jit(solution)/shard_map/ppermute | solution.py:367
  195.2 2.0 collective-permute-done.34.refs_1_
  197.2 1.3 collective-permute-start.40
  203.2 10.7 %collective-permute-done.41 = f32[3,1792]{1,0:T(4,128)S(1)} collective-permute-done((f32[3,1792]{1,0:T(4,128)S(1)}, f32[3,1792]{1,0:T(4,128)S(1)}, u32[]{:S(2)}, u32[]{:S(2)}) %collective-permute-start.41) | collective-permute-done | bytes 21536 | tf_op jit(solution)/shard_map/ppermute | solution.py:367
  216.6 5.4 %collective-permute-start.45 = (f32[3,1792]{1,0:T(4,128)S(1)}, f32[3,1792]{1,0:T(4,128)S(1)}, u32[]{:S(2)}, u32[]{:S(2)}) collective-permute-start(f32[3,1792]{1,0:T(4,128)S(1)} %add.64), channel_id=1, source_target_pairs={{0,1},{1,0},{2,3},{3,2},{4,5},{5,4},{6,7},{7,6},{8,9},{9,8},{10,11... | collective-permute-start | bytes 64520 | tf_op jit(solution)/shard_map/ppermute | solution.py:367
  225.6 1.6 collective-permute-start.46
  227.2 5.2 %collective-permute-done.46.refs_9_ = bf16[1,608,128]{2,1,0:T(8,128)(2,1)S(1)} collective-permute-done((bf16[1,608,128]{2,1,0:T(8,128)(2,1)S(1)}, bf16[1,608,128]{2,1,0:T(8,128)(2,1)S(1)}, u32[]{:S(2)}, u32[]{:S(2)}) %collective-permute-start.46) | collective-permute-done | bytes 155680 | tf_op jit(solution)/shard_map/ppermute | solution.py:367
  233.4 7.8 %collective-permute-done.48.refs_11_ = bf16[1,384,128]{2,1,0:T(8,128)(2,1)S(1)} collective-permute-done((bf16[1,384,128]{2,1,0:T(8,128)(2,1)S(1)}, bf16[1,384,128]{2,1,0:T(8,128)(2,1)S(1)}, u32[]{:S(2)}, u32[]{:S(2)}) %collective-permute-start.48) | collective-permute-done | bytes 98336 | tf_op jit(solution)/shard_map/ppermute | solution.py:367
  241.1 2.2 finish.1
  243.4 6.7 %collective-permute-start.49 = (bf16[2528,128]{1,0:T(8,128)(2,1)S(1)}, bf16[2528,128]{1,0:T(8,128)(2,1)S(1)}, u32[]{:S(2)}, u32[]{:S(2)}) collective-permute-start(bf16[2528,128]{1,0:T(8,128)(2,1)S(1)} %get-tuple-element.378), channel_id=1, source_target_pairs={{0,1},{1,0},{2,3},{3,2},{4,5},{5,4},{6,7},{7,6},{8,9},{9,8},{10,11... | collective-permute-start | bytes 1941512 | tf_op jit(solution)/shard_map/ppermute | solution.py:367
  251.8 2.2 join.1
  (297 shorter events, 44.1 us)
Async XLA Ops:
  0.6 5.0 %collective-permute-start.2 = (bf16[72,1024]{1,0:T(8,128)(2,1)}, bf16[72,1024]{1,0:T(8,128)(2,1)S(1)}, u32[]{:S(2)}, u32[]{:S(2)}) collective-permute-start(bf16[72,1024]{1,0:T(8,128)(2,1)} %param.22), channel_id=1, source_target_pairs={{0,16},{16,0},{1,17},{17,1},{2,18},{18,2},{3,19},{19,3},{4,20},{20... | collective-permute-start | bytes 442376 | tf_op jit(solution)/shard_map/ppermute | solution.py:371
  0.7 13.3 %collective-permute-start = (bf16[256,768]{1,0:T(8,128)(2,1)}, bf16[256,768]{1,0:T(8,128)(2,1)S(1)}, u32[]{:S(2)}, u32[]{:S(2)}) collective-permute-start(bf16[256,768]{1,0:T(8,128)(2,1)} %param.21), channel_id=1, source_target_pairs={{0,16},{16,0},{1,17},{17,1},{2,18},{18,2},{3,19},{19,3},{4,20},{20... | collective-permute-start | bytes 1179656 | tf_op jit(solution)/shard_map/ppermute | solution.py:371
  2.2 11.9 %collective-permute-start.1 = (s32[2]{0:T(128)}, s32[2]{0:T(128)S(1)}, u32[]{:S(2)}, u32[]{:S(2)}) collective-permute-start(s32[2]{0:T(128)} %param.23), channel_id=1, source_target_pairs={{0,16},{16,0},{1,17},{17,1},{2,18},{18,2},{3,19},{19,3},{4,20},{20... | collective-permute-start | bytes 32 | tf_op jit(solution)/shard_map/ppermute | solution.py:371
  6.1 20.8 %collective-permute-start.3 = (bf16[192,1024]{1,0:T(8,128)(2,1)S(1)}, bf16[192,1024]{1,0:T(8,128)(2,1)S(1)}, u32[]{:S(2)}, u32[]{:S(2)}) collective-permute-start(bf16[192,1024]{1,0:T(8,128)(2,1)S(1)} %fusion.x_ref.refs_0_), channel_id=1, source_target_pairs={{0,1},{1,0},{2,3},{3,2},{4,5},{5,4},{6,7},{7,6},{8,9},{9,8},{10,11... | collective-permute-start | bytes 1179656 | tf_op jit(solution)/shard_map/ppermute | solution.py:367
  15.1 17.1 %collective-permute-start.5 = (bf16[72,1024]{1,0:T(8,128)(2,1)S(1)}, bf16[72,1024]{1,0:T(8,128)(2,1)S(1)}, u32[]{:S(2)}, u32[]{:S(2)}) collective-permute-start(bf16[72,1024]{1,0:T(8,128)(2,1)S(1)} %copy-done.69), channel_id=1, source_target_pairs={{0,16},{16,0},{1,17},{17,1},{2,18},{18,2},{3,19},{19,3},{4,20},{20... | collective-permute-start | bytes 442376 | tf_op jit(solution)/shard_map/ppermute | solution.py:371
  15.5 25.6 %collective-permute-start.6 = (bf16[256,768]{1,0:T(8,128)(2,1)}, bf16[256,768]{1,0:T(8,128)(2,1)}, u32[]{:S(2)}, u32[]{:S(2)}) collective-permute-start(bf16[256,768]{1,0:T(8,128)(2,1)} %cot_ref), channel_id=1, source_target_pairs={{0,16},{16,0},{1,17},{17,1},{2,18},{18,2},{3,19},{19,3},{4,20},{20... | collective-permute-start | bytes 1179656 | tf_op jit(solution)/shard_map/ppermute | solution.py:371
  16.6 54.4 %collective-permute-start.12 = (bf16[512,768]{1,0:T(8,128)(2,1)}, bf16[512,768]{1,0:T(8,128)(2,1)}, u32[]{:S(2)}, u32[]{:S(2)}) collective-permute-start(bf16[512,768]{1,0:T(8,128)(2,1)} %pad_maximum_fusion.x_ref.source_ref.refs_0_), channel_id=1, source_target_pairs={{0,1},{1,0},{2,3},{3,2},{4,5},{5,4},{6,7},{7,6},{8,9},{9,8},{10,11... | collective-permute-start | bytes 2359304 | tf_op jit(solution)/shard_map/ppermute | solution.py:367
  27.6 5.0 %collective-permute-start.4 = (bf16[192,2048]{1,0:T(8,128)(2,1)S(1)}, bf16[192,2048]{1,0:T(8,128)(2,1)S(1)}, u32[]{:S(2)}, u32[]{:S(2)}) collective-permute-start(bf16[192,2048]{1,0:T(8,128)(2,1)S(1)} %get-tuple-element.204.pack1_ref.refs_4_), channel_id=1, source_target_pairs={{0,1},{1,0},{2,3},{3,2},{4,5},{5,4},{6,7},{7,6},{8,9},{9,8},{10,11... | collective-permute-start | bytes 2359304 | tf_op jit(solution)/shard_map/ppermute | solution.py:367
  32.7 8.4 %collective-permute-start.7 = (bf16[192,2048]{1,0:T(8,128)(2,1)S(1)}, bf16[192,2048]{1,0:T(8,128)(2,1)S(1)}, u32[]{:S(2)}, u32[]{:S(2)}) collective-permute-start(bf16[192,2048]{1,0:T(8,128)(2,1)S(1)} %get-tuple-element.215.refs_10_), channel_id=1, source_target_pairs={{0,1},{1,0},{2,3},{3,2},{4,5},{5,4},{6,7},{7,6},{8,9},{9,8},{10,11... | collective-permute-start | bytes 2359304 | tf_op jit(solution)/shard_map/ppermute | solution.py:367
  41.1 4.3 %collective-permute-start.8 = (bf16[192,5120]{1,0:T(8,128)(2,1)S(1)}, bf16[192,5120]{1,0:T(8,128)(2,1)S(1)}, u32[]{:S(2)}, u32[]{:S(2)}) collective-permute-start(bf16[192,5120]{1,0:T(8,128)(2,1)S(1)} %get-tuple-element.216.pack3_ref.refs_12_), channel_id=1, source_target_pairs={{0,1},{1,0},{2,3},{3,2},{4,5},{5,4},{6,7},{7,6},{8,9},{9,8},{10,11... | collective-permute-start | bytes 5898248 | tf_op jit(solution)/shard_map/ppermute | solution.py:367
  47.8 13.3 %collective-permute-start.11 = (bf16[192,1024]{1,0:T(8,128)(2,1)S(1)}, bf16[192,1024]{1,0:T(8,128)(2,1)S(1)}, u32[]{:S(2)}, u32[]{:S(2)}) collective-permute-start(bf16[192,1024]{1,0:T(8,128)(2,1)S(1)} %get-tuple-element.228.refs_6_), channel_id=1, source_target_pairs={{0,1},{1,0},{2,3},{3,2},{4,5},{5,4},{6,7},{7,6},{8,9},{9,8},{10,11... | collective-permute-start | bytes 1179656 | tf_op jit(solution)/shard_map/ppermute | solution.py:367
  52.4 8.8 %collective-permute-start.10 = (bf16[192,1024]{1,0:T(8,128)(2,1)S(1)}, bf16[192,1024]{1,0:T(8,128)(2,1)S(1)}, u32[]{:S(2)}, u32[]{:S(2)}) collective-permute-start(bf16[192,1024]{1,0:T(8,128)(2,1)S(1)} %get-tuple-element.321.refs_2_.dq_ref), channel_id=1, source_target_pairs={{0,1},{1,0},{2,3},{3,2},{4,5},{5,4},{6,7},{7,6},{8,9},{9,8},{10,11... | collective-permute-start | bytes 1179656 | tf_op jit(solution)/shard_map/ppermute | solution.py:367
  60.5 10.5 %collective-permute-start.13 = (bf16[512,2048]{1,0:T(8,128)(2,1)S(1)}, bf16[512,2048]{1,0:T(8,128)(2,1)S(1)}, u32[]{:S(2)}, u32[]{:S(2)}) collective-permute-start(bf16[512,2048]{1,0:T(8,128)(2,1)S(1)} %get-tuple-element.239.refs_4_.dkv_ref), channel_id=1, source_target_pairs={{0,1},{1,0},{2,3},{3,2},{4,5},{5,4},{6,7},{7,6},{8,9},{9,8},{10,11... | collective-permute-start | bytes 6291464 | tf_op jit(solution)/shard_map/ppermute | solution.py:367
  68.4 16.8 %collective-permute-start.14 = (bf16[4,640,128]{2,1,0:T(8,128)(2,1)S(1)}, bf16[4,640,128]{2,1,0:T(8,128)(2,1)S(1)}, u32[]{:S(2)}, u32[]{:S(2)}) collective-permute-start(bf16[4,640,128]{2,1,0:T(8,128)(2,1)S(1)} %get-tuple-element.242), channel_id=1, source_target_pairs={{0,2},{1,3},{2,0},{3,1},{4,6},{5,7},{6,4},{7,5},{8,10},{9,11},{10,... | collective-permute-start | bytes 1966088 | tf_op jit(solution)/shard_map/ppermute | solution.py:367
  69.7 16.0 %collective-permute-start.15 = (bf16[4,640,128]{2,1,0:T(8,128)(2,1)S(1)}, bf16[4,640,128]{2,1,0:T(8,128)(2,1)S(1)}, u32[]{:S(2)}, u32[]{:S(2)}) collective-permute-start(bf16[4,640,128]{2,1,0:T(8,128)(2,1)S(1)} %get-tuple-element.243), channel_id=1, source_target_pairs={{0,4},{1,5},{2,6},{3,7},{4,0},{5,1},{6,2},{7,3},{8,12},{9,13},{10,... | collective-permute-start | bytes 1966088 | tf_op jit(solution)/shard_map/ppermute | solution.py:367
  71.0 17.0 %collective-permute-start.18 = (bf16[512,1792]{1,0:T(8,128)(2,1)S(1)}, bf16[512,1792]{1,0:T(8,128)(2,1)S(1)}, u32[]{:S(2)}, u32[]{:S(2)}) collective-permute-start(bf16[512,1792]{1,0:T(8,128)(2,1)S(1)} %get-tuple-element.246.pack1_ref.refs_6_), channel_id=1, source_target_pairs={{0,1},{1,0},{2,3},{3,2},{4,5},{5,4},{6,7},{7,6},{8,9},{9,8},{10,11... | collective-permute-start | bytes 5505032 | tf_op jit(solution)/shard_map/ppermute | solution.py:367
  85.7 15.9 %collective-permute-start.16 = (bf16[4,640,128]{2,1,0:T(8,128)(2,1)S(1)}, bf16[4,640,128]{2,1,0:T(8,128)(2,1)S(1)}, u32[]{:S(2)}, u32[]{:S(2)}) collective-permute-start(bf16[4,640,128]{2,1,0:T(8,128)(2,1)S(1)} %get-tuple-element.251), channel_id=1, source_target_pairs={{0,2},{1,3},{2,0},{3,1},{4,6},{5,7},{6,4},{7,5},{8,10},{9,11},{10,... | collective-permute-start | bytes 1966088 | tf_op jit(solution)/shard_map/ppermute | solution.py:367
  86.8 15.7 %collective-permute-start.17 = (bf16[4,640,128]{2,1,0:T(8,128)(2,1)S(1)}, bf16[4,640,128]{2,1,0:T(8,128)(2,1)S(1)}, u32[]{:S(2)}, u32[]{:S(2)}) collective-permute-start(bf16[4,640,128]{2,1,0:T(8,128)(2,1)S(1)} %get-tuple-element.252), channel_id=1, source_target_pairs={{0,4},{1,5},{2,6},{3,7},{4,0},{5,1},{6,2},{7,3},{8,12},{9,13},{10,... | collective-permute-start | bytes 1966088 | tf_op jit(solution)/shard_map/ppermute | solution.py:367
  89.3 16.9 %collective-permute-start.21 = (bf16[512,3840]{1,0:T(8,128)(2,1)S(1)}, bf16[512,3840]{1,0:T(8,128)(2,1)S(1)}, u32[]{:S(2)}, u32[]{:S(2)}) collective-permute-start(bf16[512,3840]{1,0:T(8,128)(2,1)S(1)} %get-tuple-element.269.refs_12_), channel_id=1, source_target_pairs={{0,1},{1,0},{2,3},{3,2},{4,5},{5,4},{6,7},{7,6},{8,9},{9,8},{10,11... | collective-permute-start | bytes 11796488 | tf_op jit(solution)/shard_map/ppermute | solution.py:367
  104.6 22.8 %collective-permute-start.19 = (bf16[4,640,128]{2,1,0:T(8,128)(2,1)}, bf16[4,640,128]{2,1,0:T(8,128)(2,1)}, u32[]{:S(2)}, u32[]{:S(2)}) collective-permute-start(bf16[4,640,128]{2,1,0:T(8,128)(2,1)} %get-tuple-element.265), channel_id=1, source_target_pairs={{0,4},{1,5},{2,6},{3,7},{4,0},{5,1},{6,2},{7,3},{8,12},{9,13},{10,... | collective-permute-start | bytes 1966088 | tf_op jit(solution)/shard_map/ppermute | solution.py:367
  105.9 21.5 %collective-permute-start.20 = (bf16[4,640,128]{2,1,0:T(8,128)(2,1)}, bf16[4,640,128]{2,1,0:T(8,128)(2,1)}, u32[]{:S(2)}, u32[]{:S(2)}) collective-permute-start(bf16[4,640,128]{2,1,0:T(8,128)(2,1)} %get-tuple-element.266), channel_id=1, source_target_pairs={{0,2},{1,3},{2,0},{3,1},{4,6},{5,7},{6,4},{7,5},{8,10},{9,11},{10,... | collective-permute-start | bytes 1966088 | tf_op jit(solution)/shard_map/ppermute | solution.py:367
  106.3 8.6 %collective-permute-start.22 = (bf16[512,3840]{1,0:T(8,128)(2,1)S(1)}, bf16[512,3840]{1,0:T(8,128)(2,1)S(1)}, u32[]{:S(2)}, u32[]{:S(2)}) collective-permute-start(bf16[512,3840]{1,0:T(8,128)(2,1)S(1)} %get-tuple-element.270.pack3_ref.refs_14_), channel_id=1, source_target_pairs={{0,1},{1,0},{2,3},{3,2},{4,5},{5,4},{6,7},{7,6},{8,9},{9,8},{10,11... | collective-permute-start | bytes 11796488 | tf_op jit(solution)/shard_map/ppermute | solution.py:367
  114.8 8.7 %collective-permute-start.23 = (bf16[512,3840]{1,0:T(8,128)(2,1)S(1)}, bf16[512,3840]{1,0:T(8,128)(2,1)S(1)}, u32[]{:S(2)}, u32[]{:S(2)}) collective-permute-start(bf16[512,3840]{1,0:T(8,128)(2,1)S(1)} %get-tuple-element.275.pack4_ref.refs_10_), channel_id=1, source_target_pairs={{0,1},{1,0},{2,3},{3,2},{4,5},{5,4},{6,7},{7,6},{8,9},{9,8},{10,11... | collective-permute-start | bytes 11796488 | tf_op jit(solution)/shard_map/ppermute | solution.py:367
  127.4 5.5 %collective-permute-start.24 = (bf16[192,2048]{1,0:T(8,128)(2,1)S(1)}, bf16[192,2048]{1,0:T(8,128)(2,1)S(1)}, u32[]{:S(2)}, u32[]{:S(2)}) collective-permute-start(bf16[192,2048]{1,0:T(8,128)(2,1)S(1)} %get-tuple-element.284.refs_2_.dkv_ref), channel_id=1, source_target_pairs={{0,1},{1,0},{2,3},{3,2},{4,5},{5,4},{6,7},{7,6},{8,9},{9,8},{10,11... | collective-permute-start | bytes 2359304 | tf_op jit(solution)/shard_map/ppermute | solution.py:367
  130.0 26.4 %collective-permute-start.28 = (bf16[2,640,128]{2,1,0:T(8,128)(2,1)}, bf16[2,640,128]{2,1,0:T(8,128)(2,1)}, u32[]{:S(2)}, u32[]{:S(2)}) collective-permute-start(bf16[2,640,128]{2,1,0:T(8,128)(2,1)} %get-tuple-element.298), channel_id=1, source_target_pairs={{0,8},{1,9},{2,10},{3,11},{4,12},{5,13},{6,14},{7,15},{8,0},{9,1},... | collective-permute-start | bytes 983048 | tf_op jit(solution)/shard_map/ppermute | solution.py:367
  132.3 4.2 %collective-permute-start.25 = (bf16[512,1024]{1,0:T(8,128)(2,1)S(1)}, bf16[512,1024]{1,0:T(8,128)(2,1)S(1)}, u32[]{:S(2)}, u32[]{:S(2)}) collective-permute-start(bf16[512,1024]{1,0:T(8,128)(2,1)S(1)} %get-tuple-element.316.refs_2_.dq_ref), channel_id=1, source_target_pairs={{0,1},{1,0},{2,3},{3,2},{4,5},{5,4},{6,7},{7,6},{8,9},{9,8},{10,11... | collective-permute-start | bytes 3145736 | tf_op jit(solution)/shard_map/ppermute | solution.py:367
  135.4 21.0 %collective-permute-start.27 = (bf16[2,1280,128]{2,1,0:T(8,128)(2,1)S(1)}, bf16[2,1280,128]{2,1,0:T(8,128)(2,1)S(1)}, u32[]{:S(2)}, u32[]{:S(2)}) collective-permute-start(bf16[2,1280,128]{2,1,0:T(8,128)(2,1)S(1)} %get-tuple-element.293), channel_id=1, source_target_pairs={{0,2},{1,3},{2,0},{3,1},{4,6},{5,7},{6,4},{7,5},{8,10},{9,11},{10,... | collective-permute-start | bytes 1966088 | tf_op jit(solution)/shard_map/ppermute | solution.py:367
  160.6 18.7 %collective-permute-start.29 = (bf16[4,768,128]{2,1,0:T(8,128)(2,1)S(1)}, bf16[4,768,128]{2,1,0:T(8,128)(2,1)S(1)}, u32[]{:S(2)}, u32[]{:S(2)}) collective-permute-start(bf16[4,768,128]{2,1,0:T(8,128)(2,1)S(1)} %get-tuple-element.311), channel_id=1, source_target_pairs={{0,2},{1,3},{2,0},{3,1},{4,6},{5,7},{6,4},{7,5},{8,10},{9,11},{10,... | collective-permute-start | bytes 2359304 | tf_op jit(solution)/shard_map/ppermute | solution.py:367
  162.0 7.8 %collective-permute-start.32 = (f32[3,1792]{1,0:T(4,128)S(1)}, f32[3,1792]{1,0:T(4,128)S(1)}, u32[]{:S(2)}, u32[]{:S(2)}) collective-permute-start(f32[3,1792]{1,0:T(4,128)S(1)} %copy-done.70), channel_id=1, source_target_pairs={{0,8},{1,9},{2,10},{3,11},{4,12},{5,13},{6,14},{7,15},{8,0},{9,1},... | collective-permute-start | bytes 64520 | tf_op jit(solution)/shard_map/ppermute | solution.py:367
  162.1 16.2 %collective-permute-start.30 = (bf16[1,1280,128]{2,1,0:T(8,128)(2,1)S(1)}, bf16[1,1280,128]{2,1,0:T(8,128)(2,1)S(1)}, u32[]{:S(2)}, u32[]{:S(2)}) collective-permute-start(bf16[1,1280,128]{2,1,0:T(8,128)(2,1)S(1)} %get-tuple-element.312), channel_id=1, source_target_pairs={{0,4},{1,5},{2,6},{3,7},{4,0},{5,1},{6,2},{7,3},{8,12},{9,13},{10,... | collective-permute-start | bytes 983048 | tf_op jit(solution)/shard_map/ppermute | solution.py:367
  162.3 16.0 %collective-permute-start.31 = (bf16[2,640,128]{2,1,0:T(8,128)(2,1)S(1)}, bf16[2,640,128]{2,1,0:T(8,128)(2,1)S(1)}, u32[]{:S(2)}, u32[]{:S(2)}) collective-permute-start(bf16[2,640,128]{2,1,0:T(8,128)(2,1)S(1)} %get-tuple-element.313), channel_id=1, source_target_pairs={{0,8},{1,9},{2,10},{3,11},{4,12},{5,13},{6,14},{7,15},{8,0},{9,1},... | collective-permute-start | bytes 983048 | tf_op jit(solution)/shard_map/ppermute | solution.py:367
  180.1 15.1 %collective-permute-start.33 = (bf16[2,768,128]{2,1,0:T(8,128)(2,1)S(1)}, bf16[2,768,128]{2,1,0:T(8,128)(2,1)S(1)}, u32[]{:S(2)}, u32[]{:S(2)}) collective-permute-start(bf16[2,768,128]{2,1,0:T(8,128)(2,1)S(1)} %get-tuple-element.337), channel_id=1, source_target_pairs={{0,4},{1,5},{2,6},{3,7},{4,0},{5,1},{6,2},{7,3},{8,12},{9,13},{10,... | collective-permute-start | bytes 1179656 | tf_op jit(solution)/shard_map/ppermute | solution.py:367
  180.8 16.3 %collective-permute-start.34 = (bf16[4,736,128]{2,1,0:T(8,128)(2,1)S(1)}, bf16[4,736,128]{2,1,0:T(8,128)(2,1)S(1)}, u32[]{:S(2)}, u32[]{:S(2)}) collective-permute-start(bf16[4,736,128]{2,1,0:T(8,128)(2,1)S(1)} %get-tuple-element.338), channel_id=1, source_target_pairs={{0,2},{1,3},{2,0},{3,1},{4,6},{5,7},{6,4},{7,5},{8,10},{9,11},{10,... | collective-permute-start | bytes 2261000 | tf_op jit(solution)/shard_map/ppermute | solution.py:367
  181.4 13.7 %collective-permute-start.35 = (bf16[1,1280,128]{2,1,0:T(8,128)(2,1)S(1)}, bf16[1,1280,128]{2,1,0:T(8,128)(2,1)S(1)}, u32[]{:S(2)}, u32[]{:S(2)}) collective-permute-start(bf16[1,1280,128]{2,1,0:T(8,128)(2,1)S(1)} %add_convert_fusion.1), channel_id=1, source_target_pairs={{0,8},{1,9},{10,2},{11,3},{12,4},{13,5},{14,6},{15,7},{16,24},{17,... | collective-permute-start | bytes 983048 | tf_op jit(solution)/shard_map/ppermute | solution.py:1377
  185.1 10.1 %collective-permute-start.36 = (f32[3,1792]{1,0:T(4,128)S(1)}, f32[3,1792]{1,0:T(4,128)S(1)}, u32[]{:S(2)}, u32[]{:S(2)}) collective-permute-start(f32[3,1792]{1,0:T(4,128)S(1)} %add.60), channel_id=1, source_target_pairs={{0,4},{1,5},{2,6},{3,7},{4,0},{5,1},{6,2},{7,3},{8,12},{9,13},{10,... | collective-permute-start | bytes 64520 | tf_op jit(solution)/shard_map/ppermute | solution.py:367
  197.2 16.7 %collective-permute-start.40 = (bf16[1,1280,128]{2,1,0:T(8,128)(2,1)S(1)}, bf16[1,1280,128]{2,1,0:T(8,128)(2,1)S(1)}, u32[]{:S(2)}, u32[]{:S(2)}) collective-permute-start(bf16[1,1280,128]{2,1,0:T(8,128)(2,1)S(1)} %add_convert_fusion), channel_id=1, source_target_pairs={{16,0},{17,1},{18,2},{19,3},{20,4},{21,5},{22,6},{23,7},{24,8},{25... | collective-permute-start | bytes 983048 | tf_op jit(solution)/shard_map/ppermute | solution.py:1379
  199.3 14.7 %collective-permute-start.38 = (bf16[2,736,128]{2,1,0:T(8,128)(2,1)S(1)}, bf16[2,736,128]{2,1,0:T(8,128)(2,1)S(1)}, u32[]{:S(2)}, u32[]{:S(2)}) collective-permute-start(bf16[2,736,128]{2,1,0:T(8,128)(2,1)S(1)} %get-tuple-element.348), channel_id=1, source_target_pairs={{0,4},{1,5},{2,6},{3,7},{4,0},{5,1},{6,2},{7,3},{8,12},{9,13},{10,... | collective-permute-start | bytes 1130504 | tf_op jit(solution)/shard_map/ppermute | solution.py:367
  200.6 13.4 %collective-permute-start.39 = (bf16[4,608,128]{2,1,0:T(8,128)(2,1)S(1)}, bf16[4,608,128]{2,1,0:T(8,128)(2,1)S(1)}, u32[]{:S(2)}, u32[]{:S(2)}) collective-permute-start(bf16[4,608,128]{2,1,0:T(8,128)(2,1)S(1)} %get-tuple-element.349), channel_id=1, source_target_pairs={{0,2},{1,3},{2,0},{3,1},{4,6},{5,7},{6,4},{7,5},{8,10},{9,11},{10,... | collective-permute-start | bytes 1867784 | tf_op jit(solution)/shard_map/ppermute | solution.py:367
  202.3 11.7 %collective-permute-start.37 = (bf16[1,768,128]{2,1,0:T(8,128)(2,1)S(1)}, bf16[1,768,128]{2,1,0:T(8,128)(2,1)S(1)}, u32[]{:S(2)}, u32[]{:S(2)}) collective-permute-start(bf16[1,768,128]{2,1,0:T(8,128)(2,1)S(1)} %get-tuple-element.345), channel_id=1, source_target_pairs={{0,8},{1,9},{2,10},{3,11},{4,12},{5,13},{6,14},{7,15},{8,0},{9,1},... | collective-permute-start | bytes 589832 | tf_op jit(solution)/shard_map/ppermute | solution.py:367
  202.3 11.6 %collective-permute-start.41 = (f32[3,1792]{1,0:T(4,128)S(1)}, f32[3,1792]{1,0:T(4,128)S(1)}, u32[]{:S(2)}, u32[]{:S(2)}) collective-permute-start(f32[3,1792]{1,0:T(4,128)S(1)} %add.62), channel_id=1, source_target_pairs={{0,2},{1,3},{2,0},{3,1},{4,6},{5,7},{6,4},{7,5},{8,10},{9,11},{10,... | collective-permute-start | bytes 64520 | tf_op jit(solution)/shard_map/ppermute | solution.py:367
  214.7 8.7 %collective-permute-start.43 = (bf16[2,608,128]{2,1,0:T(8,128)(2,1)S(1)}, bf16[2,608,128]{2,1,0:T(8,128)(2,1)S(1)}, u32[]{:S(2)}, u32[]{:S(2)}) collective-permute-start(bf16[2,608,128]{2,1,0:T(8,128)(2,1)S(1)} %get-tuple-element.360), channel_id=1, source_target_pairs={{0,4},{1,5},{2,6},{3,7},{4,0},{5,1},{6,2},{7,3},{8,12},{9,13},{10,... | collective-permute-start | bytes 933896 | tf_op jit(solution)/shard_map/ppermute | solution.py:367
  214.8 8.7 %collective-permute-start.44 = (bf16[4,384,128]{2,1,0:T(8,128)(2,1)S(1)}, bf16[4,384,128]{2,1,0:T(8,128)(2,1)S(1)}, u32[]{:S(2)}, u32[]{:S(2)}) collective-permute-start(bf16[4,384,128]{2,1,0:T(8,128)(2,1)S(1)} %get-tuple-element.361), channel_id=1, source_target_pairs={{0,2},{1,3},{2,0},{3,1},{4,6},{5,7},{6,4},{7,5},{8,10},{9,11},{10,... | collective-permute-start | bytes 1179656 | tf_op jit(solution)/shard_map/ppermute | solution.py:367
  216.2 7.2 %collective-permute-start.42 = (bf16[1,736,128]{2,1,0:T(8,128)(2,1)S(1)}, bf16[1,736,128]{2,1,0:T(8,128)(2,1)S(1)}, u32[]{:S(2)}, u32[]{:S(2)}) collective-permute-start(bf16[1,736,128]{2,1,0:T(8,128)(2,1)S(1)} %get-tuple-element.357), channel_id=1, source_target_pairs={{0,8},{1,9},{2,10},{3,11},{4,12},{5,13},{6,14},{7,15},{8,0},{9,1},... | collective-permute-start | bytes 565256 | tf_op jit(solution)/shard_map/ppermute | solution.py:367
  216.6 6.3 %collective-permute-start.45 = (f32[3,1792]{1,0:T(4,128)S(1)}, f32[3,1792]{1,0:T(4,128)S(1)}, u32[]{:S(2)}, u32[]{:S(2)}) collective-permute-start(f32[3,1792]{1,0:T(4,128)S(1)} %add.64), channel_id=1, source_target_pairs={{0,1},{1,0},{2,3},{3,2},{4,5},{5,4},{6,7},{7,6},{8,9},{9,8},{10,11... | collective-permute-start | bytes 64520 | tf_op jit(solution)/shard_map/ppermute | solution.py:367
  224.1 8.3 %collective-permute-start.47 = (bf16[2,384,128]{2,1,0:T(8,128)(2,1)S(1)}, bf16[2,384,128]{2,1,0:T(8,128)(2,1)S(1)}, u32[]{:S(2)}, u32[]{:S(2)}) collective-permute-start(bf16[2,384,128]{2,1,0:T(8,128)(2,1)S(1)} %get-tuple-element.370), channel_id=1, source_target_pairs={{0,4},{1,5},{2,6},{3,7},{4,0},{5,1},{6,2},{7,3},{8,12},{9,13},{10,... | collective-permute-start | bytes 589832 | tf_op jit(solution)/shard_map/ppermute | solution.py:367
  225.6 6.8 %collective-permute-start.46 = (bf16[1,608,128]{2,1,0:T(8,128)(2,1)S(1)}, bf16[1,608,128]{2,1,0:T(8,128)(2,1)S(1)}, u32[]{:S(2)}, u32[]{:S(2)}) collective-permute-start(bf16[1,608,128]{2,1,0:T(8,128)(2,1)S(1)} %get-tuple-element.367), channel_id=1, source_target_pairs={{0,8},{1,9},{2,10},{3,11},{4,12},{5,13},{6,14},{7,15},{8,0},{9,1},... | collective-permute-start | bytes 466952 | tf_op jit(solution)/shard_map/ppermute | solution.py:367
  233.0 8.2 %collective-permute-start.48 = (bf16[1,384,128]{2,1,0:T(8,128)(2,1)S(1)}, bf16[1,384,128]{2,1,0:T(8,128)(2,1)S(1)}, u32[]{:S(2)}, u32[]{:S(2)}) collective-permute-start(bf16[1,384,128]{2,1,0:T(8,128)(2,1)S(1)} %get-tuple-element.375), channel_id=1, source_target_pairs={{0,8},{1,9},{2,10},{3,11},{4,12},{5,13},{6,14},{7,15},{8,0},{9,1},... | collective-permute-start | bytes 294920 | tf_op jit(solution)/shard_map/ppermute | solution.py:367
  243.4 8.4 %collective-permute-start.49 = (bf16[2528,128]{1,0:T(8,128)(2,1)S(1)}, bf16[2528,128]{1,0:T(8,128)(2,1)S(1)}, u32[]{:S(2)}, u32[]{:S(2)}) collective-permute-start(bf16[2528,128]{1,0:T(8,128)(2,1)S(1)} %get-tuple-element.378), channel_id=1, source_target_pairs={{0,1},{1,0},{2,3},{3,2},{4,5},{5,4},{6,7},{7,6},{8,9},{9,8},{10,11... | collective-permute-start | bytes 1941512 | tf_op jit(solution)/shard_map/ppermute | solution.py:367
  (94 other events, 876.7 us)
